TPU v7x, 32 devices: a whole 2x2x4 slice. The times are simulated.
32 devices in a mesh: rep: 2 (over core), shard: 16 (over z, y, x).
Axes of the slice: x: 2, y: 2, z: 4, core: 2. Of those that a mesh axis runs over, the one named last changes fastest.
Arguments:
- frames: bfloat16 [24000, 1280], P(('rep', 'shard')), may hold values from -6 to 6
- upstream: bfloat16 [24000, 1280], P(('rep', 'shard')), may hold values from -6 to 6
- lengths: int32 [16], replicated, may hold values from 375 to 1500, as said below
- master_qkv: float32 [3, 1280, 1280], P(None, 'shard'), may hold values from -0.15625 to 0.15625
- master_out: float32 [1280, 1280], P('shard'), may hold values from -0.25 to 0.25
- master_up: float32 [1280, 5120], P('shard'), may hold values from -0.15625 to 0.15625
- master_down: float32 [5120, 1280], P('shard'), may hold values from -0.078125 to 0.078125
- master_small: float32 [15360], P('shard'), may hold values from -1.2 to 1.5, as said below
- first_qkv: bfloat16 [3, 1280, 1280], P(None, 'shard'), may hold values from -448 to 448
- first_out: bfloat16 [1280, 1280], P('shard'), may hold values from -48 to 48
- first_up: bfloat16 [1280, 5120], P('shard'), may hold values from -256 to 256
- first_down: bfloat16 [5120, 1280], P('shard'), may hold values from -640 to 640
- first_small: bfloat16 [15360], P('shard'), may hold values from -627.4233 to 627.4233
- second_qkv: float32 [3, 1280, 1280], P(None, 'shard'), may hold values from 6000 to 24000
- second_out: float32 [1280, 1280], P('shard'), may hold values from 64 to 256
- second_up: float32 [1280, 5120], P('shard'), may hold values from 2400 to 9600
- second_down: float32 [5120, 1280], P('shard'), may hold values from 12000 to 48000
- second_small: float32 [15360], P('shard'), may hold values from 2160 to 96000
Outputs:
- mixed: float32 [24000, 1280], P(('rep', 'shard'))
- grad_frames: float32 [24000, 1280], P(('rep', 'shard'))
- updated_qkv: float32 [3, 1280, 1280], P(None, 'shard')
- casted_qkv: bfloat16 [3, 1280, 1280], P(None, 'shard')
- momentum_qkv: float32 [3, 1280, 1280], P(None, 'shard')
- variance_qkv: float32 [3, 1280, 1280], P(None, 'shard')
- updated_out: float32 [1280, 1280], P('shard')
- casted_out: bfloat16 [1280, 1280], P('shard')
- momentum_out: float32 [1280, 1280], P('shard')
- variance_out: float32 [1280, 1280], P('shard')
- updated_up: float32 [1280, 5120], P('shard')
- casted_up: bfloat16 [1280, 5120], P('shard')
- momentum_up: float32 [1280, 5120], P('shard')
- variance_up: float32 [1280, 5120], P('shard')
- updated_down: float32 [5120, 1280], P('shard')
- casted_down: bfloat16 [5120, 1280], P('shard')
- momentum_down: float32 [5120, 1280], P('shard')
- variance_down: float32 [5120, 1280], P('shard')
- updated_small: float32 [15360], P('shard')
- casted_small: bfloat16 [15360], P('shard')
- momentum_small: float32 [15360], P('shard')
- variance_small: float32 [15360], P('shard')
Inputs may be any that keep to these rules, and one draw needn't show every extreme that they name: lengths[c] frames of clip c count; some clip has all 1500. `master_small`: gains in the two norms' gain blocks, biases elsewhere.
All inputs are finite; a program needn't handle non-finite values.
Results may differ from a plain program's by a relative error of at most 0.012.
The roundings to bfloat16 on the way count: a program that leaves them out, or rounds other values in their place, can miss the bound.
Values may be sent and summed in bfloat16 or wider, within the bound.
No kernel may reach another device: no remote copies, remote signals or barrier semaphores. Data moves between devices by JAX's collectives and lax.ppermute only.
A program may use at most 320 MiB of HBM per device.

v0:
```python
import jax
import jax.numpy as jnp
from jax import lax
from jax.sharding import PartitionSpec as P

HEAD_DIM = 80
STEP = 10


LN_EPS = 1e-05
NEG_FILL = -1e30
BETA_ONE = 0.5
BETA_TWO = 0.5
ADAM_EPS = 1e-08
RATES = (0.04, 0.5, 0.04, 0.02, 0.3)
DECAYS = (0.01, 0.01, 0.01, 0.01, 0.0)


def from_partner(value, axis, bit):
    mask = 2**bit
    pairs = [(source, source ^ mask) for source in range(lax.axis_size(axis))]
    return lax.ppermute(value, axis, pairs)


def normalize(values, gain, shift):
    center = values - jnp.mean(values, -1, keepdims=True)
    spread = jnp.mean(center * center, -1, keepdims=True)
    return center * lax.rsqrt(spread + LN_EPS) * gain + shift


def gelu_exact(values):
    return jax.nn.gelu(values, approximate=False)


def split_heads(matrix):
    return matrix.reshape(matrix.shape[0], -1, HEAD_DIM).transpose(1, 0, 2)


def join_heads(stacked):
    return stacked.transpose(1, 0, 2).reshape(stacked.shape[1], -1)


def column_sums(matrix):
    return jnp.sum(matrix.astype(jnp.float32), 0)


def unpack_small(small_vec, width):
    blocks = tuple((small_vec[index * width : (index + 1) * width] for index in range(8)))
    return blocks + (small_vec[8 * width :],)


def adam_update(master, moment_one, second, gradient, step_rate, decay_rate, step_number):
    momentum = BETA_ONE * moment_one.astype(jnp.float32) + (1.0 - BETA_ONE) * gradient
    variance = BETA_TWO * second + (1.0 - BETA_TWO) * gradient * gradient
    momentum_hat = momentum / (1.0 - BETA_ONE**step_number)
    variance_hat = variance / (1.0 - BETA_TWO**step_number)
    updated = master - step_rate * (
        momentum_hat / (jnp.sqrt(variance_hat) + ADAM_EPS) + decay_rate * master
    )
    return (updated, updated.astype(jnp.bfloat16), momentum, variance)


def local(
    frames,
    upstream,
    lengths,
    master_qkv,
    master_out,
    master_up,
    master_down,
    master_small,
    first_qkv,
    first_out,
    first_up,
    first_down,
    first_small,
    second_qkv,
    second_out,
    second_up,
    second_down,
    second_small,
):
    half_rows, model_width = frames.shape
    shard_count = lax.axis_size("shard")
    shard_pos = lax.axis_index("shard")
    half_index = shard_pos % 2
    clip_id = (lax.axis_index("rep") * shard_count + shard_pos) // 2
    length = lax.dynamic_index_in_dim(lengths, clip_id, 0, keepdims=False)
    row_steps = jnp.arange(half_rows, dtype=jnp.int32)
    positions = jnp.concatenate(
        [half_index * half_rows + row_steps, (1 - half_index) * half_rows + row_steps]
    )
    counted = positions < length
    scaling = HEAD_DIM ** (-0.5)
    copy_qkv = master_qkv.astype(jnp.bfloat16)
    copy_out = master_out.astype(jnp.bfloat16)
    copy_up = master_up.astype(jnp.bfloat16)
    copy_down = master_down.astype(jnp.bfloat16)
    copy_small = master_small.astype(jnp.bfloat16)
    inputs = frames.astype(jnp.float32)
    grad_output = upstream.astype(jnp.float32)

    def scores_of(query_head, key_head):
        raw = (
            jnp.einsum("qd,kd->qk", query_head, key_head, preferred_element_type=jnp.float32)
            * scaling
        )
        return jnp.where(counted[None, :], raw, NEG_FILL)

    def attend(bundle):
        query_head, key_head, value_head = bundle
        scores = scores_of(query_head, key_head)
        row_top = jnp.max(scores, -1, keepdims=True)
        powers = jnp.exp(scores - row_top)
        row_total = jnp.sum(powers, -1, keepdims=True)
        attn_probs = powers / row_total
        context_head = jnp.dot(
            attn_probs.astype(jnp.bfloat16), value_head, preferred_element_type=jnp.float32
        )
        return (context_head, (row_top + jnp.log(row_total))[:, 0])

    def attend_back(bundle):
        query_head, key_head, value_head, grad_head, log_total = bundle
        scores = scores_of(query_head, key_head)
        attn_probs = jnp.exp(scores - log_total[:, None])
        grad_probs = jnp.einsum(
            "qd,kd->qk", grad_head, value_head, preferred_element_type=jnp.float32
        )
        row_inner = jnp.sum(attn_probs * grad_probs, -1, keepdims=True)
        grad_scores = (attn_probs * (grad_probs - row_inner)).astype(jnp.bfloat16)
        grad_query_head = (
            jnp.dot(grad_scores, key_head, preferred_element_type=jnp.float32) * scaling
        )
        grad_key_head = (
            jnp.einsum("qk,qd->kd", grad_scores, query_head, preferred_element_type=jnp.float32)
            * scaling
        )
        grad_value_head = jnp.einsum(
            "qk,qd->kd",
            attn_probs.astype(jnp.bfloat16),
            grad_head,
            preferred_element_type=jnp.float32,
        )
        return (grad_query_head, grad_key_head, grad_value_head)

    w_qkv, w_out, w_up, w_down, small_low = (
        lax.all_gather(copy_qkv, "shard", axis=1, tiled=True),
        lax.all_gather(copy_out, "shard", axis=0, tiled=True),
        lax.all_gather(copy_up, "shard", axis=0, tiled=True),
        lax.all_gather(copy_down, "shard", axis=0, tiled=True),
        lax.all_gather(copy_small, "shard", axis=0, tiled=True),
    )
    small_vec = small_low.astype(jnp.float32)
    (
        gain_one,
        shift_one,
        bias_query,
        bias_value,
        bias_out,
        gain_two,
        shift_two,
        bias_down,
        bias_up,
    ) = unpack_small(small_vec, model_width)
    normed_low = normalize(inputs, gain_one, shift_one).astype(jnp.bfloat16)
    projected = jnp.einsum("td,jde->jte", normed_low, w_qkv, preferred_element_type=jnp.float32)
    query_low = (projected[0] + bias_query).astype(jnp.bfloat16)
    key_low = projected[1].astype(jnp.bfloat16)
    value_low = (projected[2] + bias_value).astype(jnp.bfloat16)
    far_key, far_value = from_partner((key_low, value_low), "shard", 0)
    query_heads = split_heads(query_low)
    key_heads = split_heads(jnp.concatenate([key_low, far_key], 0))
    value_heads = split_heads(jnp.concatenate([value_low, far_value], 0))
    context_heads, log_totals = lax.map(attend, (query_heads, key_heads, value_heads))
    context_low = join_heads(context_heads).astype(jnp.bfloat16)
    middle = inputs + jnp.dot(context_low, w_out, preferred_element_type=jnp.float32) + bias_out
    normed_two_low = normalize(middle, gain_two, shift_two).astype(jnp.bfloat16)
    hidden_pre = jnp.dot(normed_two_low, w_up, preferred_element_type=jnp.float32) + bias_up
    hidden_low = gelu_exact(hidden_pre).astype(jnp.bfloat16)
    mixed = jnp.dot(hidden_low, w_down, preferred_element_type=jnp.float32) + bias_down + middle
    back_qkv, back_out, back_up, back_down = (
        lax.all_gather(copy_qkv, "shard", axis=1, tiled=True),
        lax.all_gather(copy_out, "shard", axis=0, tiled=True),
        lax.all_gather(copy_up, "shard", axis=0, tiled=True),
        lax.all_gather(copy_down, "shard", axis=0, tiled=True),
    )
    grad_down = jnp.einsum("tf,td->fd", hidden_low, upstream, preferred_element_type=jnp.float32)
    grad_bias_down = jnp.sum(grad_output, 0)
    grad_hidden = jnp.einsum("td,fd->tf", upstream, back_down, preferred_element_type=jnp.float32)
    grad_pre_low = jax.vjp(gelu_exact, hidden_pre)[1](grad_hidden)[0].astype(jnp.bfloat16)
    grad_up = jnp.einsum(
        "td,tf->df", normed_two_low, grad_pre_low, preferred_element_type=jnp.float32
    )
    grad_bias_up = column_sums(grad_pre_low)
    grad_normed_two = jnp.einsum(
        "tf,df->td", grad_pre_low, back_up, preferred_element_type=jnp.float32
    )
    pull_two = jax.vjp(normalize, middle, gain_two, shift_two)[1]
    grad_middle_part, grad_gain_two, grad_shift_two = pull_two(grad_normed_two)
    grad_middle = grad_output + grad_middle_part
    grad_attended_low = grad_middle.astype(jnp.bfloat16)
    grad_out_proj = jnp.einsum(
        "td,te->de", context_low, grad_attended_low, preferred_element_type=jnp.float32
    )
    grad_bias_out = column_sums(grad_attended_low)
    grad_context_low = jnp.einsum(
        "te,de->td", grad_attended_low, back_out, preferred_element_type=jnp.float32
    ).astype(jnp.bfloat16)
    grad_query_heads, grad_key_heads, grad_value_heads = lax.map(
        attend_back,
        (query_heads, key_heads, value_heads, split_heads(grad_context_low), log_totals),
    )
    grad_query_low = join_heads(grad_query_heads).astype(jnp.bfloat16)
    grad_key_rows = join_heads(grad_key_heads)
    grad_value_rows = join_heads(grad_value_heads)
    back_key, back_value = from_partner(
        (grad_key_rows[half_rows:], grad_value_rows[half_rows:]), "shard", 0
    )
    grad_key_low = (grad_key_rows[:half_rows] + back_key).astype(jnp.bfloat16)
    grad_value_low = (grad_value_rows[:half_rows] + back_value).astype(jnp.bfloat16)
    stacked_grads = jnp.stack([grad_query_low, grad_key_low, grad_value_low])
    grad_qkv = jnp.einsum(
        "td,jte->jde", normed_low, stacked_grads, preferred_element_type=jnp.float32
    )
    grad_bias_query = column_sums(grad_query_low)
    grad_bias_value = column_sums(grad_value_low)
    grad_normed_one = jnp.einsum(
        "jte,jde->td", stacked_grads, back_qkv, preferred_element_type=jnp.float32
    )
    pull_one = jax.vjp(normalize, inputs, gain_one, shift_one)[1]
    grad_inputs_part, grad_gain_one, grad_shift_one = pull_one(grad_normed_one)
    grad_inputs = grad_middle + grad_inputs_part
    grad_small = jnp.concatenate(
        [
            grad_gain_one,
            grad_shift_one,
            grad_bias_query,
            grad_bias_value,
            grad_bias_out,
            grad_gain_two,
            grad_shift_two,
            grad_bias_down,
            grad_bias_up,
        ]
    )
    owned_qkv, owned_out, owned_up, owned_down, owned_small = (
        lax.psum_scatter(grad_qkv, "shard", scatter_dimension=1, tiled=True),
        lax.psum_scatter(grad_out_proj, "shard", scatter_dimension=0, tiled=True),
        lax.psum_scatter(grad_up, "shard", scatter_dimension=0, tiled=True),
        lax.psum_scatter(grad_down, "shard", scatter_dimension=0, tiled=True),
        lax.psum_scatter(grad_small, "shard", scatter_dimension=0, tiled=True),
    )
    total_qkv, total_out, total_up, total_down, total_small = lax.psum(
        (owned_qkv, owned_out, owned_up, owned_down, owned_small), "rep"
    )
    new_qkv, cast_qkv, mom_qkv, var_qkv = adam_update(
        master_qkv, first_qkv, second_qkv, total_qkv, RATES[0], DECAYS[0], STEP
    )
    new_out, cast_out, mom_out, var_out = adam_update(
        master_out, first_out, second_out, total_out, RATES[1], DECAYS[1], STEP
    )
    new_up, cast_up, mom_up, var_up = adam_update(
        master_up, first_up, second_up, total_up, RATES[2], DECAYS[2], STEP
    )
    new_down, cast_down, mom_down, var_down = adam_update(
        master_down, first_down, second_down, total_down, RATES[3], DECAYS[3], STEP
    )
    new_small, cast_small, mom_small, var_small = adam_update(
        master_small, first_small, second_small, total_small, RATES[4], DECAYS[4], STEP
    )
    return (
        mixed,
        grad_inputs,
        new_qkv,
        cast_qkv,
        mom_qkv,
        var_qkv,
        new_out,
        cast_out,
        mom_out,
        var_out,
        new_up,
        cast_up,
        mom_up,
        var_up,
        new_down,
        cast_down,
        mom_down,
        var_down,
        new_small,
        cast_small,
        mom_small,
        var_small,
    )


def solution(mesh):
    return jax.shard_map(
        local,
        mesh=mesh,
        in_specs=(
            P(("rep", "shard"), None),
            P(("rep", "shard"), None),
            P(),
            P(None, "shard", None),
            P("shard", None),
            P("shard", None),
            P("shard", None),
            P("shard"),
            P(None, "shard", None),
            P("shard", None),
            P("shard", None),
            P("shard", None),
            P("shard"),
            P(None, "shard", None),
            P("shard", None),
            P("shard", None),
            P("shard", None),
            P("shard"),
        ),
        out_specs=(
            P(("rep", "shard"), None),
            P(("rep", "shard"), None),
            P(None, "shard", None),
            P(None, "shard", None),
            P(None, "shard", None),
            P(None, "shard", None),
            P("shard", None),
            P("shard", None),
            P("shard", None),
            P("shard", None),
            P("shard", None),
            P("shard", None),
            P("shard", None),
            P("shard", None),
            P("shard", None),
            P("shard", None),
            P("shard", None),
            P("shard", None),
            P("shard"),
            P("shard"),
            P("shard"),
            P("shard"),
        ),
        check_vma=False,
    )
```

profile of v0, /device:TPU:0, one launch (start us, length us, event | category | flops | bytes accessed | tf_op | source)
XLA Modules:
  0.0 3090.1 jit_solution(11569880318348438557)
XLA Ops:
  15.5 80.1 %all-reduce = bf16[15360]{0:T(1024)(128)(2,1)S(1)} all-reduce(bf16[15360]{0:T(1024)(128)(2,1)S(1)} %dynamic-update-slice), channel_id=1, replica_groups=mesh['rep'=2,'shard'=16] {'shard'}, use_global_device_ids=true, to_apply=%add | all-reduce | flops 15360 | bytes 61440
  97.8 43.6 %all-gather.5.cloned.1.call-done = bf16[3,1280,1280]{2,1,0:T(8,128)(2,1)} async-done(((bf16[3,80,1280]{2,1,0:T(8,128)(2,1)}), bf16[3,1280,1280]{2,1,0:T(8,128)(2,1)}) %all-gather.5.cloned.1.call-update) | async-done | bytes 9830416 | tf_op jit(solution)/shard_map/all_gather | solution.py:147
  141.4 10.7 convolution_bitcast_fusion.2
  180.3 32.3 %collective-permute-done = bf16[750,1280]{1,0:T(8,128)(2,1)} collective-permute-done((bf16[750,1280]{1,0:T(8,128)(2,1)}, bf16[750,1280]{1,0:T(8,128)(2,1)}, u32[]{:S(2)}, u32[]{:S(2)}) %collective-permute-start) | collective-permute-done | bytes 1920032 | tf_op jit(solution)/shard_map/ppermute | solution.py:22
  217.1 6.3 copy.107
  223.3 7.7 copy.110
  231.0 30.9 %collective-permute-done.1 = bf16[750,1280]{1,0:T(8,128)(2,1)} collective-permute-done((bf16[750,1280]{1,0:T(8,128)(2,1)}, bf16[750,1280]{1,0:T(8,128)(2,1)}, u32[]{:S(2)}, u32[]{:S(2)}) %collective-permute-start.1) | collective-permute-done | bytes 1920032 | tf_op jit(solution)/shard_map/ppermute | solution.py:22
  266.4 6.3 copy.108
  272.8 7.7 copy.111
  281.9 120.3 %while.26 = (s32[]{:T(128)}, bf16[16,750,80]{1,2,0:T(8,128)(2,1)}, f32[16,750]{1,0:T(8,128)}, pred[1500]{0:T(1024)(128)(4,1)S(1)}, bf16[16,750,80]{2,1,0:T(8,128...) while((s32[]{:T(128)}, bf16[16,750,80]{1,2,0:T(8,128)(2,1)}, ...), condition=%wide.region_5.6_spmd, body=%wide.region_2.5_spmd.sunk | while | flops 373499232 | bytes 14750973 | solution.py:174
  410.6 18.1 fusion.82
  428.7 122.0 %all-gather.11.cloned.1.call-done = bf16[5120,1280]{1,0:T(8,128)(2,1)} async-done(((bf16[320,1280]{1,0:T(8,128)(2,1)}), bf16[5120,1280]{1,0:T(8,128)(2,1)}) %all-gather.11.cloned.1.call-update) | async-done | bytes 13107216 | tf_op jit(solution)/shard_map/all_gather | solution.py:150
  550.6 50.7 %convert_reduce_fusion = (f32[5120]{0:T(1024)}, bf16[750,5120]{1,0:T(8,128)(2,1)}, f32[750,5120]{1,0:T(8,128)}) fusion(f32[750,5120]{1,0:T(8,128)} %fusion.82, f32[5120]{0:T(1024)S(1)} %slice.100, bf16[750,1280]{1,0:T(8,128)(2,1)} %param.23, bf16[5120,1280]{1,0:T(8,128)(2,1)} %all-gather.11.cloned.1.call-done), kind=kOutput, calls=%fused_computation.56 | convolution fusion | flops 10118394880 | bytes 53468160 | tf_op jit(solution)/shard_map/td,fd->tf/dot_general | solution.py:189
  601.4 19.7 multiply_reduce_fusion.1
  633.7 195.5 %while.27 = (s32[]{:T(128)}, bf16[16,750,80]{1,2,0:T(8,128)(2,1)S(1)}, f32[16,1500,80]{1,2,0:T(8,128)}, f32[16,1500,80]{1,2,0:T(8,128)}, pred[1500]{0:T(1024)(12...) while((s32[]{:T(128)}, ...), condition=%wide.region_12.13_spmd, body=%wide.region_10.12_spmd.sunk | while | flops 910304192 | bytes 36846540 | solution.py:209
  829.1 8.4 fusion.97
  844.3 7.8 fusion.96
  871.4 58.0 %collective-permute-done.3 = f32[750,1280]{1,0:T(8,128)} collective-permute-done((f32[750,1280]{1,0:T(8,128)}, f32[750,1280]{1,0:T(8,128)}, u32[]{:S(2)}, u32[]{:S(2)}) %collective-permute-start.3) | collective-permute-done | bytes 3840032 | tf_op jit(solution)/shard_map/ppermute | solution.py:22
  933.4 77.0 %collective-permute-done.2 = f32[750,1280]{1,0:T(8,128)} collective-permute-done((f32[750,1280]{1,0:T(8,128)}, f32[750,1280]{1,0:T(8,128)}, u32[]{:S(2)}, u32[]{:S(2)}) %collective-permute-start.2) | collective-permute-done | bytes 3840032 | tf_op jit(solution)/shard_map/ppermute | solution.py:22
  1014.3 13.7 convolution_bitcast_fusion.1
  1028.0 27.4 copy.122
  1055.4 7.5 fusion.101
  1063.7 19.3 fusion.81
  1083.7 11.3 multiply_convert_fusion.1
  1098.0 14.1 fusion.102
  1115.5 18.4 fusion.54
  1133.9 601.7 %all-reduce.7.cloned.1.call-done = f32[3,1280,1280]{2,0,1:T(4,128)} async-done(((f32[3,1280,1280]{2,0,1:T(4,128)}), f32[3,1280,1280]{2,0,1:T(4,128)}) %all-reduce.7.cloned.1.call-update) | async-done | bytes 19660816
  1738.5 139.8 %reduce-scatter.4.cloned.1.call-done = f32[80,1280]{1,0:T(8,128)} async-done(((f32[1280,1280]{1,0:T(8,128)}), f32[80,1280]{1,0:T(8,128)}) %reduce-scatter.4.cloned.1.call-update) | async-done | bytes 409616 | tf_op jit(solution)/shard_map/reduce_scatter | solution.py:248
  1878.4 542.4 %reduce-scatter.6.cloned.1.call-done = f32[80,5120]{1,0:T(8,128)} async-done(((f32[1280,5120]{1,0:T(8,128)}), f32[80,5120]{1,0:T(8,128)}) %reduce-scatter.6.cloned.1.call-update) | async-done | bytes 1638416 | tf_op jit(solution)/shard_map/reduce_scatter | solution.py:249
  2420.7 546.0 %reduce-scatter.8.cloned.1.call-done = f32[320,1280]{1,0:T(8,128)} async-done(((f32[5120,1280]{1,0:T(8,128)}), f32[320,1280]{1,0:T(8,128)}) %reduce-scatter.8.cloned.1.call-update) | async-done | bytes 1638416 | tf_op jit(solution)/shard_map/reduce_scatter | solution.py:250
  2966.8 13.2 bitcast_reduce_fusion
  2986.9 78.6 %all-reduce.2 = f32[15360]{0:T(1024)S(1)} all-reduce(f32[15360]{0:T(1024)S(1)} %constant_dynamic-update-slice_fusion), channel_id=6, replica_groups=mesh['rep'=2,'shard'=16] {'shard'}, use_global_device_ids=true, to_apply=%region_32.33.clone | all-reduce | flops 15360 | bytes 122880
  (432 shorter events, 452.1 us)
Async XLA Ops:
  7.2 88.4 %copy-start.2 = (bf16[750,1280]{1,0:T(8,128)(2,1)S(1)}, bf16[750,1280]{1,0:T(8,128)(2,1)}, u32[]{:S(2)}) copy-start(bf16[750,1280]{1,0:T(8,128)(2,1)} %param.22) | copy-start | bytes 5760004
  7.2 134.2 %all-gather.5.cloned.1.call-start = ((), (), s32[]{:S(2)}) async-start(), calls=%async_computation.3 | async-start | bytes 10444800 | tf_op jit(solution)/shard_map/all_gather | solution.py:147
  9.6 392.6 %all-gather.7.cloned.1.call-start = ((), (), s32[]{:S(2)}) async-start(), calls=%async_computation.4 | async-start | bytes 3481600 | tf_op jit(solution)/shard_map/all_gather | solution.py:148
  11.4 399.2 %all-gather.9.cloned.1.call-start = ((), (), s32[]{:S(2)}) async-start(), calls=%async_computation.5 | async-start | bytes 13926400 | tf_op jit(solution)/shard_map/all_gather | solution.py:149
  13.9 536.8 %all-gather.11.cloned.1.call-start = ((), (), s32[]{:S(2)}) async-start(), calls=%async_computation.6 | async-start | bytes 13926400 | tf_op jit(solution)/shard_map/all_gather | solution.py:150
  95.9 56.2 %copy-start.40 = (f32[750]{0:T(1024)}, f32[750]{0:T(1024)S(1)}, u32[]{:S(2)}) copy-start(f32[750]{0:T(1024)S(1)} %broadcast_multiply_fusion.1) | copy-start | bytes 9004
  97.2 54.9 %copy-start.46 = (f32[750]{0:T(1024)}, f32[750]{0:T(1024)S(1)}, u32[]{:S(2)}) copy-start(f32[750]{0:T(1024)S(1)} %fusion.76) | copy-start | bytes 9004
  97.8 54.3 %copy-start.38 = (f32[1280]{0:T(1024)}, f32[1280]{0:T(1024)S(1)}, u32[]{:S(2)}) copy-start(f32[1280]{0:T(1024)S(1)} %get-tuple-element.326) | copy-start | bytes 15364
  97.8 54.3 %copy-start.55 = (f32[1280]{0:T(1024)}, f32[1280]{0:T(1024)S(1)}, u32[]{:S(2)}) copy-start(f32[1280]{0:T(1024)S(1)} %get-tuple-element.327) | copy-start | bytes 15364
  97.8 312.8 %copy-start.33 = (f32[1280]{0:T(1024)}, f32[1280]{0:T(1024)S(1)}, u32[]{:S(2)}) copy-start(f32[1280]{0:T(1024)S(1)} %get-tuple-element.322) | copy-start | bytes 15364
  153.7 58.8 %collective-permute-start = (bf16[750,1280]{1,0:T(8,128)(2,1)}, bf16[750,1280]{1,0:T(8,128)(2,1)}, u32[]{:S(2)}, u32[]{:S(2)}) collective-permute-start(bf16[750,1280]{1,0:T(8,128)(2,1)} %fusion.67), channel_id=1, source_target_pairs={{0,1},{1,0},{2,3},{3,2},{4,5},{5,4},{6,7},{7,6},{8,9},{9,8},{10,11... | collective-permute-start | bytes 5760008 | tf_op jit(solution)/shard_map/ppermute | solution.py:22
  158.8 103.2 %collective-permute-start.1 = (bf16[750,1280]{1,0:T(8,128)(2,1)}, bf16[750,1280]{1,0:T(8,128)(2,1)}, u32[]{:S(2)}, u32[]{:S(2)}) collective-permute-start(bf16[750,1280]{1,0:T(8,128)(2,1)} %fusion.62), channel_id=1, source_target_pairs={{0,1},{1,0},{2,3},{3,2},{4,5},{5,4},{6,7},{7,6},{8,9},{9,8},{10,11... | collective-permute-start | bytes 5760008 | tf_op jit(solution)/shard_map/ppermute | solution.py:22
  160.8 1574.8 %all-reduce.7.cloned.1.call-start = ((), (), s32[]{:S(2)}) async-start(), calls=%async_computation.10 | async-start | bytes 52428800
  161.1 389.5 %copy-start.36 = (f32[5120]{0:T(1024)}, f32[5120]{0:T(1024)S(1)}, u32[]{:S(2)}) copy-start(f32[5120]{0:T(1024)S(1)} %slice.100) | copy-start | bytes 61444
  843.0 86.5 %collective-permute-start.3 = (f32[750,1280]{1,0:T(8,128)}, f32[750,1280]{1,0:T(8,128)}, u32[]{:S(2)}, u32[]{:S(2)}) collective-permute-start(f32[750,1280]{1,0:T(8,128)} %copy.119), channel_id=1, source_target_pairs={{0,1},{1,0},{2,3},{3,2},{4,5},{5,4},{6,7},{7,6},{8,9},{9,8},{10,11... | collective-permute-start | bytes 11520008 | tf_op jit(solution)/shard_map/ppermute | solution.py:22
  857.6 152.8 %collective-permute-start.2 = (f32[750,1280]{1,0:T(8,128)}, f32[750,1280]{1,0:T(8,128)}, u32[]{:S(2)}, u32[]{:S(2)}) collective-permute-start(f32[750,1280]{1,0:T(8,128)} %copy.117), channel_id=1, source_target_pairs={{0,1},{1,0},{2,3},{3,2},{4,5},{5,4},{6,7},{7,6},{8,9},{9,8},{10,11... | collective-permute-start | bytes 11520008 | tf_op jit(solution)/shard_map/ppermute | solution.py:22
  871.4 138.9 %copy-start.7 = (f32[750,1280]{1,0:T(8,128)S(1)}, f32[750,1280]{1,0:T(8,128)}, u32[]{:S(2)}) copy-start(f32[750,1280]{1,0:T(8,128)} %copy.118) | copy-start | bytes 11520004
  933.4 79.6 %copy-start.20 = (bf16[750,1280]{1,0:T(8,128)(2,1)}, bf16[750,1280]{1,0:T(8,128)(2,1)S(1)}, u32[]{:S(2)}) copy-start(bf16[750,1280]{1,0:T(8,128)(2,1)S(1)} %get-tuple-element.291) | copy-start | bytes 5760004
  933.4 80.9 %copy-start.3 = (bf16[750,1280]{1,0:T(8,128)(2,1)S(1)}, bf16[750,1280]{1,0:T(8,128)(2,1)}, u32[]{:S(2)}) copy-start(bf16[750,1280]{1,0:T(8,128)(2,1)} %param.22) | copy-start | bytes 5760004
  933.4 80.9 %copy-start.19 = (bf16[1,750,1280]{2,1,0:T(8,128)(2,1)S(1)}, bf16[1,750,1280]{2,1,0:T(8,128)(2,1)}, u32[]{:S(2)}) copy-start(bf16[1,750,1280]{2,1,0:T(8,128)(2,1)} %copy.121) | copy-start | bytes 5760004
  933.4 80.9 %copy-start.39 = (f32[1280]{0:T(1024)S(1)}, f32[1280]{0:T(1024)}, u32[]{:S(2)}) copy-start(f32[1280]{0:T(1024)} %copy-done.38) | copy-start | bytes 15364
  933.4 80.9 %copy-start.41 = (f32[750]{0:T(1024)S(1)}, f32[750]{0:T(1024)}, u32[]{:S(2)}) copy-start(f32[750]{0:T(1024)} %copy-done.40) | copy-start | bytes 9004
  933.4 80.9 %copy-start.47 = (f32[750]{0:T(1024)S(1)}, f32[750]{0:T(1024)}, u32[]{:S(2)}) copy-start(f32[750]{0:T(1024)} %copy-done.46) | copy-start | bytes 9004
  933.4 80.9 %copy-start.56 = (f32[1280]{0:T(1024)S(1)}, f32[1280]{0:T(1024)}, u32[]{:S(2)}) copy-start(f32[1280]{0:T(1024)} %copy-done.55) | copy-start | bytes 15364
  1055.4 823.0 %reduce-scatter.4.cloned.1.call-start = ((), (), s32[]{:S(2)}) async-start(), calls=%async_computation.7 | async-start | bytes 6963200 | tf_op jit(solution)/shard_map/reduce_scatter | solution.py:248
  1063.0 1357.7 %reduce-scatter.6.cloned.1.call-start = ((), (), s32[]{:S(2)}) async-start(), calls=%async_computation.8 | async-start | bytes 27852800 | tf_op jit(solution)/shard_map/reduce_scatter | solution.py:249
  1083.0 1883.8 %reduce-scatter.8.cloned.1.call-start = ((), (), s32[]{:S(2)}) async-start(), calls=%async_computation.9 | async-start | bytes 27852800 | tf_op jit(solution)/shard_map/reduce_scatter | solution.py:250
  1112.1 1957.0 %all-reduce.9.cloned.1.call-start = ((), (), s32[]{:S(2)}) async-start(), calls=%async_computation.11 | async-start | bytes 9830400 | tf_op jit(solution)/shard_map/psum | solution.py:253
  2983.6 84.9 %copy-start.53 = (f32[960]{0:T(1024)S(1)}, f32[960]{0:T(1024)}, u32[]{:S(2)}) copy-start(f32[960]{0:T(1024)} %param.29) | copy-start | bytes 11524
  2983.6 84.9 %copy-start.59 = (f32[960]{0:T(1024)S(1)}, f32[960]{0:T(1024)}, u32[]{:S(2)}) copy-start(f32[960]{0:T(1024)} %param.39) | copy-start | bytes 11524
  2983.6 84.9 %copy-start.60 = (bf16[960]{0:T(1024)(128)(2,1)S(1)}, bf16[960]{0:T(1024)(128)(2,1)}, u32[]{:S(2)}) copy-start(bf16[960]{0:T(1024)(128)(2,1)} %param.34) | copy-start | bytes 5764
  2983.6 85.5 %copy-start.16 = (f32[3,80,1280]{2,1,0:T(8,128)S(1)}, f32[3,80,1280]{2,1,0:T(8,128)}, u32[]{:S(2)}) copy-start(f32[3,80,1280]{2,1,0:T(8,128)} %param.25) | copy-start | bytes 3686404
  (44 other events, 297.2 us)
Sparse Core Ops, SparseCore 0:
  11.4 129.9 all-gather.4
  144.7 85.3 all-gather.6
  233.5 158.6 all-gather.8
  395.4 155.1 all-gather.10
  1055.5 680.0 all-reduce.6
  1737.8 140.4 reduce-scatter.3
  1880.7 540.0 reduce-scatter.5
  2423.0 543.6 reduce-scatter.7
  2970.2 35.3 all-reduce.8
where the time goes:
time: 3100 us; the launch traced here: 3090 us
  waiting for transfers between devices  2190 us (71%)
  matrix products  451 us (15%)
  local copies, waits for them, and re-layouts  171 us (6%)
  blocking collectives  162 us (5%)
  other arithmetic  91.5 us (3%)
    unnamed x10, waiting for transfers between devices  602 us
    reduce_scatter x1, waiting for transfers between devices, local(): lax.psum_scatter(grad_down, 'shard', scatter_dimension=0, tiled=True)  546 us
    reduce_scatter x1, waiting for transfers between devices, local(): lax.psum_scatter(grad_up, 'shard', scatter_dimension=0, tiled=True)  542 us
    ppermute x4, waiting for transfers between devices, from_partner(): return lax.ppermute(value, axis, pairs)  198 us
    unnamed x2, blocking collectives  159 us
    reduce_scatter x1, waiting for transfers between devices, local(): lax.psum_scatter(grad_out_proj, 'shard', scatter_dimension=0, tiled=True)  140 us
    all_gather x1, waiting for transfers between devices, local(): lax.all_gather(copy_down, 'shard', axis=0, tiled=True)  122 us
    dot_general x32, matrix products, scores_of(): jnp.einsum('qd,kd->qk', query_head, key_head, preferred_element_type=jnp....  76.3 us
  transfers between devices with their start and end apart: 13, of which 10 were waited for; matrix products, arithmetic and copies ran while one was open for 11% of the time, Pallas kernels for 0%

commit v1 on v0

v1 whole, which is shorter than its diff:
```python
import functools
import math

import jax
import jax.numpy as jnp
from jax import lax
from jax.experimental import pallas as pl
from jax.experimental.pallas import tpu as pltpu
from jax.sharding import PartitionSpec as P

HEAD_DIM = 80
STEP = 10

LN_EPS = 1e-05
NEG_FILL = -1e30
BETA_ONE = 0.5
BETA_TWO = 0.5
ADAM_EPS = 1e-08
RATES = (0.04, 0.5, 0.04, 0.02, 0.3)
DECAYS = (0.01, 0.01, 0.01, 0.01, 0.0)

F32 = jnp.float32
BF16 = jnp.bfloat16
MIB = 1024 * 1024
SCALING = HEAD_DIM**-0.5
SCORE_SCALE = SCALING * math.log2(math.e)
MASK_ROWS = 16
SMALL_COST = pl.CostEstimate(flops=0, bytes_accessed=MIB, transcendentals=0)
VMEM_SPEC = pl.BlockSpec(memory_space=pltpu.VMEM)
ANY_SPEC = pl.BlockSpec(memory_space=pl.ANY)
NN = (((1,), (0,)), ((), ()))
NT = (((1,), (1,)), ((), ()))


def product(left, right, dims=NN):
    return lax.dot_general(left, right, dims, preferred_element_type=F32)


def call(body, out_shape, limit=48, **options):
    return pl.pallas_call(
        body,
        out_shape=out_shape,
        compiler_params=pltpu.CompilerParams(vmem_limit_bytes=limit * MIB),
        cost_estimate=SMALL_COST,
        **options,
    )


def array(shape, dtype):
    return jax.ShapeDtypeStruct(tuple(shape), dtype)


def xor_pairs(count, mask):
    return [(source, source ^ mask) for source in range(count)]


def across_cores(value):
    return lax.ppermute(value, "rep", xor_pairs(lax.axis_size("rep"), 1))


def swap_clips(value):
    reps, shards = lax.axis_size("rep"), lax.axis_size("shard")
    pairs = []
    for rep in range(reps):
        for shard in range(shards):
            if (rep % 2) != (shard % 2):
                pairs.append((rep * shards + shard, (rep ^ 1) * shards + (shard ^ 1)))
    got = lax.ppermute(value.astype(BF16), ("rep", "shard"), pairs)
    moved = (lax.axis_index("rep") % 2) != (lax.axis_index("shard") % 2)
    return jnp.where(moved, got.astype(value.dtype), value)


def after(value, *others):
    return lax.optimization_barrier((value,) + others)[0]


def flip(index, mask):
    out, bit = index, 1
    while bit <= mask:
        if mask & bit:
            out = out + bit * (1 - 2 * ((index // bit) % 2))
        bit *= 2
    return out


def gather_orders(shards):
    far = [1 << k for k in range(int(math.log2(shards)))][::-1]
    most = [b for b in far if b >= 8]
    axes = {"x": 1, "y": 2, "z": 4}
    names = ("xyz", "xzy", "yxz", "yzx", "zxy", "zyx")
    return {name: most + [axes[axis] for axis in name] for name in names}


def relative_places(order):
    places = [0]
    for mask in order:
        places = places + [mask ^ r for r in places]
    return places


class Doubling:
    def __init__(self, blocks, orders):
        self.held, self.orders, self.step, self.got = blocks, orders, 0, None

    def behind(self, *others):
        self.held = [after(held, *others) for held in self.held]

    def start(self):
        shards = lax.axis_size("shard")
        masks = [order[self.step] for order in self.orders]
        if self.step == 0:
            rows = [held.shape[1] for held in self.held]
            together = jnp.concatenate(self.held, 1)
            together = lax.ppermute(together, "shard", xor_pairs(shards, masks[0]))
            ends = [sum(rows[: i + 1]) for i in range(len(rows))]
            self.got = [together[:, end - row : end] for end, row in zip(ends, rows)]
        else:
            self.got = [
                lax.ppermute(held, "shard", xor_pairs(shards, mask))
                for held, mask in zip(self.held, masks)
            ]
        self.step += 1

    def finish(self, *behind):
        if behind:
            self.got = [after(got, *behind) for got in self.got]
        if self.step < len(self.orders[0]):
            self.held = [jnp.concatenate(pair, 0) for pair in zip(self.held, self.got)]
        return self.held

    def halves(self):
        return list(zip(self.held, self.got, self.orders))

    def pair(self, at):
        part = Doubling(self.held[at : at + 2], self.orders[at : at + 2])
        part.step = self.step
        return part


def scatter_plan(order):
    kept = [0]
    sent = []
    for mask in order[::-1]:
        sent.append([mask ^ r for r in kept])
        kept = kept + sent[-1]
    return sent[::-1] + [[0]]


class Halving:
    def __init__(self, chunks, orders):
        self.chunks, self.orders = chunks, orders
        self.got = [[] for _ in chunks]

    def step(self, *behind):
        index = len(self.got[0])
        shards = lax.axis_size("shard")
        sends = [chunk[index] for chunk in self.chunks]
        if behind:
            sends = [after(send, *behind) for send in sends]
        if index:
            sends = add_blocks(sends, self.got, 1, BF16)
        masks = [order[index] for order in self.orders]
        if index == len(self.orders[0]) - 1 and len(sends) > 1:
            rows = [send.shape[1] for send in sends]
            together = jnp.concatenate(sends, 1)
            together = lax.ppermute(together, "shard", xor_pairs(shards, masks[0]))
            ends = [sum(rows[: i + 1]) for i in range(len(rows))]
            arrived = [together[:, end - row : end] for end, row in zip(ends, rows)]
        else:
            arrived = [
                lax.ppermute(send, "shard", xor_pairs(shards, mask))
                for send, mask in zip(sends, masks)
            ]
        for got, new in zip(self.got, arrived):
            got.append(new)
        return sends

    def result(self, *behind):
        stays = [chunk[-1] for chunk in self.chunks]
        if behind:
            stays = [after(stay, *behind) for stay in stays]
        return add_blocks(stays, self.got, 0, F32)


def over_groups(value):
    reps = lax.axis_size("rep")
    mask = 2
    while mask < reps:
        value = value + lax.ppermute(value, "rep", xor_pairs(reps, mask))
        mask *= 2
    return value


def reduce_small(vector):
    shards, here = lax.axis_size("shard"), lax.axis_index("shard")
    reps = lax.axis_size("rep")
    held, mask = vector, shards // 2
    while mask >= 1:
        upper = (here // mask) % 2 == 1
        low, high = held[:mask], held[mask:]
        got = lax.ppermute(jnp.where(upper, low, high), "shard", xor_pairs(shards, mask))
        held = jnp.where(upper, high, low) + got
        mask //= 2
    held, mask = held[0], 1
    while mask < reps:
        held = held + lax.ppermute(held, "rep", xor_pairs(reps, mask))
        mask *= 2
    return held


def row_slice(start, size):
    return pl.ds(pl.multiple_of(start, 8), size)


def place_first(halves, shards, block, half, cut, small_rows):
    rest = block - 2 * cut

    def body(*refs):
        ins, (qkv, out, small) = refs[:6], refs[6:]
        here = lax.axis_index("shard")
        for index, (low, _, order) in enumerate(halves):
            for place, rel in enumerate(relative_places(order)):
                ref = ins[2 * index + place // low.shape[0]].at[place % low.shape[0]]
                at = flip(here, rel)
                qkv[at, :, index * half : (index + 1) * half] = ref[:block, :]
                if index < 2:
                    out[at, index * cut : (index + 1) * cut, :] = ref[block : block + cut, :]
                else:
                    out[at, 2 * cut :, :] = ref[block : block + rest, :]
                    small[at] = ref[block + rest :, :]

    shapes = (
        array((shards, block, 3 * half), BF16),
        array((shards, block, half), BF16),
        array((shards, small_rows, half), BF16),
    )
    return call(
        body, shapes, in_specs=[VMEM_SPEC] * 6, out_specs=[VMEM_SPEC] * 3, name="place_first"
    )(*[part for low, got, _ in halves for part in (low, got)])


def write_parts(outs, plan, source, here):
    for out, part in zip(outs, plan):
        for place, rel in enumerate(part):
            out[place] = source[flip(here, rel)]


def add_blocks(firsts, others, place, dtype):
    inputs, specs = [], []
    for first, rest in zip(firsts, others):
        inputs.append(first)
        specs.append(pl.BlockSpec(first.shape, lambda i: (0, 0, 0)))
        for other in rest:
            inputs.append(other)
            specs.append(pl.BlockSpec(first.shape, lambda i, at=place: (at, 0, 0)))

    def body(*refs):
        at = 0
        for index, rest in enumerate(others):
            total = refs[at][...].astype(F32)
            for ref in refs[at + 1 : at + 1 + len(rest)]:
                total = total + ref[...].astype(F32)
            refs[len(inputs) + index][...] = total.astype(dtype)
            at += 1 + len(rest)

    return list(call(
        body,
        [array(first.shape, dtype) for first in firsts],
        grid=(1,),
        in_specs=specs,
        out_specs=[pl.BlockSpec(first.shape, lambda i: (0, 0, 0)) for first in firsts],
        name="add_blocks",
    )(*inputs))


def part_shapes(plan, rows, width):
    return [array((len(part), rows, width), BF16) for part in plan]


def norm_rows(values):
    center = values - jnp.mean(values, -1, keepdims=True)
    spread = jnp.mean(center * center, -1, keepdims=True)
    inverse = lax.rsqrt(spread + LN_EPS)
    return center * inverse, inverse


def project(own, other, gain, shift, w_qkv, bias):
    _, padded, width = own.shape
    columns = w_qkv.shape[1]
    third = columns // 3

    def body(own_ref, other_ref, gain_ref, shift_ref, w_ref, bias_ref, normed_ref, out_ref):
        values = jnp.where(pl.program_id(0) == 0, own_ref[...], other_ref[...]).astype(F32)
        unit, _ = norm_rows(values)
        normed = (unit * gain_ref[...] + shift_ref[...]).astype(BF16)
        normed_ref[...] = normed
        for part in range(3):
            cols = slice(part * third, (part + 1) * third)
            result = product(normed, w_ref[:, cols]) + bias_ref[:, cols]
            out_ref[cols, :] = result.astype(BF16).T

    line = pl.BlockSpec((1, width), lambda i: (0, 0))
    rows = pl.BlockSpec((None, padded, width), lambda i: (0, 0, 0))
    return call(
        body,
        (array((2 * padded, width), BF16), array((columns, 2 * padded), BF16)),
        grid=(2,),
        in_specs=[
            rows,
            rows,
            line,
            line,
            pl.BlockSpec((width, columns), lambda i: (0, 0)),
            pl.BlockSpec((1, columns), lambda i: (0, 0)),
        ],
        out_specs=(
            pl.BlockSpec((padded, width), lambda i: (i, 0)),
            pl.BlockSpec((columns, padded), lambda i: (0, i)),
        ),
        name="project",
    )(own, other, gain, shift, w_qkv, bias)


def attend_kernel(mask_ref, q_ref, k_ref, v_ref, out_ref, lse_ref, kt, qt, *, step):
    dim, keys = k_ref.shape
    kt[...] = jnp.zeros_like(kt)
    kt[:dim, :] = k_ref[...]
    kt[dim : dim + MASK_ROWS, :] = mask_ref[:MASK_ROWS, :]
    k_rows = kt[...].T
    qt[...] = jnp.zeros_like(qt)
    qt[:dim, :] = q_ref[...]
    qt[dim : dim + MASK_ROWS, :] = mask_ref[MASK_ROWS:, :]
    for start in range(0, keys, step):
        cols = slice(start, start + step)
        scores = jnp.dot(k_rows, qt[:, cols], preferred_element_type=F32)
        top = jnp.max(scores, 0, keepdims=True) * SCORE_SCALE
        powers = jnp.exp2(scores * SCORE_SCALE - top)
        total = jnp.sum(powers, 0, keepdims=True)
        context = jnp.dot(v_ref[...], powers.astype(BF16), preferred_element_type=F32)
        out_ref[:, cols] = (context / total).astype(BF16)
        lse_ref[:, cols] = top + jnp.log2(total)


def attend(qkv, masks, first, heads):
    _, _, dim, rows = qkv.shape
    step = 512

    def head_block(which):
        return pl.BlockSpec((None, None, dim, rows), lambda h: (which, first + h, 0, 0))

    return pl.pallas_call(
        functools.partial(attend_kernel, step=step),
        grid=(heads,),
        out_shape=(
            jax.ShapeDtypeStruct((heads, dim, rows), BF16),
            jax.ShapeDtypeStruct((heads, 1, rows), F32),
        ),
        in_specs=[
            pl.BlockSpec(masks.shape, lambda h: (0, 0)),
            head_block(0),
            head_block(1),
            head_block(2),
        ],
        out_specs=(
            pl.BlockSpec((None, dim, rows), lambda h: (h, 0, 0)),
            pl.BlockSpec((None, 1, rows), lambda h: (h, 0, 0)),
        ),
        scratch_shapes=[pltpu.VMEM((128, rows), BF16), pltpu.VMEM((128, rows), BF16)],
        compiler_params=pltpu.CompilerParams(vmem_limit_bytes=48 * MIB),
        cost_estimate=SMALL_COST,
        name="attend",
    )(masks, qkv, qkv, qkv)


def attend_back_kernel(
    mask_ref, q_ref, k_ref, v_ref, g_ref, ctx_ref, lse_ref, gq_ref, gk_ref, gv_ref, kt, qt, pad, acc_k, acc_v, *, step
):
    dim, keys = k_ref.shape
    kt[...] = jnp.zeros_like(kt)
    kt[:dim, :] = k_ref[...]
    kt[dim : dim + MASK_ROWS, :] = mask_ref[:MASK_ROWS, :]
    k_rows = kt[...].T
    pad[...] = jnp.zeros_like(pad)
    pad[:dim, :] = v_ref[...]
    v_rows = pad[...].T
    qt[...] = jnp.zeros_like(qt)
    qt[:dim, :] = q_ref[...]
    qt[dim : dim + MASK_ROWS, :] = mask_ref[MASK_ROWS:, :]
    q_rows = qt[...].T
    pad[:dim, :] = g_ref[...]
    g_rows = pad[...].T
    inner = jnp.sum(g_ref[...].astype(F32) * ctx_ref[...].astype(F32), 0, keepdims=True)
    for start in range(0, keys, step):
        cols = slice(start, start + step)
        scores = jnp.dot(k_rows, qt[:, cols], preferred_element_type=F32)
        probs = jnp.exp2(scores * SCORE_SCALE - lse_ref[:, cols])
        grad_probs = jnp.dot(v_rows, pad[:, cols], preferred_element_type=F32)
        grad_scores = (probs * (grad_probs - inner[:, cols])).astype(BF16)
        part_v = jnp.dot(probs.astype(BF16), g_rows[cols, :], preferred_element_type=F32)
        part_k = jnp.dot(grad_scores, q_rows[cols, :], preferred_element_type=F32)
        if start == 0:
            acc_v[...] = part_v
            acc_k[...] = part_k
        else:
            acc_v[...] += part_v
            acc_k[...] += part_k
        grad_query = jnp.dot(k_ref[...], grad_scores, preferred_element_type=F32)
        gq_ref[:, cols] = (grad_query * SCALING).astype(BF16)
    gv_ref[...] = acc_v[...].T[:dim, :].astype(BF16)
    gk_ref[...] = (acc_k[...].T[:dim, :] * SCALING).astype(BF16)


def attend_back(qkv, masks, grad_context, context, lse, first, inside, heads):
    _, dim, rows = context.shape
    step = 512

    def head_block(which):
        return pl.BlockSpec((None, None, dim, rows), lambda h: (which, first + h, 0, 0))

    plain = pl.BlockSpec((None, dim, rows), lambda h: (h, 0, 0))
    return pl.pallas_call(
        functools.partial(attend_back_kernel, step=step),
        grid=(heads,),
        out_shape=[jax.ShapeDtypeStruct((heads, dim, rows), BF16)] * 3,
        in_specs=[
            pl.BlockSpec(masks.shape, lambda h: (0, 0)),
            head_block(0),
            head_block(1),
            head_block(2),
            pl.BlockSpec((None, dim, rows), lambda h: (first + h, 0, 0)),
            pl.BlockSpec((None, dim, rows), lambda h: (inside + h, 0, 0)),
            pl.BlockSpec((None, 1, rows), lambda h: (inside + h, 0, 0)),
        ],
        out_specs=[plain] * 3,
        scratch_shapes=[pltpu.VMEM((128, rows), BF16)] * 3 + [pltpu.VMEM((rows, 128), F32)] * 2,
        compiler_params=pltpu.CompilerParams(vmem_limit_bytes=48 * MIB),
        cost_estimate=SMALL_COST,
        name="attend_back",
    )(masks, qkv, qkv, qkv, grad_context, context, lse)


def attended(contexts, gots, w_own, w_other, frames, bias, gain, shift):
    _, padded, width = frames.shape
    half = width // 2
    step = 256
    tiles = padded // step

    def body(ca, cb, ga, gb, wo_ref, wt_ref, frames_ref, bias_ref, gain_ref, shift_ref, middle_ref, normed_ref):
        first = lax.axis_index("rep") % 2 == 0
        own = jnp.concatenate([ca[...], cb[...]], 0)
        got = jnp.concatenate([ga[...], gb[...]], 0)
        low = jnp.where(first, own, got).T
        high = jnp.where(first, got, own).T
        by_own = product(low, wo_ref[:half, :]) + product(high, wo_ref[half:, :])
        by_other = product(low, wt_ref[:half, :]) + product(high, wt_ref[half:, :])
        result = jnp.concatenate(
            [jnp.where(first, by_own, by_other), jnp.where(first, by_other, by_own)], 1
        )
        middle = result + frames_ref[...].astype(F32) + bias_ref[...]
        middle_ref[...] = middle
        unit, _ = norm_rows(middle)
        normed_ref[...] = (unit * gain_ref[...] + shift_ref[...]).astype(BF16)

    part = half // 2
    line = pl.BlockSpec((1, width), lambda i: (0, 0))
    here = pl.BlockSpec((part, step), lambda i: (0, i))
    there = pl.BlockSpec((part, step), lambda i: (0, i + tiles))
    matrix = pl.BlockSpec((width, half), lambda i: (0, 0))
    rows = pl.BlockSpec((step, width), lambda i: (i, 0))
    return call(
        body,
        (array((padded, width), F32), array((padded, width), BF16)),
        grid=(tiles,),
        in_specs=[here, here, there, there, matrix, matrix]
        + [pl.BlockSpec((None, step, width), lambda i: (0, i, 0)), line, line, line],
        out_specs=(rows, rows),
        name="attended",
    )(*contexts, *gots, w_own, w_other, frames, bias, gain, shift)


def feed(own, other, up_own, up_other, weights, bias, plans):
    padded, width = own.shape
    stacks_given = [part for halves in weights for part in halves[:2]] if isinstance(weights, list) else [weights]
    count_in = len(stacks_given)
    block, units = stacks_given[0].shape[-2:]
    shards = width // block
    tile = 256
    tiles = units // tile
    up_plan, down_plan = plans

    def body(*refs):
        x_refs, u_refs = refs[0:2], refs[2:4]
        stacks, refs = refs[4 : 4 + count_in], refs[4 + count_in :]
        bias_ref, mixed_own, grad_own, send, sums_ref = refs[:5]
        up_outs = refs[5 : 5 + len(up_plan)]
        down_outs = refs[5 + len(up_plan) : 5 + len(up_plan) + len(down_plan)]
        w_up, w_down, hidden_t, x_t, grad_pre, hidden, blocks, sems = refs[5 + len(up_plan) + len(down_plan) :]
        index = pl.program_id(0)
        here = lax.axis_index("shard")

        def rows_step(which):
            x_ref, u_ref = x_refs[which], u_refs[which]
            cols = slice(which * padded, (which + 1) * padded)
            wu, wd = w_up[...].reshape(width, units), w_down[...].reshape(units, width)

            def products(t):
                part = slice(t * tile, (t + 1) * tile)
                return product(x_ref[...], wu[:, part]), product(u_ref[...], wd[part, :], NT)

            ahead = products(0)
            for t in range(tiles):
                part = slice(t * tile, (t + 1) * tile)
                pre, grad_hidden = ahead
                if t + 1 < tiles:
                    ahead = products(t + 1)
                pre = pre + bias_ref[:, part]
                phi = 0.5 + 0.5 * lax.erf(pre * (0.5**0.5))
                hid = (pre * phi).astype(BF16)
                hidden[:, part] = hid
                hidden_t[part, cols] = hid.T
                density = jnp.exp(pre * pre * -0.5) * (1.0 / math.sqrt(2.0 * math.pi))
                grad = (grad_hidden * (phi + pre * density)).astype(BF16)
                grad_pre[cols, part] = grad
                total = jnp.sum(grad.astype(F32), 0, keepdims=True)
                if which == 1:
                    sums_ref[:, part] = total
                else:
                    sums_ref[:, part] += total
            mixed_ref, grad_ref = ((mixed_own, grad_own), (send.at[1], send.at[0]))[which]
            for t in range(width // tile):
                part = slice(t * tile, (t + 1) * tile)
                mixed_ref[:, part] = product(hidden[...], wd[:, part]).astype(mixed_ref.dtype)
                grad_ref[:, part] = product(grad_pre[cols, :], wu[part, :], NT).astype(grad_ref.dtype)

        @pl.when(index == 0)
        def _():
            copies = []

            def copy_in(source, matrix, at):
                copies.append(pltpu.make_async_copy(source, matrix.at[at], sems.at[len(copies)]))
                copies[-1].start()

            for which, matrix in enumerate((w_up, w_down)):
                if count_in == 1:
                    for at in range(shards):
                        copy_in(stacks[0].at[at, which], matrix, at)
                else:
                    for place, rel in enumerate(relative_places(weights[which][2])):
                        stack = stacks[2 * which + place // (shards // 2)]
                        copy_in(stack.at[place % (shards // 2)], matrix, flip(here, rel))
            for which in range(2):
                x_t[:, which * padded : (which + 1) * padded] = x_refs[which][...].T
            for copy in copies:
                copy.wait()
            rows_step(1)

        @pl.when(index == 1)
        def _():
            rows_step(0)

        @pl.when(index >= 2)
        def _():
            part = pl.ds(pl.multiple_of((index - 2) * tile, tile), tile)
            down = product(hidden_t[:, :padded], u_refs[0][:, part]) + product(
                hidden_t[:, padded:], u_refs[1][:, part]
            )
            blocks[...] = down.astype(BF16).reshape(shards, block, tile)
            write_parts(down_outs, down_plan, blocks, here)
            up = product(x_t[...], grad_pre[:, part])
            blocks[...] = up.astype(BF16).reshape(shards, block, tile)
            write_parts(up_outs, up_plan, blocks, here)

    once = pl.Buffered(1)
    whole = pl.BlockSpec((padded, width), lambda i: (0, 0), pipeline_mode=once)
    line = pl.BlockSpec((1, units), lambda i: (0, 0))
    second = pl.BlockSpec((None, padded, width), lambda i: (1, 0, 0), pipeline_mode=once)
    shapes = [
        array((padded, width), F32),
        array((padded, width), F32),
        array((2, padded, width), BF16),
        array((1, units), F32),
    ]
    specs = [
        whole,
        whole,
        pl.BlockSpec((2, padded, width), lambda i: (0, 0, 0), pipeline_mode=once),
        line,
    ]
    for plan, size in ((up_plan, units), (down_plan, width)):
        shapes += part_shapes(plan, block, size)
        specs += [
            pl.BlockSpec((len(part), block, tile), lambda i: (0, 0, jnp.maximum(i - 2, 0)))
            for part in plan
        ]
    results = call(
        body,
        shapes,
        limit=60,
        grid=(2 + tiles,),
        in_specs=[whole, whole, second, second] + [ANY_SPEC] * count_in + [line],
        out_specs=specs,
        scratch_shapes=[
            pltpu.VMEM((shards, block, units), BF16),
            pltpu.VMEM((shards, block, width), BF16),
            pltpu.VMEM((units, 2 * padded), BF16),
            pltpu.VMEM((width, 2 * padded), BF16),
            pltpu.VMEM((2 * padded, units), BF16),
            pltpu.VMEM((padded, units), BF16),
            pltpu.VMEM((shards, block, tile), BF16),
            pltpu.SemaphoreType.DMA((2 * shards,)),
        ],
        name="feed",
    )(own, other, up_own, up_other, *stacks_given, bias)
    count = 4 + len(up_plan)
    return results[:4], results[4:count], results[count:]


def norm_back(sums, values, gain, base, low_out):
    given = [item if isinstance(item, tuple) else (item, None) for item in (*sums, values, base)]
    padded, width = given[0][0].shape[-2:]
    step = 256

    def body(*refs):
        parts = refs[: len(sums)]
        values_ref, base_ref, gain_ref = refs[len(parts) : len(parts) + 3]
        outs = refs[len(parts) + 3 :]
        sums_ref = outs[-1]
        grads = parts[0][...].astype(F32)
        for ref in parts[1:]:
            grads = grads + ref[...].astype(F32)
        unit, inverse = norm_rows(values_ref[...].astype(F32))
        scaled = grads * gain_ref[...]
        inner = (
            scaled
            - jnp.mean(scaled, -1, keepdims=True)
            - unit * jnp.mean(scaled * unit, -1, keepdims=True)
        )
        result = base_ref[...].astype(F32) + inverse * inner
        outs[0][...] = result
        lines = [jnp.sum(grads * unit, 0, keepdims=True), jnp.sum(grads, 0, keepdims=True)]
        if low_out:
            low = result.astype(BF16)
            outs[1][...] = low
            lines.append(jnp.sum(low.astype(F32), 0, keepdims=True))
            lines.append(jnp.sum(base_ref[...].astype(F32), 0, keepdims=True))

        @pl.when(pl.program_id(0) == 0)
        def _():
            sums_ref[...] = jnp.zeros_like(sums_ref)

        for place, line in enumerate(lines):
            sums_ref[place : place + 1, :] += line

    rows = pl.BlockSpec((step, width), lambda i: (i, 0))
    shapes = [array((padded, width), F32)]
    if low_out:
        shapes.append(array((padded, width), BF16))
    shapes.append(array((8, width), F32))
    return call(
        body,
        shapes,
        grid=(padded // step,),
        in_specs=[
            rows
            if place is None
            else pl.BlockSpec((None, step, width), lambda i, place=place: (place, i, 0))
            for _, place in given
        ]
        + [pl.BlockSpec((1, width), lambda i: (0, 0))],
        out_specs=[rows] * (len(shapes) - 1) + [pl.BlockSpec((8, width), lambda i: (0, 0))],
        name="norm_back",
    )(*[item for item, _ in given], gain)


def attended_back(own, other, w_own, w_other, contexts, gots, plan, shards):
    padded, width = own.shape
    half = width // 2
    block = width // shards

    def body(*refs):
        own_ref, other_ref, wo_ref, wt_ref, ca, cb, ga, gb = refs[:8]
        context_ref, outs, blocks = refs[8], refs[9:-1], refs[-1]
        core = lax.axis_index("rep") % 2
        here = lax.axis_index("shard")
        mine = pl.ds(pl.multiple_of(core * half, half), half)
        theirs = pl.ds(pl.multiple_of((1 - core) * half, half), half)
        for place, ref in enumerate((own_ref, other_ref)):
            cols = slice(place * padded, (place + 1) * padded)
            result = product(wo_ref[mine, :], ref[:, mine], NT)
            result = result + product(wt_ref[mine, :], ref[:, theirs], NT)
            context_ref[:, cols] = result.astype(BF16)
        for heads, (pair, near, far) in enumerate(
            (
                ((ca, cb), slice(0, padded), slice(padded, 2 * padded)),
                ((ga, gb), slice(padded, 2 * padded), slice(0, padded)),
            )
        ):
            for place, ref in enumerate(pair):
                result = product(ref[:, near], own_ref[:, mine])
                result = result + product(ref[:, far], other_ref[:, mine])
                count = shards // 4
                at = (core if heads == 0 else 1 - core) * (shards // 2) + place * count
                blocks[pl.ds(at, count)] = result.astype(BF16).reshape(count, block, half)
        write_parts(outs, plan, blocks, here)

    shapes = [array((half, 2 * padded), BF16)] + part_shapes(plan, block, half)
    results = call(
        body,
        shapes,
        in_specs=[VMEM_SPEC] * 8,
        out_specs=[VMEM_SPEC] * len(shapes),
        scratch_shapes=[pltpu.VMEM((shards, block, half), BF16)],
        name="attended_back",
    )(own, other, w_own, w_other, *contexts, *gots)
    return results[0], results[1:]


def project_back(grads, w_qkv):
    part, rows = grads[0].shape
    count = len(grads)
    padded = rows // 2
    width, columns = w_qkv.shape

    def body(*refs):
        w_ref, own_ref, other_ref = refs[count:]

        def run(out_ref):
            stacked = jnp.concatenate([ref[...] for ref in refs[:count]], 0).T
            out_ref[...] = product(stacked, w_ref[...], NT).astype(out_ref.dtype)

        @pl.when(pl.program_id(0) == 0)
        def _():
            run(other_ref)

        @pl.when(pl.program_id(0) == 1)
        def _():
            run(own_ref)

    whole = pl.BlockSpec((padded, width), lambda i: (0, 0))
    return call(
        body,
        (array((padded, width), F32), array((padded, width), BF16)),
        grid=(2,),
        in_specs=[pl.BlockSpec((part, padded), lambda i: (0, 1 - i))] * count
        + [pl.BlockSpec((width, columns), lambda i: (0, 0))],
        out_specs=(whole, whole),
        name="project_back",
    )(*grads, w_qkv)


def project_grads(normed, groups, plans):
    rows, width = normed.shape
    half = sum(piece.shape[0] for piece in groups[0])
    shards = sum(len(p) for p in plans[0])
    block = width // shards
    given = [normed] + [piece for group in groups for piece in group]

    def body(*refs):
        normed_ref, outs, (turned, blocks) = refs[0], refs[len(given) : -2], refs[-2:]
        here = lax.axis_index("shard")
        turned[...] = normed_ref[...].T
        at, place_in = 0, 1
        for group, plan in zip(groups, plans):
            stacked = jnp.concatenate([ref[...] for ref in refs[place_in : place_in + len(group)]], 0)
            place_in += len(group)
            result = product(turned[...], stacked, NT)
            blocks[...] = result.astype(BF16).reshape(shards, block, half)
            write_parts(outs[at : at + len(plan)], plan, blocks, here)
            at += len(plan)

    shapes = []
    for plan in plans:
        shapes += part_shapes(plan, block, half)
    flat = call(
        body,
        shapes,
        in_specs=[VMEM_SPEC] * len(given),
        out_specs=[VMEM_SPEC] * len(shapes),
        scratch_shapes=[pltpu.VMEM((width, rows), BF16), pltpu.VMEM((shards, block, half), BF16)],
        name="project_grads",
    )(*given)
    parts, at = [], 0
    for plan in plans:
        parts.append(list(flat[at : at + len(plan)]))
        at += len(plan)
    return parts


def adam_values(master, moment_one, second, gradient, step_rate, decay_rate):
    momentum = BETA_ONE * moment_one.astype(F32) + (1.0 - BETA_ONE) * gradient
    variance = BETA_TWO * second + (1.0 - BETA_TWO) * gradient * gradient
    momentum_hat = momentum / (1.0 - BETA_ONE**STEP)
    variance_hat = variance / (1.0 - BETA_TWO**STEP)
    updated = master - step_rate * (
        momentum_hat / (jnp.sqrt(variance_hat) + ADAM_EPS) + decay_rate * master
    )
    return updated, updated.astype(BF16), momentum, variance


def adam_feed(own, other, up_state, down_state, shards):
    block, columns = up_state[0].shape
    down_rows, width = down_state[0].shape
    piece = columns // (4 * shards)
    step = 8
    tiles = block // step

    def gradients(refs, core):
        own_refs, other_refs = refs[:4], refs[4:8]
        first = core == 0
        lows = [jnp.where(first, a[0], b[0]) for a, b in zip(own_refs, other_refs)]
        highs = [jnp.where(first, b[0], a[0]) for a, b in zip(own_refs, other_refs)]
        return lows, highs

    def body(*refs):
        core = lax.axis_index("rep") % 2
        lows, highs = gradients(refs, core)
        ups = refs[8:11]
        downs = refs[11:14]
        up_outs, down_outs = refs[14:18], refs[18:22]
        sources = (lows[0], lows[2], highs[0], highs[2])
        gradient = jnp.concatenate(
            [
                source[:, at * piece : (at + 1) * piece]
                for at in range(shards)
                for source in sources
            ],
            1,
        )
        values = adam_values(*[ref[...] for ref in ups], gradient, RATES[2], DECAYS[2])
        for out, value in zip(up_outs, values):
            out[...] = value
        for place, gradient in enumerate((lows[1], lows[3], highs[1], highs[3])):
            values = adam_values(*[ref[place] for ref in downs], gradient, RATES[3], DECAYS[3])
            for out, value in zip(down_outs, values):
                out[place] = value

    grads = [pl.BlockSpec((1, step * 2, g.shape[2]), lambda i: (0, i, 0)) for g in own]
    up_spec = pl.BlockSpec((step * 2, columns), lambda i: (i, 0))
    down_spec = pl.BlockSpec((4, step * 2, width), lambda i: (0, i, 0))
    kinds = (F32, BF16, F32, F32)
    downs = [value.reshape(4, block, width) for value in down_state]
    results = call(
        body,
        [array((block, columns), kind) for kind in kinds]
        + [array((4, block, width), kind) for kind in kinds],
        grid=(-(-block // (step * 2)),),
        in_specs=grads * 2 + [up_spec] * 3 + [down_spec] * 3,
        out_specs=[up_spec] * 4 + [down_spec] * 4,
        name="adam_feed",
    )(*own, *other, *up_state, *downs)
    return tuple(results[:4]), tuple(value.reshape(down_rows, width) for value in results[4:])


def adam_update(master, moment_one, second, gradient, step_rate, decay_rate):
    momentum = BETA_ONE * moment_one.astype(F32) + (1.0 - BETA_ONE) * gradient
    variance = BETA_TWO * second + (1.0 - BETA_TWO) * gradient * gradient
    momentum_hat = momentum / (1.0 - BETA_ONE**STEP)
    variance_hat = variance / (1.0 - BETA_TWO**STEP)
    updated = master - step_rate * (
        momentum_hat / (jnp.sqrt(variance_hat) + ADAM_EPS) + decay_rate * master
    )
    return (updated, updated.astype(BF16), momentum, variance)


def by_core(core, own, other, axis):
    return jnp.where(
        core == 0, jnp.concatenate([own, other], axis), jnp.concatenate([other, own], axis)
    )


def local(
    frames,
    upstream,
    lengths,
    master_qkv,
    master_out,
    master_up,
    master_down,
    master_small,
    first_qkv,
    first_out,
    first_up,
    first_down,
    first_small,
    second_qkv,
    second_out,
    second_up,
    second_down,
    second_small,
):
    half_rows, width = frames.shape
    shards, here = lax.axis_size("shard"), lax.axis_index("shard")
    rep = lax.axis_index("rep")
    core = rep % 2
    padded = -(-half_rows // 256) * 256
    rows = 2 * padded
    half = width // 2
    heads = half // HEAD_DIM
    units = master_up.shape[1] // 2
    unit_block = units // shards
    block = width // shards
    quarter = units // 2
    orders = gather_orders(shards)
    count = len(orders["xyz"])
    cut = 2 * block // 5
    small_rows = 16 * block // 80
    small_size = master_small.shape[0]

    both_moved = swap_clips(jnp.stack([frames, upstream]))
    low_qkv = lax.dynamic_slice_in_dim(master_qkv, core * half, half, 2).astype(BF16)
    low_out = lax.dynamic_slice_in_dim(master_out, core * half, half, 1).astype(BF16)
    low_small = jnp.pad(master_small.astype(BF16), (0, small_rows * half - small_size))
    first_wave = Doubling(
        [
            jnp.concatenate([low_qkv[0], low_out[:cut]], 0)[None],
            jnp.concatenate([low_qkv[1], low_out[cut : 2 * cut]], 0)[None],
            jnp.concatenate(
                [low_qkv[2], low_out[2 * cut :], low_small.reshape(small_rows, half)], 0
            )[None],
        ],
        [orders["xzy"], orders["yxz"], orders["zyx"]],
    )
    first_wave.start()

    low_up = lax.dynamic_index_in_dim(
        master_up.reshape(block, shards, 2, 2, unit_block // 2), core, 2, keepdims=False
    ).astype(BF16)
    low_down = lax.dynamic_slice_in_dim(master_down, core * unit_block, unit_block, 0).astype(BF16)
    low_ups = [low_up[:, :, index].reshape(block, quarter) for index in range(2)]
    wave = Doubling(
        [low_ups[0][None], low_down[None, :block], low_ups[1][None], low_down[None, block:]],
        [orders["zyx"], orders["xzy"], orders["xzy"], orders["yzx"]],
    )

    held = first_wave.finish()
    wave.behind(*held)
    wave.start()
    for step in range(1, count - 1):
        first_wave.start()
        held = first_wave.finish()
    both_own = jnp.pad(after(both_moved, *held), ((0, 0), (0, padded - half_rows), (0, 0)))
    held = wave.finish(both_own)
    first_wave.behind(*held)
    first_wave.start()
    wave_a, wave_b = wave.pair(0), wave.pair(2)
    for step in range(1, count - 3):
        wave_a.start()
        wave_a.finish()
        wave_b.start()
        wave_b.finish()
    wave_a.start()
    w_qkv, w_out_own, small = place_first(first_wave.halves(), shards, block, half, cut, small_rows)
    both_other, w_out_other = (
        across_cores(after(both_own, *first_wave.got)),
        across_cores(after(w_out_own, *wave_a.got).reshape(width, half)),
    )
    w_qkv, w_out_own = w_qkv.reshape(width, 3 * half), w_out_own.reshape(width, half)
    small = small.reshape(shards, -1)[:, :small_size].reshape(-1).astype(F32)
    wave_b.behind(w_qkv)
    wave_b.start()
    held_a = wave_a.finish(w_qkv)
    wave_a.start()

    pieces = [small[index * width : (index + 1) * width] for index in range(8)]
    gain_one, shift_one, bias_query, bias_value, bias_out, gain_two, shift_two, bias_down = [
        piece[None] for piece in pieces
    ]
    bias_up = lax.dynamic_index_in_dim(
        small[8 * width :].reshape(shards, 2, 2, unit_block // 2), core, 1, keepdims=False
    )
    bias_query = lax.dynamic_slice_in_dim(bias_query, core * half, half, 1)
    bias_value = lax.dynamic_slice_in_dim(bias_value, core * half, half, 1)
    bias_qkv = jnp.concatenate([bias_query, jnp.zeros_like(bias_query), bias_value], 1)

    rep_of_clip = 2 * (rep // 2) + here % 2
    clip = (rep_of_clip * shards + here) // 2
    length = lax.dynamic_index_in_dim(lengths, clip, 0, keepdims=False)
    steps = jnp.arange(padded, dtype=jnp.int32)
    positions = jnp.concatenate([core * half_rows + steps, (1 - core) * half_rows + steps])
    real = jnp.concatenate([steps, steps]) < half_rows
    fill = jnp.where(real & (positions < length), 0.0, NEG_FILL).astype(BF16)
    first_row = jnp.arange(MASK_ROWS)[:, None] == 0
    masks = jnp.concatenate(
        [
            jnp.where(first_row, fill[None, :], 0.0),
            jnp.broadcast_to(jnp.where(first_row, 1.0, 0.0), (MASK_ROWS, rows)),
        ],
        0,
    ).astype(BF16)

    normed_one, qkv = project(
        after(both_own, *held_a, *wave_b.held, w_out_other),
        both_other,
        gain_one,
        shift_one,
        w_qkv,
        bias_qkv,
    )
    held = wave_a.finish(qkv) + wave_b.finish(qkv)
    wave_a.start()
    wave_b.start()
    qkv = qkv.reshape(3, heads, HEAD_DIM, rows)
    some = heads // 2
    context_a, lse_a = attend(after(qkv, *held), masks, 0, some)
    context_b, lse_b = attend(after(qkv, context_a), masks, some, heads - some)
    flat_a = context_a.reshape(half // 2, rows)
    flat_b = context_b.reshape(half // 2, rows)
    wave_a.finish(context_b)
    held = wave_b.finish(context_b)
    wave_b.start()
    got_a = across_cores(after(flat_a, *wave_a.got, *held))
    got_b = across_cores(after(flat_b, *wave_a.got, *held))
    middle, normed_own = attended(
        (flat_a, flat_b), (got_a, got_b), w_out_own, w_out_other, both_own, bias_out, gain_two, shift_two
    )
    normed_other = across_cores(normed_own)

    back = {name: order[::-1] for name, order in orders.items()}
    feed_names = (("zxy", "yxz"), ("zxy", "xyz"))
    groups = []

    def feed_half(index, weights, *behind):
        names = feed_names[index]
        sums, up_parts, down_parts = feed(
            after(normed_own, *behind),
            normed_other,
            both_own,
            both_other,
            weights,
            bias_up[:, index].reshape(1, quarter),
            [scatter_plan(back[name]) for name in names],
        )
        return sums, Halving([list(up_parts), list(down_parts)], [back[name] for name in names])

    (mixed_a, grad_a, send_a, sums_up_a), chunks_a = feed_half(0, wave_a.halves(), *held)
    sent = chunks_a.step()
    got_sums_a = across_cores(send_a)
    wave_b.finish(grad_a)
    (mixed_b, grad_b, send_b, sums_up_b), chunks_b = feed_half(1, wave_b.halves(), *sent, send_a)
    arrived = [after(got[0], grad_b) for got in chunks_a.got]
    chunks_a.got = [[got] for got in arrived]
    got_sums_a = after(got_sums_a, grad_b)
    got_sums_b = across_cores(after(send_b, got_sums_a, *arrived))
    grad_middle, grad_attended, sums_two = norm_back(
        (grad_a, grad_b, (got_sums_a, 0), (got_sums_b, 0)),
        middle,
        gain_two,
        (both_own, 1),
        True,
    )
    grad_attended_other = across_cores(grad_attended)
    sent = chunks_b.step(grad_attended_other)
    sent = sent + chunks_a.step(grad_attended_other)
    grad_context, out_parts = attended_back(
        after(grad_attended, *sent),
        grad_attended_other,
        w_out_own,
        w_out_other,
        (flat_a, flat_b),
        (got_a, got_b),
        scatter_plan(back["xyz"]),
        shards,
    )
    chunks_out = Halving([list(out_parts)], [back["xyz"]])
    grad_context = grad_context.reshape(heads, HEAD_DIM, rows)
    calls = 4
    each = heads // calls
    grads = []
    sent = []
    for index in range(calls):
        inside = index * each
        context, lse = (context_a, lse_a) if inside < some else (context_b, lse_b)
        grads.append(
            attend_back(
                after(qkv, *sent), masks, grad_context, context, lse, inside, inside % some, each
            )
        )
        done = grads[-1][0]
        if index == 0:
            mixed = after(mixed_a, done) + mixed_b + got_sums_a[1].astype(F32) + got_sums_b[1].astype(F32)
            mixed = (mixed + bias_down + middle)[:half_rows]
            sent = [mixed] + chunks_out.step(mixed)
        elif index == 1:
            for _ in range(count - 4):
                chunks_a.step(done)
            sent = chunks_a.step(done)
            sent = sent + chunks_b.step(done) + chunks_out.step(done)
        elif index == 2:
            sent = chunks_a.step(done)
            sent = sent + chunks_b.step(done) + chunks_out.step(done)
            for _ in range(count - 4):
                sent = chunks_b.step() + chunks_out.step()
            mixed = after(mixed, *sent)
            sent = sent + [mixed]
            swapped_mixed = swap_clips(mixed)
        else:
            own_a = chunks_a.result(done)
            sent = chunks_b.step(done) + own_a + chunks_out.step(done)
    flat = [[piece[which].reshape(each * HEAD_DIM, rows) for piece in grads] for which in range(3)]
    flat[0][0] = after(flat[0][0], *sent)
    partial_one, send_one = project_back([piece for group in flat for piece in group], w_qkv)
    mixed = after(swapped_mixed, partial_one)
    own_b = chunks_b.result(partial_one)
    (own_out,) = chunks_out.result(partial_one)
    got_one = across_cores(after(send_one, mixed, *own_b, own_out))
    early = [over_groups(value) for value in own_a + own_b + [own_out]]
    cut_rows = block // 2
    wide_out = jnp.concatenate([early[4][:, :cut_rows], early[4][:, cut_rows:]], 2)
    early_other = across_cores(jnp.concatenate(early[:4] + [wide_out], 1))
    grad_frames, sums_one = norm_back(
        (partial_one, got_one), (both_own, 0), gain_one, grad_middle, False
    )
    early_send = grad_frames[:half_rows]
    swapped = swap_clips(early_send)
    names = ("zxy", "xyz", "yzx")
    parts = project_grads(
        after(normed_one, early_send), flat, [scatter_plan(back[name]) for name in names]
    )
    early_other = after(early_other, parts[0][0])
    splits = [early_other[:, i * block : (i + 1) * block] for i in range(4)]
    wide_out = early_other[:, 4 * block :]
    early_other = splits + [jnp.concatenate([wide_out[:, :, :half], wide_out[:, :, half:]], 1)]
    chunks_late = Halving(parts, [back[name] for name in names])
    sent = chunks_late.step(early_other[0])

    def in_half(values):
        return lax.dynamic_update_slice_in_dim(jnp.zeros((width,), F32), values, core * half, 0)

    def head_sums(pieces_of):
        return in_half(jnp.concatenate([jnp.sum(piece.astype(F32), 1) for piece in pieces_of]))

    sums_up = jnp.stack([sums.reshape(shards, unit_block // 2) for sums in (sums_up_a, sums_up_b)], 1)
    sums_up_all = lax.dynamic_update_slice_in_dim(
        jnp.zeros((shards, 2, unit_block), F32), sums_up.reshape(shards, 1, unit_block), core, 1
    )
    grad_small = jnp.concatenate(
        [
            sums_one[0],
            sums_one[1],
            head_sums(flat[0]),
            head_sums(flat[2]),
            sums_two[2],
            sums_two[0],
            sums_two[1],
            sums_two[3],
            sums_up_all.reshape(-1),
        ]
    ).reshape(shards, small_size)
    new_up, new_down = adam_feed(
        [after(early[0], *sent)] + early[1:4],
        early_other[:4],
        (master_up, first_up, second_up),
        (master_down, first_down, second_down),
        shards,
    )
    grad_frames = after(swapped, new_up[0])
    sent = chunks_late.step(new_up[0], grad_frames)
    total_small = reduce_small(after(grad_small, *sent))
    total_out = by_core(core, early[4][0], after(early_other[4], *sent)[0], 1)
    while len(chunks_late.got[0]) < count:
        sent = chunks_late.step()
    late = over_groups(jnp.concatenate(chunks_late.result(), 0))
    late_other = across_cores(late)
    total_qkv = by_core(core, late, late_other, 2)

    new_qkv = adam_update(master_qkv, first_qkv, second_qkv, total_qkv, RATES[0], DECAYS[0])
    new_out = adam_update(master_out, first_out, second_out, total_out, RATES[1], DECAYS[1])
    new_small = adam_update(
        master_small, first_small, second_small, total_small, RATES[4], DECAYS[4]
    )
    return (mixed, grad_frames) + new_qkv + new_out + new_up + new_down + new_small


def solution(mesh):
    rows = P(("rep", "shard"), None)
    weights = (P(None, "shard", None), P("shard", None), P("shard", None), P("shard", None), P("shard"))
    outs = (rows, rows)
    for spec in weights:
        outs = outs + (spec,) * 4
    return jax.shard_map(
        local,
        mesh=mesh,
        in_specs=(rows, rows, P()) + weights * 3,
        out_specs=outs,
        check_vma=False,
    )
```

time: 3100 us -> 708 us (0.23)
  waiting for transfers between devices: 2190 us -> 178 us
  matrix products: 451 us -> 0 us
  Pallas kernels: 0 us -> 313 us
  blocking collectives: 162 us -> 0 us
  local copies, waits for them, and re-layouts: 171 us -> 89.6 us
  starting transfers between devices: 4.55 us -> 79 us
  other arithmetic: 91.5 us -> 36.1 us
    reduce_scatter x3 -> x0, waiting for transfers between devices: 1230 us -> none  [the longest x1 546 us: local(): lax.psum_scatter(grad_down, 'shard', scatter_dimension=0, tiled=True)]
    unnamed x10 -> x0, waiting for transfers between devices: 602 us -> none
    dot_general x124 -> x0, matrix products: 451 us -> none  [the longest x32 76.3 us: scores_of(): jnp.einsum('qd,kd->qk', query_head, key_head, preferred_element_type=jnp....]
    pallas_call x0 -> x33, Pallas kernels: none -> 313 us  [the longest x2 105 us: feed(): call(body, shapes, limit=60, grid=(2 + tiles,), in_specs=[whole, whole, s...]
    all_gather x4 -> x0, waiting for transfers between devices: 166 us -> none  [the longest x1 122 us: local(): lax.all_gather(copy_down, 'shard', axis=0, tiled=True)]
    unnamed x2 -> x0, blocking collectives: 159 us -> none
    ppermute x4 -> x70, starting transfers between devices: 3.92 us -> 79 us  [the longest x25 27.9 us: step(): lax.ppermute(send, 'shard', xor_pairs(shards, mask))]
    slice x11 -> x17, local copies, waits for them, and re-layouts: 48.4 us -> 8.23 us  [the longest x3 1.79 us: step(): arrived = [together[:, end - row:end] for end, row in zip(ends, rows)]]
  transfers between devices with their start and end apart: 13 -> 70, of which waited for: 10 -> 27; matrix products, arithmetic and copies ran while one was open for 11% -> 9% of each run, Pallas kernels for 0% -> 35%
where the time goes in v1:
time: 708 us; the launch traced here: 698 us
  Pallas kernels  313 us (44%)
  waiting for transfers between devices  178 us (25%)
  local copies, waits for them, and re-layouts  89.6 us (13%)
  starting transfers between devices  79 us (11%)
  other arithmetic  36.1 us (5%)
    pallas_call x2, Pallas kernels, feed(): call(body, shapes, limit=60, grid=(2 + tiles,), in_specs=[whole, whole, s...  105 us
    ppermute x21, waiting for transfers between devices, start(): lax.ppermute(held, 'shard', xor_pairs(shards, mask))  87.1 us
    unnamed x334, local copies, waits for them, and re-layouts  58.6 us
    pallas_call x4, Pallas kernels, attend_back(): pl.pallas_call(functools.partial(attend_back_kernel, step=step), grid=(he...  52.2 us
    pallas_call x2, Pallas kernels, attend(): pl.pallas_call(functools.partial(attend_kernel, step=step), grid=(heads,)...  35 us
    ppermute x25, starting transfers between devices, step(): lax.ppermute(send, 'shard', xor_pairs(shards, mask))  27.9 us
    pallas_call x1, Pallas kernels, project(): call(body, (array((2 * padded, width), BF16), array((columns, 2 * padded)...  27.5 us
    ppermute x2, waiting for transfers between devices, start(): together = lax.ppermute(together, 'shard', xor_pairs(shards, masks[0]))  27.4 us
  transfers between devices with their start and end apart: 70, of which 27 were waited for; matrix products, arithmetic and copies ran while one was open for 9% of the time, Pallas kernels for 35%

profile of v1, /device:TPU:0, one launch (start us, length us, event | category | flops | bytes accessed | tf_op | source)
XLA Modules:
  0.0 698.2 jit_solution(7202173841057494884)
XLA Ops:
  3.1 4.9 copy.51
  23.0 13.7 %collective-permute-done.1 = bf16[1,336,640]{2,1,0:T(8,128)(2,1)S(1)} collective-permute-done((bf16[1,336,640]{2,1,0:T(8,128)(2,1)S(1)}, bf16[1,336,640]{2,1,0:T(8,128)(2,1)S(1)}, u32[]{:S(2)}, u32[]{:S(2)}) %collective-permute-start.1) | collective-permute-done | bytes 430112 | tf_op jit(solution)/shard_map/ppermute | solution.py:114
  45.4 16.4 %collective-permute-done.2 = bf16[2,112,640]{2,1,0:T(8,128)(2,1)S(1)} collective-permute-done((bf16[2,112,640]{2,1,0:T(8,128)(2,1)S(1)}, bf16[2,112,640]{2,1,0:T(8,128)(2,1)S(1)}, u32[]{:S(2)}, u32[]{:S(2)}) %collective-permute-start.2) | collective-permute-done | bytes 286752 | tf_op jit(solution)/shard_map/ppermute | solution.py:119
  65.4 13.7 %collective-permute-done.8 = bf16[1,320,1280]{2,1,0:T(8,128)(2,1)S(1)} collective-permute-done((bf16[1,320,1280]{2,1,0:T(8,128)(2,1)S(1)}, bf16[1,320,1280]{2,1,0:T(8,128)(2,1)S(1)}, u32[]{:S(2)}, u32[]{:S(2)}) %collective-permute-start.8) | collective-permute-done | bytes 819232 | tf_op jit(solution)/shard_map/ppermute | solution.py:114
  79.2 8.5 %collective-permute-done.3 = bf16[4,112,640]{2,1,0:T(8,128)(2,1)S(1)} collective-permute-done((bf16[4,112,640]{2,1,0:T(8,128)(2,1)S(1)}, bf16[4,112,640]{2,1,0:T(8,128)(2,1)S(1)}, u32[]{:S(2)}, u32[]{:S(2)}) %collective-permute-start.3) | collective-permute-done | bytes 573472 | tf_op jit(solution)/shard_map/ppermute | solution.py:119
  99.3 23.4 %collective-permute-done.10.refs_1_ = bf16[8,112,640]{2,1,0:T(8,128)(2,1)S(1)} collective-permute-done((bf16[8,112,640]{2,1,0:T(8,128)(2,1)S(1)}, bf16[8,112,640]{2,1,0:T(8,128)(2,1)S(1)}, u32[]{:S(2)}, u32[]{:S(2)}) %collective-permute-start.10) | collective-permute-done | bytes 1146912 | tf_op jit(solution)/shard_map/ppermute | solution.py:119
  152.5 27.5 %project.1 = (bf16[1536,1280]{1,0:T(8,128)(2,1)S(1)}, bf16[1920,1536]{1,0:T(8,128)(2,1)}) custom-call(bf16[2,768,1280]{2,1,0:T(8,128)(2,1)} %pad.9.own_ref.frames_ref.refs_2_.refs_5_, bf16[2,768,1280]{2,1,0:T(8,128)(2,1)} %collective-permute-done.15.other_ref.refs_3_, f32[1,1280]{1,0:T(1,128)S(1)} %broadcast_in_dim.95.gain_ref.refs_4_, ...), custom_call_target="tpu_custom_call" | custom-call | bytes 1048576 | tf_op jit(solution)/shard_map/project/pallas_call | solution.py:304
  189.1 17.3 %attend.2 = (bf16[4,80,1536]{2,1,0:T(8,128)(2,1)S(1)}, f32[4,1,1536]{2,1,0:T(1,128)S(1)}) custom-call(bf16[32,1536]{1,0:T(8,128)(2,1)S(1)} %pad_maximum_fusion.16.mask_ref, bf16[3,8,80,1536]{3,2,1,0:T(8,128)(2,1)} %bitcast.116, bf16[3,8,80,1536]{3,2,1,0:T(8,128)(2,1)} %bitcast.117, bf16[3,8,80,1536]{3,2,1,0:T(8,128)(2,1)} %bitcast.118), custom_call_target="tpu_custom_call" | custom-call | bytes 1048576 | tf_op jit(solution)/shard_map/attend/pallas_call | solution.py:351
  206.5 17.6 %attend.3 = (bf16[4,80,1536]{2,1,0:T(8,128)(2,1)S(1)}, f32[4,1,1536]{2,1,0:T(1,128)S(1)}) custom-call(bf16[32,1536]{1,0:T(8,128)(2,1)S(1)} %pad_maximum_fusion.16.mask_ref, bf16[3,8,80,1536]{3,2,1,0:T(8,128)(2,1)} %bitcast.119, bf16[3,8,80,1536]{3,2,1,0:T(8,128)(2,1)} %bitcast.120, bf16[3,8,80,1536]{3,2,1,0:T(8,128)(2,1)} %bitcast.121), custom_call_target="tpu_custom_call" | custom-call | bytes 1048576 | tf_op jit(solution)/shard_map/attend/pallas_call | solution.py:351
  230.2 8.5 %attended.1 = (f32[768,1280]{1,0:T(8,128)}, bf16[768,1280]{1,0:T(8,128)(2,1)}) custom-call(bf16[320,1536]{1,0:T(8,128)(2,1)S(1)} %bitcast.83, bf16[320,1536]{1,0:T(8,128)(2,1)S(1)} %bitcast.80, bf16[320,1536]{1,0:T(8,128)(2,1)S(1)} %collective-permute-done.24.ga.refs_6_, bf16[320,1536]{1,0:T(8,128)(2,1)S(1)} %collective-permute-done.25.gb.refs_7_, ...), custom_call_target="tpu_custom_call" | custom-call | bytes 1048576 | tf_op jit(solution)/shard_map/attended/pallas_call | solution.py:470
  243.0 46.1 %feed.2 = (f32[768,1280]{1,0:T(8,128)}, f32[768,1280]{1,0:T(8,128)}, bf16[2,768,1280]{2,1,0:T(8,128)(2,1)}, f32[1,1280]{1,0:T(1,128)}, bf16[8,80,1280]{2,1,0:T(8...) custom-call(bf16[768,1280]{1,0:T(8,128)(2,1)} %get-tuple-element.264, ...), custom_call_target="tpu_custom_call" | custom-call | bytes 1048576 | tf_op jit(solution)/shard_map/feed/pallas_call | solution.py:595
  292.7 35.6 %collective-permute-done.27.refs_5_ = bf16[8,80,1280]{2,1,0:T(8,128)(2,1)} collective-permute-done((bf16[8,80,1280]{2,1,0:T(8,128)(2,1)}, bf16[8,80,1280]{2,1,0:T(8,128)(2,1)}, u32[]{:S(2)}, u32[]{:S(2)}) %collective-permute-start.27) | collective-permute-done | bytes 1638432 | tf_op jit(solution)/shard_map/ppermute | solution.py:119
  328.3 59.0 %feed.3 = (f32[768,1280]{1,0:T(8,128)}, f32[768,1280]{1,0:T(8,128)}, bf16[2,768,1280]{2,1,0:T(8,128)(2,1)}, f32[1,1280]{1,0:T(1,128)}, bf16[8,80,1280]{2,1,0:T(8...) custom-call(bf16[768,1280]{1,0:T(8,128)(2,1)} %get-tuple-element.264, ...), custom_call_target="tpu_custom_call" | custom-call | bytes 1048576 | tf_op jit(solution)/shard_map/feed/pallas_call | solution.py:595
  387.5 7.0 collective-permute-done.32.refs_3_
  396.3 8.2 %norm_back.2 = (f32[768,1280]{1,0:T(8,128)S(1)}, bf16[768,1280]{1,0:T(8,128)(2,1)S(1)}, f32[8,1280]{1,0:T(8,128)S(1)}) custom-call(f32[768,1280]{1,0:T(8,128)} %get-tuple-element.260.refs_0_, f32[768,1280]{1,0:T(8,128)} %get-tuple-element.267.refs_1_, bf16[2,768,1280]{2,1,0:T(8,128)(2,1)} %collective-permute-done.29.refs_2_, ...), custom_call_target="tpu_custom_call" | custom-call | bytes 1048576 | tf_op jit(solution)/shard_map/norm_back/pallas_call | solution.py:659
  405.3 5.0 slice_bitcast_fusion.1
  419.3 10.7 %attended_back.1 = (bf16[640,1536]{1,0:T(8,128)(2,1)}, bf16[8,80,640]{2,1,0:T(8,128)(2,1)}, bf16[4,80,640]{2,1,0:T(8,128)(2,1)S(1)}, bf16[2,80,640]{2,1,0:T(8,12...) custom-call(bf16[768,1280]{1,0:T(8,128)(2,1)} %copy-done.26, ...), custom_call_target="tpu_custom_call" | custom-call | bytes 1048576 | tf_op jit(solution)/shard_map/attended_back/pallas_call | solution.py:707
  431.5 13.2 %attend_back.4 = (bf16[2,80,1536]{2,1,0:T(8,128)(2,1)S(1)}, bf16[2,80,1536]{2,1,0:T(8,128)(2,1)S(1)}, bf16[2,80,1536]{2,1,0:T(8,128)(2,1)S(1)}) custom-call(bf16[32,1536]{1,0:T(8,128)(2,1)S(1)} %pad_maximum_fusion.16.mask_ref, bf16[3,8,80,1536]{3,2,1,0:T(8,128)(2,1)} %bitcast.122, bf16[3,8,80,1536]{3,2,1,0:T(8,128)(2,1)} %bitcast.123, ...), custom_call_target="tpu_custom_call" | custom-call | bytes 1048576 | tf_op jit(solution)/shard_map/attend_back/pallas_call | solution.py:421
  444.8 7.6 %slice_add_fusion = f32[750,1280]{1,0:T(8,128)} fusion(f32[768,1280]{1,0:T(8,128)} %get-tuple-element.273.refs_4_, f32[768,1280]{1,0:T(8,128)} %get-tuple-element.290, f32[768,1280]{1,0:T(8,128)} %get-tuple-element.289, f32[1280]{0:T(1024)S(1)} %copy-done.138, bf16[768,1280]{1,0:T(8,128)(2,1)} %slice_bitcast_fusion, bf16[768,1280]{1,0:T(8,128)(2,1)S(1)} %copy-done.109), kind=kLoop, calls=%fused_computation | loop fusion | flops 6720000 | bytes 19205120 | tf_op jit(solution)/shard_map/add | solution.py:1081
  454.2 13.1 %attend_back.5 = (bf16[2,80,1536]{2,1,0:T(8,128)(2,1)S(1)}, bf16[2,80,1536]{2,1,0:T(8,128)(2,1)S(1)}, bf16[2,80,1536]{2,1,0:T(8,128)(2,1)S(1)}) custom-call(bf16[32,1536]{1,0:T(8,128)(2,1)S(1)} %pad_maximum_fusion.16.mask_ref, bf16[3,8,80,1536]{3,2,1,0:T(8,128)(2,1)} %bitcast.125, bf16[3,8,80,1536]{3,2,1,0:T(8,128)(2,1)} %bitcast.126, ...), custom_call_target="tpu_custom_call" | custom-call | bytes 1048576 | tf_op jit(solution)/shard_map/attend_back/pallas_call | solution.py:421
  480.0 13.0 %attend_back.6 = (bf16[2,80,1536]{2,1,0:T(8,128)(2,1)S(1)}, bf16[2,80,1536]{2,1,0:T(8,128)(2,1)S(1)}, bf16[2,80,1536]{2,1,0:T(8,128)(2,1)S(1)}) custom-call(bf16[32,1536]{1,0:T(8,128)(2,1)S(1)} %pad_maximum_fusion.16.mask_ref, bf16[3,8,80,1536]{3,2,1,0:T(8,128)(2,1)} %bitcast.128, bf16[3,8,80,1536]{3,2,1,0:T(8,128)(2,1)} %bitcast.129, ...), custom_call_target="tpu_custom_call" | custom-call | bytes 1048576 | tf_op jit(solution)/shard_map/attend_back/pallas_call | solution.py:421
  498.5 5.4 collective-permute-start.47
  522.4 12.9 %attend_back.7 = (bf16[2,80,1536]{2,1,0:T(8,128)(2,1)S(1)}, bf16[2,80,1536]{2,1,0:T(8,128)(2,1)S(1)}, bf16[2,80,1536]{2,1,0:T(8,128)(2,1)S(1)}) custom-call(bf16[32,1536]{1,0:T(8,128)(2,1)S(1)} %pad_maximum_fusion.16.mask_ref, bf16[3,8,80,1536]{3,2,1,0:T(8,128)(2,1)} %bitcast.131, bf16[3,8,80,1536]{3,2,1,0:T(8,128)(2,1)} %bitcast.132, ...), custom_call_target="tpu_custom_call" | custom-call | bytes 1048576 | tf_op jit(solution)/shard_map/attend_back/pallas_call | solution.py:421
  535.4 12.2 %collective-permute-done.48.refs_3_ = bf16[2,80,640]{2,1,0:T(8,128)(2,1)S(1)} collective-permute-done((bf16[2,80,640]{2,1,0:T(8,128)(2,1)}, bf16[2,80,640]{2,1,0:T(8,128)(2,1)S(1)}, u32[]{:S(2)}, u32[]{:S(2)}) %collective-permute-start.48) | collective-permute-done | bytes 204832 | tf_op jit(solution)/shard_map/ppermute | solution.py:171
  548.6 5.6 collective-permute-start.50
  560.6 14.2 %project_back.1 = (f32[768,1280]{1,0:T(8,128)}, bf16[768,1280]{1,0:T(8,128)(2,1)}) custom-call(bf16[160,1536]{1,0:T(8,128)(2,1)S(1)} %bitcast.88, bf16[160,1536]{1,0:T(8,128)(2,1)S(1)} %bitcast.93, bf16[160,1536]{1,0:T(8,128)(2,1)S(1)} %bitcast.97, bf16[160,1536]{1,0:T(8,128)(2,1)S(1)} %bitcast.101, bf16[160,1536]{1,0:T(8,128)(2,1)S(1)} %bitcast.105, ...), custom_call_target="tpu_custom_call" | custom-call | bytes 1048576 | tf_op jit(solution)/shard_map/project_back/pallas_call | solution.py:740
  592.1 6.5 norm_back.3
  605.0 13.4 %project_grads.1 = (bf16[8,80,640]{2,1,0:T(8,128)(2,1)}, bf16[4,80,640]{2,1,0:T(8,128)(2,1)S(1)}, bf16[2,80,640]{2,1,0:T(8,128)(2,1)S(1)}, bf16[1,80,640]{2,1,0:...) custom-call(bf16[1536,1280]{1,0:T(8,128)(2,1)} %copy-done.20, ...), custom_call_target="tpu_custom_call" | custom-call | bytes 1048576 | tf_op jit(solution)/shard_map/project_grads/pallas_call | solution.py:774
  630.3 9.4 %adam_feed.1 = (f32[80,5120]{1,0:T(8,128)}, bf16[80,5120]{1,0:T(8,128)(2,1)}, f32[80,5120]{1,0:T(8,128)}, f32[80,5120]{1,0:T(8,128)}, f32[4,80,1280]{2,1,0:T(8,1...) custom-call(f32[1,80,1280]{2,1,0:T(8,128)S(1)} %copy-done.44, ...), custom_call_target="tpu_custom_call" | custom-call | bytes 1048576 | tf_op jit(solution)/shard_map/adam_feed/pallas_call | solution.py:842
  640.8 5.0 convert_select_fusion
  663.1 6.6 collective-permute-done.67
  680.0 11.8 %collective-permute-done.63 = bf16[1,240,640]{2,1,0:T(8,128)(2,1)S(1)} collective-permute-done((bf16[1,240,640]{2,1,0:T(8,128)(2,1)S(1)}, bf16[1,240,640]{2,1,0:T(8,128)(2,1)S(1)}, u32[]{:S(2)}, u32[]{:S(2)}) %collective-permute-start.63) | collective-permute-done | bytes 307232 | tf_op jit(solution)/shard_map/ppermute | solution.py:166
  (607 shorter events, 222.3 us)
Async XLA Ops:
  8.0 80.9 %collective-permute-start = (bf16[2,750,1280]{2,0,1:T(2,128)(2,1)}, bf16[2,750,1280]{2,0,1:T(2,128)(2,1)}, u32[]{:S(2)}, u32[]{:S(2)}) collective-permute-start(bf16[2,750,1280]{2,0,1:T(2,128)(2,1)} %copy.51), channel_id=1, source_target_pairs={{1,16},{3,18},{5,20},{7,22},{9,24},{11,26},{13,28},{15,30},{16,1},... | collective-permute-start | bytes 11520008 | tf_op jit(solution)/shard_map/ppermute | solution.py:68
  40.3 38.8 %collective-permute-start.8 = (bf16[1,320,1280]{2,1,0:T(8,128)(2,1)S(1)}, bf16[1,320,1280]{2,1,0:T(8,128)(2,1)S(1)}, u32[]{:S(2)}, u32[]{:S(2)}) collective-permute-start(bf16[1,320,1280]{2,1,0:T(8,128)(2,1)S(1)} %pad_maximum_fusion.4), channel_id=1, source_target_pairs={{0,8},{1,9},{2,10},{3,11},{4,12},{5,13},{6,14},{7,15},{8,0},{9,1},... | collective-permute-start | bytes 2457608 | tf_op jit(solution)/shard_map/ppermute | solution.py:114
  61.9 25.8 %collective-permute-start.3 = (bf16[4,112,640]{2,1,0:T(8,128)(2,1)S(1)}, bf16[4,112,640]{2,1,0:T(8,128)(2,1)S(1)}, u32[]{:S(2)}, u32[]{:S(2)}) collective-permute-start(bf16[4,112,640]{2,1,0:T(8,128)(2,1)S(1)} %pad_maximum_fusion.5), channel_id=1, source_target_pairs={{0,4},{1,5},{2,6},{3,7},{4,0},{5,1},{6,2},{7,3},{8,12},{9,13},{10,... | collective-permute-start | bytes 1720328 | tf_op jit(solution)/shard_map/ppermute | solution.py:119
  98.9 26.4 %collective-permute-start.12 = (bf16[8,112,640]{2,1,0:T(8,128)(2,1)S(1)}, bf16[8,112,640]{2,1,0:T(8,128)(2,1)S(1)}, u32[]{:S(2)}, u32[]{:S(2)}) collective-permute-start(bf16[8,112,640]{2,1,0:T(8,128)(2,1)S(1)} %pad_maximum_fusion.3.refs_4_), channel_id=1, source_target_pairs={{0,1},{1,0},{2,3},{3,2},{4,5},{5,4},{6,7},{7,6},{8,9},{9,8},{10,11... | collective-permute-start | bytes 3440648 | tf_op jit(solution)/shard_map/ppermute | solution.py:119
  126.3 26.2 %collective-permute-start.15 = (bf16[2,768,1280]{2,1,0:T(8,128)(2,1)}, bf16[2,768,1280]{2,1,0:T(8,128)(2,1)}, u32[]{:S(2)}, u32[]{:S(2)}) collective-permute-start(bf16[2,768,1280]{2,1,0:T(8,128)(2,1)} %pad.9.own_ref.frames_ref.refs_2_.refs_5_), channel_id=1, source_target_pairs={{0,16},{16,0},{1,17},{17,1},{2,18},{18,2},{3,19},{19,3},{4,20},{20... | collective-permute-start | bytes 11796488 | tf_op jit(solution)/shard_map/ppermute | solution.py:58
  143.0 38.9 %collective-permute-start.16 = (bf16[4,80,1280]{2,1,0:T(8,128)(2,1)}, bf16[4,80,1280]{2,1,0:T(8,128)(2,1)S(1)}, u32[]{:S(2)}, u32[]{:S(2)}) collective-permute-start(bf16[4,80,1280]{2,1,0:T(8,128)(2,1)} %get-tuple-element.466), channel_id=1, source_target_pairs={{0,2},{1,3},{2,0},{3,1},{4,6},{5,7},{6,4},{7,5},{8,10},{9,11},{10,... | collective-permute-start | bytes 2457608 | tf_op jit(solution)/shard_map/ppermute | solution.py:119
  145.8 36.1 %collective-permute-start.17 = (bf16[4,80,1280]{2,1,0:T(8,128)(2,1)}, bf16[4,80,1280]{2,1,0:T(8,128)(2,1)S(1)}, u32[]{:S(2)}, u32[]{:S(2)}) collective-permute-start(bf16[4,80,1280]{2,1,0:T(8,128)(2,1)} %get-tuple-element.464), channel_id=1, source_target_pairs={{0,4},{1,5},{2,6},{3,7},{4,0},{5,1},{6,2},{7,3},{8,12},{9,13},{10,... | collective-permute-start | bytes 2457608 | tf_op jit(solution)/shard_map/ppermute | solution.py:119
  148.3 33.6 %collective-permute-start.18 = (bf16[2,80,1280]{2,1,0:T(8,128)(2,1)S(1)}, bf16[2,80,1280]{2,1,0:T(8,128)(2,1)S(1)}, u32[]{:S(2)}, u32[]{:S(2)}) collective-permute-start(bf16[2,80,1280]{2,1,0:T(8,128)(2,1)S(1)} %copy-done.129), channel_id=1, source_target_pairs={{0,1},{1,0},{2,3},{3,2},{4,5},{5,4},{6,7},{7,6},{8,9},{9,8},{10,11... | collective-permute-start | bytes 1228808 | tf_op jit(solution)/shard_map/ppermute | solution.py:119
  150.9 31.1 %collective-permute-start.19 = (bf16[2,80,1280]{2,1,0:T(8,128)(2,1)S(1)}, bf16[2,80,1280]{2,1,0:T(8,128)(2,1)S(1)}, u32[]{:S(2)}, u32[]{:S(2)}) collective-permute-start(bf16[2,80,1280]{2,1,0:T(8,128)(2,1)S(1)} %copy-done.127), channel_id=1, source_target_pairs={{0,2},{1,3},{2,0},{3,1},{4,6},{5,7},{6,4},{7,5},{8,10},{9,11},{10,... | collective-permute-start | bytes 1228808 | tf_op jit(solution)/shard_map/ppermute | solution.py:119
  182.0 44.1 %collective-permute-start.20 = (bf16[8,80,1280]{2,1,0:T(8,128)(2,1)S(1)}, bf16[8,80,1280]{2,1,0:T(8,128)(2,1)S(1)}, u32[]{:S(2)}, u32[]{:S(2)}) collective-permute-start(bf16[8,80,1280]{2,1,0:T(8,128)(2,1)S(1)} %constant_dynamic-update-slice_fusion.14.refs_4_), channel_id=1, source_target_pairs={{0,1},{1,0},{2,3},{3,2},{4,5},{5,4},{6,7},{7,6},{8,9},{9,8},{10,11... | collective-permute-start | bytes 4915208 | tf_op jit(solution)/shard_map/ppermute | solution.py:119
  184.0 42.1 %collective-permute-start.21 = (bf16[8,80,1280]{2,1,0:T(8,128)(2,1)S(1)}, bf16[8,80,1280]{2,1,0:T(8,128)(2,1)S(1)}, u32[]{:S(2)}, u32[]{:S(2)}) collective-permute-start(bf16[8,80,1280]{2,1,0:T(8,128)(2,1)S(1)} %constant_dynamic-update-slice_fusion.18.refs_6_), channel_id=1, source_target_pairs={{0,2},{1,3},{2,0},{3,1},{4,6},{5,7},{6,4},{7,5},{8,10},{9,11},{10,... | collective-permute-start | bytes 4915208 | tf_op jit(solution)/shard_map/ppermute | solution.py:119
  186.2 38.0 %collective-permute-start.22 = (bf16[4,80,1280]{2,1,0:T(8,128)(2,1)S(1)}, bf16[4,80,1280]{2,1,0:T(8,128)(2,1)S(1)}, u32[]{:S(2)}, u32[]{:S(2)}) collective-permute-start(bf16[4,80,1280]{2,1,0:T(8,128)(2,1)S(1)} %get-tuple-element.460), channel_id=1, source_target_pairs={{0,4},{1,5},{2,6},{3,7},{4,0},{5,1},{6,2},{7,3},{8,12},{9,13},{10,... | collective-permute-start | bytes 2457608 | tf_op jit(solution)/shard_map/ppermute | solution.py:119
  187.3 36.9 %collective-permute-start.23 = (bf16[4,80,1280]{2,1,0:T(8,128)(2,1)S(1)}, bf16[4,80,1280]{2,1,0:T(8,128)(2,1)S(1)}, u32[]{:S(2)}, u32[]{:S(2)}) collective-permute-start(bf16[4,80,1280]{2,1,0:T(8,128)(2,1)S(1)} %get-tuple-element.456), channel_id=1, source_target_pairs={{0,4},{1,5},{2,6},{3,7},{4,0},{5,1},{6,2},{7,3},{8,12},{9,13},{10,... | collective-permute-start | bytes 2457608 | tf_op jit(solution)/shard_map/ppermute | solution.py:119
  289.2 98.2 %collective-permute-start.29 = (bf16[2,768,1280]{2,1,0:T(8,128)(2,1)}, bf16[2,768,1280]{2,1,0:T(8,128)(2,1)}, u32[]{:S(2)}, u32[]{:S(2)}) collective-permute-start(bf16[2,768,1280]{2,1,0:T(8,128)(2,1)} %get-tuple-element.263), channel_id=1, source_target_pairs={{0,16},{16,0},{1,17},{17,1},{2,18},{18,2},{3,19},{19,3},{4,20},{20... | collective-permute-start | bytes 11796488 | tf_op jit(solution)/shard_map/ppermute | solution.py:58
  289.4 38.9 %collective-permute-start.27 = (bf16[8,80,1280]{2,1,0:T(8,128)(2,1)}, bf16[8,80,1280]{2,1,0:T(8,128)(2,1)}, u32[]{:S(2)}, u32[]{:S(2)}) collective-permute-start(bf16[8,80,1280]{2,1,0:T(8,128)(2,1)} %constant_dynamic-update-slice_fusion.26.refs_4_), channel_id=1, source_target_pairs={{0,2},{1,3},{2,0},{3,1},{4,6},{5,7},{6,4},{7,5},{8,10},{9,11},{10,... | collective-permute-start | bytes 4915208 | tf_op jit(solution)/shard_map/ppermute | solution.py:119
  290.2 38.2 %collective-permute-start.28 = (bf16[8,80,1280]{2,1,0:T(8,128)(2,1)}, bf16[8,80,1280]{2,1,0:T(8,128)(2,1)}, u32[]{:S(2)}, u32[]{:S(2)}) collective-permute-start(bf16[8,80,1280]{2,1,0:T(8,128)(2,1)} %constant_dynamic-update-slice_fusion.29.refs_6_), channel_id=1, source_target_pairs={{0,1},{1,0},{2,3},{3,2},{4,5},{5,4},{6,7},{7,6},{8,9},{9,8},{10,11... | collective-permute-start | bytes 4915208 | tf_op jit(solution)/shard_map/ppermute | solution.py:119
  290.4 96.9 %collective-permute-start.30 = (bf16[8,80,1280]{2,1,0:T(8,128)(2,1)}, bf16[8,80,1280]{2,1,0:T(8,128)(2,1)S(1)}, u32[]{:S(2)}, u32[]{:S(2)}) collective-permute-start(bf16[8,80,1280]{2,1,0:T(8,128)(2,1)} %get-tuple-element.261), channel_id=1, source_target_pairs={{0,2},{1,3},{2,0},{3,1},{4,6},{5,7},{6,4},{7,5},{8,10},{9,11},{10,... | collective-permute-start | bytes 4915208 | tf_op jit(solution)/shard_map/ppermute | solution.py:171
  291.7 95.7 %collective-permute-start.31 = (bf16[8,80,1280]{2,1,0:T(8,128)(2,1)}, bf16[8,80,1280]{2,1,0:T(8,128)(2,1)}, u32[]{:S(2)}, u32[]{:S(2)}) collective-permute-start(bf16[8,80,1280]{2,1,0:T(8,128)(2,1)} %get-tuple-element.262), channel_id=1, source_target_pairs={{0,4},{1,5},{2,6},{3,7},{4,0},{5,1},{6,2},{7,3},{8,12},{9,13},{10,... | collective-permute-start | bytes 4915208 | tf_op jit(solution)/shard_map/ppermute | solution.py:171
  415.7 52.3 %collective-permute-start.34 = (bf16[4,80,1280]{2,1,0:T(8,128)(2,1)}, bf16[4,80,1280]{2,1,0:T(8,128)(2,1)S(1)}, u32[]{:S(2)}, u32[]{:S(2)}) collective-permute-start(bf16[4,80,1280]{2,1,0:T(8,128)(2,1)} %get-tuple-element.283), channel_id=1, source_target_pairs={{0,1},{1,0},{2,3},{3,2},{4,5},{5,4},{6,7},{7,6},{8,9},{9,8},{10,11... | collective-permute-start | bytes 2457608 | tf_op jit(solution)/shard_map/ppermute | solution.py:171
  416.0 52.1 %collective-permute-start.35 = (bf16[4,80,1280]{2,1,0:T(8,128)(2,1)}, bf16[4,80,1280]{2,1,0:T(8,128)(2,1)S(1)}, u32[]{:S(2)}, u32[]{:S(2)}) collective-permute-start(bf16[4,80,1280]{2,1,0:T(8,128)(2,1)} %get-tuple-element.284), channel_id=1, source_target_pairs={{0,1},{1,0},{2,3},{3,2},{4,5},{5,4},{6,7},{7,6},{8,9},{9,8},{10,11... | collective-permute-start | bytes 2457608 | tf_op jit(solution)/shard_map/ppermute | solution.py:171
  417.8 54.2 %collective-permute-start.36 = (bf16[8,80,1280]{2,1,0:T(8,128)(2,1)}, bf16[8,80,1280]{2,1,0:T(8,128)(2,1)S(1)}, u32[]{:S(2)}, u32[]{:S(2)}) collective-permute-start(bf16[8,80,1280]{2,1,0:T(8,128)(2,1)} %get-tuple-element.276), channel_id=1, source_target_pairs={{0,2},{1,3},{2,0},{3,1},{4,6},{5,7},{6,4},{7,5},{8,10},{9,11},{10,... | collective-permute-start | bytes 4915208 | tf_op jit(solution)/shard_map/ppermute | solution.py:171
  419.0 53.0 %collective-permute-start.37 = (bf16[8,80,1280]{2,1,0:T(8,128)(2,1)}, bf16[8,80,1280]{2,1,0:T(8,128)(2,1)}, u32[]{:S(2)}, u32[]{:S(2)}) collective-permute-start(bf16[8,80,1280]{2,1,0:T(8,128)(2,1)} %get-tuple-element.278), channel_id=1, source_target_pairs={{0,4},{1,5},{2,6},{3,7},{4,0},{5,1},{6,2},{7,3},{8,12},{9,13},{10,... | collective-permute-start | bytes 4915208 | tf_op jit(solution)/shard_map/ppermute | solution.py:171
  476.9 31.7 %collective-permute-start.41 = (bf16[4,80,1280]{2,1,0:T(8,128)(2,1)}, bf16[4,80,1280]{2,1,0:T(8,128)(2,1)S(1)}, u32[]{:S(2)}, u32[]{:S(2)}) collective-permute-start(bf16[4,80,1280]{2,1,0:T(8,128)(2,1)} %get-tuple-element.306), channel_id=1, source_target_pairs={{0,1},{1,0},{2,3},{3,2},{4,5},{5,4},{6,7},{7,6},{8,9},{9,8},{10,11... | collective-permute-start | bytes 2457608 | tf_op jit(solution)/shard_map/ppermute | solution.py:171
  477.2 31.4 %collective-permute-start.42 = (bf16[4,80,1280]{2,1,0:T(8,128)(2,1)}, bf16[4,80,1280]{2,1,0:T(8,128)(2,1)S(1)}, u32[]{:S(2)}, u32[]{:S(2)}) collective-permute-start(bf16[4,80,1280]{2,1,0:T(8,128)(2,1)} %get-tuple-element.307), channel_id=1, source_target_pairs={{0,2},{1,3},{2,0},{3,1},{4,6},{5,7},{6,4},{7,5},{8,10},{9,11},{10,... | collective-permute-start | bytes 2457608 | tf_op jit(solution)/shard_map/ppermute | solution.py:171
  478.9 28.9 %collective-permute-start.43 = (bf16[4,80,640]{2,1,0:T(8,128)(2,1)}, bf16[4,80,640]{2,1,0:T(8,128)(2,1)S(1)}, u32[]{:S(2)}, u32[]{:S(2)}) collective-permute-start(bf16[4,80,640]{2,1,0:T(8,128)(2,1)} %add_blocks.19), channel_id=1, source_target_pairs={{0,2},{1,3},{2,0},{3,1},{4,6},{5,7},{6,4},{7,5},{8,10},{9,11},{10,... | collective-permute-start | bytes 1228808 | tf_op jit(solution)/shard_map/ppermute | solution.py:171
  514.2 65.6 %collective-permute-start.44 = (bf16[750,1280]{1,0:T(8,128)(2,1)}, bf16[750,1280]{1,0:T(8,128)(2,1)}, u32[]{:S(2)}, u32[]{:S(2)}) collective-permute-start(bf16[750,1280]{1,0:T(8,128)(2,1)} %convert_element_type.133), channel_id=1, source_target_pairs={{1,16},{3,18},{5,20},{7,22},{9,24},{11,26},{13,28},{15,30},{16,1},... | collective-permute-start | bytes 5760008 | tf_op jit(solution)/shard_map/ppermute | solution.py:68
  516.1 31.5 %collective-permute-start.48 = (bf16[2,80,640]{2,1,0:T(8,128)(2,1)}, bf16[2,80,640]{2,1,0:T(8,128)(2,1)S(1)}, u32[]{:S(2)}, u32[]{:S(2)}) collective-permute-start(bf16[2,80,640]{2,1,0:T(8,128)(2,1)} %add_blocks.22), channel_id=1, source_target_pairs={{0,1},{1,0},{2,3},{3,2},{4,5},{5,4},{6,7},{7,6},{8,9},{9,8},{10,11... | collective-permute-start | bytes 614408 | tf_op jit(solution)/shard_map/ppermute | solution.py:171
  516.6 39.8 %collective-permute-start.45 = (bf16[2,80,1280]{2,1,0:T(8,128)(2,1)}, bf16[2,80,1280]{2,1,0:T(8,128)(2,1)S(1)}, u32[]{:S(2)}, u32[]{:S(2)}) collective-permute-start(bf16[2,80,1280]{2,1,0:T(8,128)(2,1)} %get-tuple-element.322), channel_id=1, source_target_pairs={{0,4},{1,5},{2,6},{3,7},{4,0},{5,1},{6,2},{7,3},{8,12},{9,13},{10,... | collective-permute-start | bytes 1228808 | tf_op jit(solution)/shard_map/ppermute | solution.py:171
  518.2 38.2 %collective-permute-start.46 = (bf16[2,80,1280]{2,1,0:T(8,128)(2,1)}, bf16[2,80,1280]{2,1,0:T(8,128)(2,1)}, u32[]{:S(2)}, u32[]{:S(2)}) collective-permute-start(bf16[2,80,1280]{2,1,0:T(8,128)(2,1)} %get-tuple-element.323), channel_id=1, source_target_pairs={{0,1},{1,0},{2,3},{3,2},{4,5},{5,4},{6,7},{7,6},{8,9},{9,8},{10,11... | collective-permute-start | bytes 1228808 | tf_op jit(solution)/shard_map/ppermute | solution.py:171
  548.6 26.2 %collective-permute-start.50 = (bf16[1,80,640]{2,1,0:T(8,128)(2,1)S(1)}, bf16[1,80,640]{2,1,0:T(8,128)(2,1)S(1)}, u32[]{:S(2)}, u32[]{:S(2)}) collective-permute-start(bf16[1,80,640]{2,1,0:T(8,128)(2,1)S(1)} %add_blocks.25), channel_id=1, source_target_pairs={{0,8},{1,9},{2,10},{3,11},{4,12},{5,13},{6,14},{7,15},{8,0},{9,1},... | collective-permute-start | bytes 307208 | tf_op jit(solution)/shard_map/ppermute | solution.py:171
  587.0 38.6 %collective-permute-start.53 = (f32[1,360,1280]{2,1,0:T(8,128)}, f32[1,360,1280]{2,1,0:T(8,128)}, u32[]{:S(2)}, u32[]{:S(2)}) collective-permute-start(f32[1,360,1280]{2,1,0:T(8,128)} %maximum_dynamic-update-slice_fusion), channel_id=1, source_target_pairs={{0,16},{16,0},{1,17},{17,1},{2,18},{18,2},{3,19},{19,3},{4,20},{20... | collective-permute-start | bytes 5529608 | tf_op jit(solution)/shard_map/ppermute | solution.py:58
  602.0 38.9 %collective-permute-start.52 = (bf16[750,1280]{1,0:T(8,128)(2,1)}, bf16[750,1280]{1,0:T(8,128)(2,1)}, u32[]{:S(2)}, u32[]{:S(2)}) collective-permute-start(bf16[750,1280]{1,0:T(8,128)(2,1)} %slice.352), channel_id=1, source_target_pairs={{1,16},{3,18},{5,20},{7,22},{9,24},{11,26},{13,28},{15,30},{16,1},... | collective-permute-start | bytes 5760008 | tf_op jit(solution)/shard_map/ppermute | solution.py:68
  (190 other events, 2244.6 us)

commit v2 on v1

--- a/solution.py
+++ b/solution.py
@@ -58,16 +58,25 @@
     return lax.ppermute(value, "rep", xor_pairs(lax.axis_size("rep"), 1))
 
 
-def swap_clips(value):
+def swap_pairs():
     reps, shards = lax.axis_size("rep"), lax.axis_size("shard")
     pairs = []
     for rep in range(reps):
         for shard in range(shards):
             if (rep % 2) != (shard % 2):
                 pairs.append((rep * shards + shard, (rep ^ 1) * shards + (shard ^ 1)))
-    got = lax.ppermute(value.astype(BF16), ("rep", "shard"), pairs)
+    return pairs
+
+
+def swap_clips(own, sent):
+    got = lax.ppermute(sent, ("rep", "shard"), swap_pairs())
     moved = (lax.axis_index("rep") % 2) != (lax.axis_index("shard") % 2)
-    return jnp.where(moved, got.astype(value.dtype), value)
+
+    def finish(*behind):
+        arrived = (after(got, *behind) if behind else got)[: own.shape[0]]
+        return jnp.where(moved, arrived.astype(own.dtype), own)
+
+    return finish, got
 
 
 def after(value, *others):
@@ -191,21 +200,35 @@
     return value
 
 
-def reduce_small(vector):
-    shards, here = lax.axis_size("shard"), lax.axis_index("shard")
-    reps = lax.axis_size("rep")
-    held, mask = vector, shards // 2
-    while mask >= 1:
-        upper = (here // mask) % 2 == 1
-        low, high = held[:mask], held[mask:]
-        got = lax.ppermute(jnp.where(upper, low, high), "shard", xor_pairs(shards, mask))
-        held = jnp.where(upper, high, low) + got
-        mask //= 2
-    held, mask = held[0], 1
-    while mask < reps:
-        held = held + lax.ppermute(held, "rep", xor_pairs(reps, mask))
-        mask *= 2
-    return held
+class SmallSum:
+    def __init__(self, vector):
+        self.held, self.mask = vector, vector.shape[0] // 2
+        self.kept = self.got = None
+
+    def start(self):
+        shards, here = lax.axis_size("shard"), lax.axis_index("shard")
+        upper = (here // self.mask) % 2 == 1
+        low, high = self.held[: self.mask], self.held[self.mask :]
+        self.kept = jnp.where(upper, high, low)
+        self.got = lax.ppermute(
+            jnp.where(upper, low, high), "shard", xor_pairs(shards, self.mask)
+        )
+        self.mask //= 2
+
+    def finish(self, *behind):
+        self.held = self.kept + (after(self.got, *behind) if behind else self.got)
+        return self.held
+
+    def result(self):
+        while self.mask >= 1:
+            self.start()
+            self.finish()
+        reps = lax.axis_size("rep")
+        held, mask = self.held[0], 1
+        while mask < reps:
+            held = held + lax.ppermute(held, "rep", xor_pairs(reps, mask))
+            mask *= 2
+        return held
 
 
 def row_slice(start, size):
@@ -285,12 +308,14 @@
 
 
 def project(own, other, gain, shift, w_qkv, bias):
-    _, padded, width = own.shape
+    padded, width = own.shape
     columns = w_qkv.shape[1]
     third = columns // 3
+    step = padded // 2
 
     def body(own_ref, other_ref, gain_ref, shift_ref, w_ref, bias_ref, normed_ref, out_ref):
-        values = jnp.where(pl.program_id(0) == 0, own_ref[...], other_ref[...]).astype(F32)
+        index = pl.program_id(0)
+        values = jnp.where(index < 2, own_ref[...], other_ref[...]).astype(F32)
         unit, _ = norm_rows(values)
         normed = (unit * gain_ref[...] + shift_ref[...]).astype(BF16)
         normed_ref[...] = normed
@@ -300,22 +325,21 @@
             out_ref[cols, :] = result.astype(BF16).T
 
     line = pl.BlockSpec((1, width), lambda i: (0, 0))
-    rows = pl.BlockSpec((None, padded, width), lambda i: (0, 0, 0))
     return call(
         body,
         (array((2 * padded, width), BF16), array((columns, 2 * padded), BF16)),
-        grid=(2,),
+        grid=(4,),
         in_specs=[
-            rows,
-            rows,
+            pl.BlockSpec((step, width), lambda i: (jnp.minimum(i, 1), 0)),
+            pl.BlockSpec((step, width), lambda i: (jnp.maximum(i - 2, 0), 0)),
             line,
             line,
             pl.BlockSpec((width, columns), lambda i: (0, 0)),
             pl.BlockSpec((1, columns), lambda i: (0, 0)),
         ],
         out_specs=(
-            pl.BlockSpec((padded, width), lambda i: (i, 0)),
-            pl.BlockSpec((columns, padded), lambda i: (0, i)),
+            pl.BlockSpec((step, width), lambda i: (i, 0)),
+            pl.BlockSpec((columns, step), lambda i: (0, i)),
         ),
         name="project",
     )(own, other, gain, shift, w_qkv, bias)
@@ -440,7 +464,7 @@
 
 
 def attended(contexts, gots, w_own, w_other, frames, bias, gain, shift):
-    _, padded, width = frames.shape
+    padded, width = frames.shape
     half = width // 2
     step = 256
     tiles = padded // step
@@ -471,8 +495,7 @@
         body,
         (array((padded, width), F32), array((padded, width), BF16)),
         grid=(tiles,),
-        in_specs=[here, here, there, there, matrix, matrix]
-        + [pl.BlockSpec((None, step, width), lambda i: (0, i, 0)), line, line, line],
+        in_specs=[here, here, there, there, matrix, matrix, rows, line, line, line],
         out_specs=(rows, rows),
         name="attended",
     )(*contexts, *gots, w_own, w_other, frames, bias, gain, shift)
@@ -573,7 +596,6 @@
     once = pl.Buffered(1)
     whole = pl.BlockSpec((padded, width), lambda i: (0, 0), pipeline_mode=once)
     line = pl.BlockSpec((1, units), lambda i: (0, 0))
-    second = pl.BlockSpec((None, padded, width), lambda i: (1, 0, 0), pipeline_mode=once)
     shapes = [
         array((padded, width), F32),
         array((padded, width), F32),
@@ -597,7 +619,7 @@
         shapes,
         limit=60,
         grid=(2 + tiles,),
-        in_specs=[whole, whole, second, second] + [ANY_SPEC] * count_in + [line],
+        in_specs=[whole] * 4 + [ANY_SPEC] * count_in + [line],
         out_specs=specs,
         scratch_shapes=[
             pltpu.VMEM((shards, block, units), BF16),
@@ -615,7 +637,7 @@
     return results[:4], results[4:count], results[count:]
 
 
-def norm_back(sums, values, gain, base, low_out):
+def norm_back(sums, values, gain, base, more_sums):
     given = [item if isinstance(item, tuple) else (item, None) for item in (*sums, values, base)]
     padded, width = given[0][0].shape[-2:]
     step = 256
@@ -637,10 +659,10 @@
         )
         result = base_ref[...].astype(F32) + inverse * inner
         outs[0][...] = result
+        low = result.astype(BF16)
+        outs[1][...] = low
         lines = [jnp.sum(grads * unit, 0, keepdims=True), jnp.sum(grads, 0, keepdims=True)]
-        if low_out:
-            low = result.astype(BF16)
-            outs[1][...] = low
+        if more_sums:
             lines.append(jnp.sum(low.astype(F32), 0, keepdims=True))
             lines.append(jnp.sum(base_ref[...].astype(F32), 0, keepdims=True))
 
@@ -652,10 +674,7 @@
             sums_ref[place : place + 1, :] += line
 
     rows = pl.BlockSpec((step, width), lambda i: (i, 0))
-    shapes = [array((padded, width), F32)]
-    if low_out:
-        shapes.append(array((padded, width), BF16))
-    shapes.append(array((8, width), F32))
+    shapes = [array((padded, width), F32), array((padded, width), BF16), array((8, width), F32)]
     return call(
         body,
         shapes,
@@ -670,6 +689,28 @@
         out_specs=[rows] * (len(shapes) - 1) + [pl.BlockSpec((8, width), lambda i: (0, 0))],
         name="norm_back",
     )(*[item for item, _ in given], gain)
+
+
+def mix(own_a, own_b, got_a, got_b, middle, bias):
+    padded, width = middle.shape
+    step = 256
+
+    def body(a_ref, b_ref, ga_ref, gb_ref, middle_ref, bias_ref, out_ref, low_ref):
+        total = a_ref[...] + b_ref[...] + ga_ref[...].astype(F32) + gb_ref[...].astype(F32)
+        total = total + bias_ref[...] + middle_ref[...]
+        out_ref[...] = total
+        low_ref[...] = total.astype(BF16)
+
+    rows = pl.BlockSpec((step, width), lambda i: (i, 0))
+    plane = pl.BlockSpec((None, step, width), lambda i: (1, i, 0))
+    return call(
+        body,
+        (array((padded, width), F32), array((padded, width), BF16)),
+        grid=(padded // step,),
+        in_specs=[rows, rows, plane, plane, rows, pl.BlockSpec((1, width), lambda i: (0, 0))],
+        out_specs=(rows, rows),
+        name="mix",
+    )(own_a, own_b, got_a, got_b, middle, bias)
 
 
 def attended_back(own, other, w_own, w_other, contexts, gots, plan, shards):
@@ -906,7 +947,7 @@
     small_rows = 16 * block // 80
     small_size = master_small.shape[0]
 
-    both_moved = swap_clips(jnp.stack([frames, upstream]))
+    frames_moved, _ = swap_clips(frames, frames)
     low_qkv = lax.dynamic_slice_in_dim(master_qkv, core * half, half, 2).astype(BF16)
     low_out = lax.dynamic_slice_in_dim(master_out, core * half, half, 1).astype(BF16)
     low_small = jnp.pad(master_small.astype(BF16), (0, small_rows * half - small_size))
@@ -932,16 +973,21 @@
         [orders["zyx"], orders["xzy"], orders["xzy"], orders["yzx"]],
     )
 
+    def own_half(values):
+        return jnp.pad(values, ((0, padded - half_rows), (0, 0)))
+
     held = first_wave.finish()
-    wave.behind(*held)
-    wave.start()
     for step in range(1, count - 1):
         first_wave.start()
+        if step == count - 2:
+            wave.behind(*held)
+            wave.start()
         held = first_wave.finish()
-    both_own = jnp.pad(after(both_moved, *held), ((0, 0), (0, padded - half_rows), (0, 0)))
-    held = wave.finish(both_own)
-    first_wave.behind(*held)
+    frames_own = own_half(frames_moved(*held))
+    first_wave.behind(frames_own)
     first_wave.start()
+    upstream_moved, upstream_got = swap_clips(upstream, after(upstream, frames_own))
+    wave.finish(*first_wave.got)
     wave_a, wave_b = wave.pair(0), wave.pair(2)
     for step in range(1, count - 3):
         wave_a.start()
@@ -949,17 +995,15 @@
         wave_b.start()
         wave_b.finish()
     wave_a.start()
+    frames_other = across_cores(after(frames_own, *first_wave.got))
     w_qkv, w_out_own, small = place_first(first_wave.halves(), shards, block, half, cut, small_rows)
-    both_other, w_out_other = (
-        across_cores(after(both_own, *first_wave.got)),
-        across_cores(after(w_out_own, *wave_a.got).reshape(width, half)),
-    )
-    w_qkv, w_out_own = w_qkv.reshape(width, 3 * half), w_out_own.reshape(width, half)
+    w_out_own = w_out_own.reshape(width, half)
+    held_a = wave_a.finish(w_qkv)
+    wave_b.behind(*held_a)
+    wave_a.start()
+    wave_b.start()
+    w_qkv = w_qkv.reshape(width, 3 * half)
     small = small.reshape(shards, -1)[:, :small_size].reshape(-1).astype(F32)
-    wave_b.behind(w_qkv)
-    wave_b.start()
-    held_a = wave_a.finish(w_qkv)
-    wave_a.start()
 
     pieces = [small[index * width : (index + 1) * width] for index in range(8)]
     gain_one, shift_one, bias_query, bias_value, bias_out, gain_two, shift_two, bias_down = [
@@ -989,29 +1033,30 @@
     ).astype(BF16)
 
     normed_one, qkv = project(
-        after(both_own, *held_a, *wave_b.held, w_out_other),
-        both_other,
-        gain_one,
-        shift_one,
-        w_qkv,
-        bias_qkv,
+        after(frames_own, *wave_a.held, *wave_b.held), frames_other, gain_one, shift_one, w_qkv, bias_qkv
     )
     held = wave_a.finish(qkv) + wave_b.finish(qkv)
+    w_out_other = across_cores(after(w_out_own, *held))
+    upstream_own = own_half(upstream_moved(qkv, *held))
+    wave_a.behind(w_out_other, upstream_own)
+    wave_b.behind(w_out_other, upstream_own)
     wave_a.start()
     wave_b.start()
+    upstream_other = across_cores(upstream_own)
     qkv = qkv.reshape(3, heads, HEAD_DIM, rows)
     some = heads // 2
-    context_a, lse_a = attend(after(qkv, *held), masks, 0, some)
+    context_a, lse_a = attend(after(qkv, *wave_a.held, *wave_b.held), masks, 0, some)
     context_b, lse_b = attend(after(qkv, context_a), masks, some, heads - some)
     flat_a = context_a.reshape(half // 2, rows)
     flat_b = context_b.reshape(half // 2, rows)
     wave_a.finish(context_b)
-    held = wave_b.finish(context_b)
+    upstream_other = after(upstream_other, context_b)
+    held = wave_b.finish(context_b, upstream_other)
     wave_b.start()
     got_a = across_cores(after(flat_a, *wave_a.got, *held))
     got_b = across_cores(after(flat_b, *wave_a.got, *held))
     middle, normed_own = attended(
-        (flat_a, flat_b), (got_a, got_b), w_out_own, w_out_other, both_own, bias_out, gain_two, shift_two
+        (flat_a, flat_b), (got_a, got_b), w_out_own, w_out_other, frames_own, bias_out, gain_two, shift_two
     )
     normed_other = across_cores(normed_own)
 
@@ -1024,8 +1069,8 @@
         sums, up_parts, down_parts = feed(
             after(normed_own, *behind),
             normed_other,
-            both_own,
-            both_other,
+            upstream_own,
+            upstream_other,
             weights,
             bias_up[:, index].reshape(1, quarter),
             [scatter_plan(back[name]) for name in names],
@@ -1033,9 +1078,10 @@
         return sums, Halving([list(up_parts), list(down_parts)], [back[name] for name in names])
 
     (mixed_a, grad_a, send_a, sums_up_a), chunks_a = feed_half(0, wave_a.halves(), *held)
-    sent = chunks_a.step()
+    wave_b.finish(grad_a)
+    sent = chunks_a.step(*wave_b.got)
+    send_a = after(send_a, *wave_b.got)
     got_sums_a = across_cores(send_a)
-    wave_b.finish(grad_a)
     (mixed_b, grad_b, send_b, sums_up_b), chunks_b = feed_half(1, wave_b.halves(), *sent, send_a)
     arrived = [after(got[0], grad_b) for got in chunks_a.got]
     chunks_a.got = [[got] for got in arrived]
@@ -1045,7 +1091,7 @@
         (grad_a, grad_b, (got_sums_a, 0), (got_sums_b, 0)),
         middle,
         gain_two,
-        (both_own, 1),
+        upstream_own,
         True,
     )
     grad_attended_other = across_cores(grad_attended)
@@ -1077,9 +1123,10 @@
         )
         done = grads[-1][0]
         if index == 0:
-            mixed = after(mixed_a, done) + mixed_b + got_sums_a[1].astype(F32) + got_sums_b[1].astype(F32)
-            mixed = (mixed + bias_down + middle)[:half_rows]
-            sent = [mixed] + chunks_out.step(mixed)
+            mixed, mixed_low = mix(
+                after(mixed_a, done), mixed_b, got_sums_a, got_sums_b, middle, bias_down
+            )
+            sent = [mixed_low] + chunks_out.step(mixed_low)
         elif index == 1:
             for _ in range(count - 4):
                 chunks_a.step(done)
@@ -1090,39 +1137,27 @@
             sent = sent + chunks_b.step(done) + chunks_out.step(done)
             for _ in range(count - 4):
                 sent = chunks_b.step() + chunks_out.step()
-            mixed = after(mixed, *sent)
-            sent = sent + [mixed]
-            swapped_mixed = swap_clips(mixed)
+            mixed_low = after(mixed_low, *sent)
+            sent = sent + [mixed_low]
+            swapped_mixed, _ = swap_clips(mixed[:half_rows], mixed_low)
         else:
             own_a = chunks_a.result(done)
             sent = chunks_b.step(done) + own_a + chunks_out.step(done)
     flat = [[piece[which].reshape(each * HEAD_DIM, rows) for piece in grads] for which in range(3)]
     flat[0][0] = after(flat[0][0], *sent)
     partial_one, send_one = project_back([piece for group in flat for piece in group], w_qkv)
-    mixed = after(swapped_mixed, partial_one)
+    mixed = swapped_mixed(partial_one)
     own_b = chunks_b.result(partial_one)
     (own_out,) = chunks_out.result(partial_one)
-    got_one = across_cores(after(send_one, mixed, *own_b, own_out))
+    got_one = across_cores(after(send_one, *own_b, own_out))
     early = [over_groups(value) for value in own_a + own_b + [own_out]]
     cut_rows = block // 2
     wide_out = jnp.concatenate([early[4][:, :cut_rows], early[4][:, cut_rows:]], 2)
     early_other = across_cores(jnp.concatenate(early[:4] + [wide_out], 1))
-    grad_frames, sums_one = norm_back(
-        (partial_one, got_one), (both_own, 0), gain_one, grad_middle, False
-    )
-    early_send = grad_frames[:half_rows]
-    swapped = swap_clips(early_send)
-    names = ("zxy", "xyz", "yzx")
-    parts = project_grads(
-        after(normed_one, early_send), flat, [scatter_plan(back[name]) for name in names]
-    )
-    early_other = after(early_other, parts[0][0])
-    splits = [early_other[:, i * block : (i + 1) * block] for i in range(4)]
-    wide_out = early_other[:, 4 * block :]
-    early_other = splits + [jnp.concatenate([wide_out[:, :, :half], wide_out[:, :, half:]], 1)]
-    chunks_late = Halving(parts, [back[name] for name in names])
-    sent = chunks_late.step(early_other[0])
-
+    grad_frames, early_send, sums_one = norm_back(
+        (partial_one, got_one), frames_own, gain_one, grad_middle, False
+    )
+    swapped, swapped_got = swap_clips(grad_frames[:half_rows], early_send)
     def in_half(values):
         return lax.dynamic_update_slice_in_dim(jnp.zeros((width,), F32), values, core * half, 0)
 
@@ -1146,6 +1181,21 @@
             sums_up_all.reshape(-1),
         ]
     ).reshape(shards, small_size)
+    small_sum = SmallSum(grad_small)
+    small_sum.start()
+    names = ("zxy", "xyz", "yzx")
+    parts = project_grads(
+        after(normed_one, early_send, small_sum.kept), flat, [scatter_plan(back[name]) for name in names]
+    )
+    early_other = after(early_other, parts[0][0])
+    small_sum.finish(parts[0][0])
+    splits = [early_other[:, i * block : (i + 1) * block] for i in range(4)]
+    wide_out = early_other[:, 4 * block :]
+    early_other = splits + [jnp.concatenate([wide_out[:, :, :half], wide_out[:, :, half:]], 1)]
+    chunks_late = Halving(parts, [back[name] for name in names])
+    sent = chunks_late.step(early_other[0], small_sum.held)
+    small_sum.start()
+
     new_up, new_down = adam_feed(
         [after(early[0], *sent)] + early[1:4],
         early_other[:4],
@@ -1153,12 +1203,18 @@
         (master_down, first_down, second_down),
         shards,
     )
-    grad_frames = after(swapped, new_up[0])
-    sent = chunks_late.step(new_up[0], grad_frames)
-    total_small = reduce_small(after(grad_small, *sent))
+    small_sum.finish(new_up[0])
+    sent = chunks_late.step(new_up[0], small_sum.held, after(swapped_got, new_up[0]))
+    small_sum.start()
+    grad_frames = swapped(*sent)
     total_out = by_core(core, early[4][0], after(early_other[4], *sent)[0], 1)
     while len(chunks_late.got[0]) < count:
-        sent = chunks_late.step()
+        sent = chunks_late.step(*([small_sum.finish()] if small_sum.mask >= 1 else []))
+        if small_sum.mask >= 1:
+            small_sum.start()
+    if small_sum.held.shape[0] > 1:
+        small_sum.finish()
+    total_small = small_sum.result()
     late = over_groups(jnp.concatenate(chunks_late.result(), 0))
     late_other = across_cores(late)
     total_qkv = by_core(core, late, late_other, 2)

time: 708 us -> 621 us (0.88)
  waiting for transfers between devices: 178 us -> 125 us
  local copies, waits for them, and re-layouts: 89.6 us -> 60.2 us
    unnamed x334 -> x305, local copies, waits for them, and re-layouts: 58.6 us -> 33.1 us
    ppermute x21, waiting for transfers between devices: 87.1 us -> 61.6 us  [start(): lax.ppermute(held, 'shard', xor_pairs(shards, mask))]
    ppermute x25, waiting for transfers between devices: 24.5 us -> 12.4 us  [step(): lax.ppermute(send, 'shard', xor_pairs(shards, mask))]
    pallas_call x1, Pallas kernels: 27.5 us -> 16.3 us  [project(): call(body, (array((2 * padded, width), BF16), array((columns, 2 * padded)...]
    add x5, other arithmetic: 7.6 us -> 0.04 us  [the longest x4 0.04 us: finish(): self.held = self.kept + (after(self.got, *behind) if behind else self.got)]
    pallas_call x2 -> x3, Pallas kernels: 105 us -> 113 us  [the longest x2 105 us: feed(): call(body, shapes, limit=60, grid=(2 + tiles,), in_specs=[whole] * 4 + [A...]
    ppermute x11 -> x12, waiting for transfers between devices: 13.7 us -> 15.6 us  [across_cores(): return lax.ppermute(value, 'rep', xor_pairs(lax.axis_size('rep'), 1))]
  transfers between devices with their start and end apart: 70 -> 72, of which waited for: 27 -> 25; matrix products, arithmetic and copies ran while one was open for 9% -> 10% of each run, Pallas kernels for 35% -> 49%
where the time goes in v2:
time: 621 us; the launch traced here: 614 us
  Pallas kernels  319 us (51%)
  waiting for transfers between devices  125 us (20%)
  starting transfers between devices  75.3 us (12%)
  local copies, waits for them, and re-layouts  60.2 us (10%)
  other arithmetic  31.3 us (5%)
    pallas_call x2, Pallas kernels, feed(): call(body, shapes, limit=60, grid=(2 + tiles,), in_specs=[whole] * 4 + [A...  105 us
    ppermute x21, waiting for transfers between devices, start(): lax.ppermute(held, 'shard', xor_pairs(shards, mask))  61.6 us
    pallas_call x4, Pallas kernels, attend_back(): pl.pallas_call(functools.partial(attend_back_kernel, step=step), grid=(he...  52.7 us
    pallas_call x2, Pallas kernels, attend(): pl.pallas_call(functools.partial(attend_kernel, step=step), grid=(heads,)...  34.9 us
    unnamed x305, local copies, waits for them, and re-layouts  33.1 us
    ppermute x25, starting transfers between devices, step(): lax.ppermute(send, 'shard', xor_pairs(shards, mask))  26.7 us
    pallas_call x16, Pallas kernels, add_blocks(): call(body, [array(first.shape, dtype) for first in firsts], grid=(1,), in...  23 us
    ppermute x2, waiting for transfers between devices, start(): together = lax.ppermute(together, 'shard', xor_pairs(shards, masks[0]))  21.9 us
  transfers between devices with their start and end apart: 72, of which 25 were waited for; matrix products, arithmetic and copies ran while one was open for 10% of the time, Pallas kernels for 49%

profile of v2, /device:TPU:0, one launch (start us, length us, event | category | flops | bytes accessed | tf_op | source)
XLA Modules:
  0.0 614.1 jit_solution(16421426720562781491)
XLA Ops:
  3.1 4.1 collective-permute-start.1
  12.7 13.6 %collective-permute-done.1 = bf16[1,336,640]{2,1,0:T(8,128)(2,1)S(1)} collective-permute-done((bf16[1,336,640]{2,1,0:T(8,128)(2,1)S(1)}, bf16[1,336,640]{2,1,0:T(8,128)(2,1)S(1)}, u32[]{:S(2)}, u32[]{:S(2)}) %collective-permute-start.1) | collective-permute-done | bytes 430112 | tf_op jit(solution)/shard_map/ppermute | solution.py:123
  52.8 13.3 %collective-permute-done.3 = bf16[4,112,640]{2,1,0:T(8,128)(2,1)} collective-permute-done((bf16[4,112,640]{2,1,0:T(8,128)(2,1)}, bf16[4,112,640]{2,1,0:T(8,128)(2,1)}, u32[]{:S(2)}, u32[]{:S(2)}) %collective-permute-start.3) | collective-permute-done | bytes 573472 | tf_op jit(solution)/shard_map/ppermute | solution.py:128
  72.1 8.3 %collective-permute-done.8 = bf16[1,320,1280]{2,1,0:T(8,128)(2,1)S(1)} collective-permute-done((bf16[1,320,1280]{2,1,0:T(8,128)(2,1)S(1)}, bf16[1,320,1280]{2,1,0:T(8,128)(2,1)S(1)}, u32[]{:S(2)}, u32[]{:S(2)}) %collective-permute-start.8) | collective-permute-done | bytes 819232 | tf_op jit(solution)/shard_map/ppermute | solution.py:123
  83.0 13.2 %collective-permute-done.11.refs_5_ = bf16[8,112,640]{2,1,0:T(8,128)(2,1)S(1)} collective-permute-done((bf16[8,112,640]{2,1,0:T(8,128)(2,1)S(1)}, bf16[8,112,640]{2,1,0:T(8,128)(2,1)S(1)}, u32[]{:S(2)}, u32[]{:S(2)}) %collective-permute-start.11) | collective-permute-done | bytes 1146912 | tf_op jit(solution)/shard_map/ppermute | solution.py:128
  96.2 5.3 collective-permute-done.10.refs_3_
  101.5 4.6 place_first.1
  112.0 11.6 %collective-permute-done.13 = bf16[2,80,1280]{2,1,0:T(8,128)(2,1)S(1)} collective-permute-done((bf16[2,80,1280]{2,1,0:T(8,128)(2,1)S(1)}, bf16[2,80,1280]{2,1,0:T(8,128)(2,1)S(1)}, u32[]{:S(2)}, u32[]{:S(2)}) %collective-permute-start.13) | collective-permute-done | bytes 409632 | tf_op jit(solution)/shard_map/ppermute | solution.py:128
  127.5 16.3 %project.1 = (bf16[1536,1280]{1,0:T(8,128)(2,1)}, bf16[1920,1536]{1,0:T(8,128)(2,1)}) custom-call(bf16[768,1280]{1,0:T(8,128)(2,1)S(1)} %pad.12.own_ref.frames_ref.refs_2_, bf16[768,1280]{1,0:T(8,128)(2,1)S(1)} %collective-permute-done.14.other_ref, f32[1,1280]{1,0:T(1,128)S(1)} %broadcast_in_dim.97.gain_ref.refs_4_, ...), custom_call_target="tpu_custom_call" | custom-call | bytes 1048576 | tf_op jit(solution)/shard_map/project/pallas_call | solution.py:328
  143.8 9.7 %collective-permute-done.18 = bf16[2,80,1280]{2,1,0:T(8,128)(2,1)S(1)} collective-permute-done((bf16[2,80,1280]{2,1,0:T(8,128)(2,1)S(1)}, bf16[2,80,1280]{2,1,0:T(8,128)(2,1)S(1)}, u32[]{:S(2)}, u32[]{:S(2)}) %collective-permute-start.18) | collective-permute-done | bytes 409632 | tf_op jit(solution)/shard_map/ppermute | solution.py:128
  163.9 17.3 %attend.2 = (bf16[4,80,1536]{2,1,0:T(8,128)(2,1)S(1)}, f32[4,1,1536]{2,1,0:T(1,128)S(1)}) custom-call(bf16[32,1536]{1,0:T(8,128)(2,1)S(1)} %pad_maximum_fusion.19.mask_ref, bf16[3,8,80,1536]{3,2,1,0:T(8,128)(2,1)} %bitcast.104, bf16[3,8,80,1536]{3,2,1,0:T(8,128)(2,1)} %bitcast.105, bf16[3,8,80,1536]{3,2,1,0:T(8,128)(2,1)} %bitcast.106), custom_call_target="tpu_custom_call" | custom-call | bytes 1048576 | tf_op jit(solution)/shard_map/attend/pallas_call | solution.py:375
  181.8 17.6 %attend.3 = (bf16[4,80,1536]{2,1,0:T(8,128)(2,1)S(1)}, f32[4,1,1536]{2,1,0:T(1,128)S(1)}) custom-call(bf16[32,1536]{1,0:T(8,128)(2,1)S(1)} %pad_maximum_fusion.19.mask_ref, bf16[3,8,80,1536]{3,2,1,0:T(8,128)(2,1)} %bitcast.107, bf16[3,8,80,1536]{3,2,1,0:T(8,128)(2,1)} %bitcast.108, bf16[3,8,80,1536]{3,2,1,0:T(8,128)(2,1)} %bitcast.109), custom_call_target="tpu_custom_call" | custom-call | bytes 1048576 | tf_op jit(solution)/shard_map/attend/pallas_call | solution.py:375
  208.6 8.9 %attended.1 = (f32[768,1280]{1,0:T(8,128)}, bf16[768,1280]{1,0:T(8,128)(2,1)}) custom-call(bf16[320,1536]{1,0:T(8,128)(2,1)S(1)} %bitcast.74, bf16[320,1536]{1,0:T(8,128)(2,1)S(1)} %bitcast.71, bf16[320,1536]{1,0:T(8,128)(2,1)S(1)} %collective-permute-done.26.ga.refs_6_, bf16[320,1536]{1,0:T(8,128)(2,1)S(1)} %collective-permute-done.27.gb.refs_7_, ...), custom_call_target="tpu_custom_call" | custom-call | bytes 1048576 | tf_op jit(solution)/shard_map/attended/pallas_call | solution.py:494
  223.1 46.0 %feed.2 = (f32[768,1280]{1,0:T(8,128)}, f32[768,1280]{1,0:T(8,128)}, bf16[2,768,1280]{2,1,0:T(8,128)(2,1)}, f32[1,1280]{1,0:T(1,128)}, bf16[8,80,1280]{2,1,0:T(8...) custom-call(bf16[768,1280]{1,0:T(8,128)(2,1)} %get-tuple-element.294, ...), custom_call_target="tpu_custom_call" | custom-call | bytes 1048576 | tf_op jit(solution)/shard_map/feed/pallas_call | solution.py:617
  272.6 59.0 %feed.3 = (f32[768,1280]{1,0:T(8,128)}, f32[768,1280]{1,0:T(8,128)}, bf16[2,768,1280]{2,1,0:T(8,128)(2,1)}, f32[1,1280]{1,0:T(1,128)}, bf16[8,80,1280]{2,1,0:T(8...) custom-call(bf16[768,1280]{1,0:T(8,128)(2,1)} %get-tuple-element.294, ...), custom_call_target="tpu_custom_call" | custom-call | bytes 1048576 | tf_op jit(solution)/shard_map/feed/pallas_call | solution.py:617
  331.7 7.0 %collective-permute-done.34.refs_3_.gb_ref = bf16[2,768,1280]{2,1,0:T(8,128)(2,1)S(1)} collective-permute-done((bf16[2,768,1280]{2,1,0:T(8,128)(2,1)}, bf16[2,768,1280]{2,1,0:T(8,128)(2,1)S(1)}, u32[]{:S(2)}, u32[]{:S(2)}) %collective-permute-start.34) | collective-permute-done | bytes 3932192 | tf_op jit(solution)/shard_map/ppermute | solution.py:58
  340.6 10.0 %norm_back.2 = (f32[768,1280]{1,0:T(8,128)}, bf16[768,1280]{1,0:T(8,128)(2,1)S(1)}, f32[8,1280]{1,0:T(8,128)S(1)}) custom-call(f32[768,1280]{1,0:T(8,128)} %get-tuple-element.285.refs_0_, f32[768,1280]{1,0:T(8,128)} %get-tuple-element.295.refs_1_, bf16[2,768,1280]{2,1,0:T(8,128)(2,1)} %collective-permute-done.31.refs_2_.ga_ref, ...), custom_call_target="tpu_custom_call" | custom-call | bytes 1048576 | tf_op jit(solution)/shard_map/norm_back/pallas_call | solution.py:678
  350.8 3.8 collective-permute-done.35.refs_1_
  360.6 10.7 %attended_back.1 = (bf16[640,1536]{1,0:T(8,128)(2,1)}, bf16[8,80,640]{2,1,0:T(8,128)(2,1)}, bf16[4,80,640]{2,1,0:T(8,128)(2,1)S(1)}, bf16[2,80,640]{2,1,0:T(8,12...) custom-call(bf16[768,1280]{1,0:T(8,128)(2,1)} %copy-done.49, ...), custom_call_target="tpu_custom_call" | custom-call | bytes 1048576 | tf_op jit(solution)/shard_map/attended_back/pallas_call | solution.py:748
  373.0 13.1 %attend_back.4 = (bf16[2,80,1536]{2,1,0:T(8,128)(2,1)S(1)}, bf16[2,80,1536]{2,1,0:T(8,128)(2,1)S(1)}, bf16[2,80,1536]{2,1,0:T(8,128)(2,1)S(1)}) custom-call(bf16[32,1536]{1,0:T(8,128)(2,1)S(1)} %pad_maximum_fusion.19.mask_ref, bf16[3,8,80,1536]{3,2,1,0:T(8,128)(2,1)} %bitcast.110, bf16[3,8,80,1536]{3,2,1,0:T(8,128)(2,1)} %bitcast.111, ...), custom_call_target="tpu_custom_call" | custom-call | bytes 1048576 | tf_op jit(solution)/shard_map/attend_back/pallas_call | solution.py:445
  388.5 7.5 %mix.1 = (f32[768,1280]{1,0:T(8,128)S(1)}, bf16[768,1280]{1,0:T(8,128)(2,1)}) custom-call(f32[768,1280]{1,0:T(8,128)} %get-tuple-element.317.a_ref, f32[768,1280]{1,0:T(8,128)} %get-tuple-element.318.b_ref, bf16[2,768,1280]{2,1,0:T(8,128)(2,1)} %collective-permute-done.31.refs_2_.ga_ref, bf16[2,768,1280]{2,1,0:T(8,128)(2,1)} %copy-done.101, ...), custom_call_target="tpu_custom_call" | custom-call | bytes 1048576 | tf_op jit(solution)/shard_map/mix/pallas_call | solution.py:706
  399.9 13.1 %attend_back.5 = (bf16[2,80,1536]{2,1,0:T(8,128)(2,1)S(1)}, bf16[2,80,1536]{2,1,0:T(8,128)(2,1)S(1)}, bf16[2,80,1536]{2,1,0:T(8,128)(2,1)S(1)}) custom-call(bf16[32,1536]{1,0:T(8,128)(2,1)S(1)} %pad_maximum_fusion.19.mask_ref, bf16[3,8,80,1536]{3,2,1,0:T(8,128)(2,1)} %bitcast.113, bf16[3,8,80,1536]{3,2,1,0:T(8,128)(2,1)} %bitcast.114, ...), custom_call_target="tpu_custom_call" | custom-call | bytes 1048576 | tf_op jit(solution)/shard_map/attend_back/pallas_call | solution.py:445
  433.0 13.1 %attend_back.6 = (bf16[2,80,1536]{2,1,0:T(8,128)(2,1)S(1)}, bf16[2,80,1536]{2,1,0:T(8,128)(2,1)S(1)}, bf16[2,80,1536]{2,1,0:T(8,128)(2,1)S(1)}) custom-call(bf16[32,1536]{1,0:T(8,128)(2,1)S(1)} %pad_maximum_fusion.19.mask_ref, bf16[3,8,80,1536]{3,2,1,0:T(8,128)(2,1)} %bitcast.116, bf16[3,8,80,1536]{3,2,1,0:T(8,128)(2,1)} %bitcast.117, ...), custom_call_target="tpu_custom_call" | custom-call | bytes 1048576 | tf_op jit(solution)/shard_map/attend_back/pallas_call | solution.py:445
  463.0 13.4 %attend_back.7 = (bf16[2,80,1536]{2,1,0:T(8,128)(2,1)S(1)}, bf16[2,80,1536]{2,1,0:T(8,128)(2,1)S(1)}, bf16[2,80,1536]{2,1,0:T(8,128)(2,1)S(1)}) custom-call(bf16[32,1536]{1,0:T(8,128)(2,1)S(1)} %pad_maximum_fusion.19.mask_ref, bf16[3,8,80,1536]{3,2,1,0:T(8,128)(2,1)} %bitcast.119, bf16[3,8,80,1536]{3,2,1,0:T(8,128)(2,1)} %bitcast.120, ...), custom_call_target="tpu_custom_call" | custom-call | bytes 1048576 | tf_op jit(solution)/shard_map/attend_back/pallas_call | solution.py:445
  488.2 14.2 %project_back.1 = (f32[768,1280]{1,0:T(8,128)}, bf16[768,1280]{1,0:T(8,128)(2,1)}) custom-call(bf16[160,1536]{1,0:T(8,128)(2,1)S(1)} %bitcast.76, bf16[160,1536]{1,0:T(8,128)(2,1)S(1)} %bitcast.81, bf16[160,1536]{1,0:T(8,128)(2,1)S(1)} %bitcast.85, bf16[160,1536]{1,0:T(8,128)(2,1)S(1)} %bitcast.89, bf16[160,1536]{1,0:T(8,128)(2,1)S(1)} %bitcast.93, ...), custom_call_target="tpu_custom_call" | custom-call | bytes 1048576 | tf_op jit(solution)/shard_map/project_back/pallas_call | solution.py:781
  513.7 8.1 %norm_back.3 = (f32[768,1280]{1,0:T(8,128)}, bf16[768,1280]{1,0:T(8,128)(2,1)S(1)}, f32[8,1280]{1,0:T(8,128)S(1)}) custom-call(f32[768,1280]{1,0:T(8,128)} %get-tuple-element.381.refs_0_, bf16[768,1280]{1,0:T(8,128)(2,1)} %collective-permute-done.53.refs_1_, bf16[768,1280]{1,0:T(8,128)(2,1)S(1)} %copy-done.1, f32[768,1280]{1,0:T(8,128)} %get-tuple-element.394.refs_3_, ...), custom_call_target="tpu_custom_call" | custom-call | bytes 1048576 | tf_op jit(solution)/shard_map/norm_back/pallas_call | solution.py:678
  530.5 13.4 %project_grads.1 = (bf16[8,80,640]{2,1,0:T(8,128)(2,1)}, bf16[4,80,640]{2,1,0:T(8,128)(2,1)S(1)}, bf16[2,80,640]{2,1,0:T(8,128)(2,1)S(1)}, bf16[1,80,640]{2,1,0:...) custom-call(bf16[1536,1280]{1,0:T(8,128)(2,1)} %get-tuple-element.40, ...), custom_call_target="tpu_custom_call" | custom-call | bytes 1048576 | tf_op jit(solution)/shard_map/project_grads/pallas_call | solution.py:815
  550.7 9.7 %adam_feed.1 = (f32[80,5120]{1,0:T(8,128)}, bf16[80,5120]{1,0:T(8,128)(2,1)}, f32[80,5120]{1,0:T(8,128)}, f32[80,5120]{1,0:T(8,128)}, f32[4,80,1280]{2,1,0:T(8,1...) custom-call(f32[1,80,1280]{2,1,0:T(8,128)S(1)} %copy-done.63, ...), custom_call_target="tpu_custom_call" | custom-call | bytes 1048576 | tf_op jit(solution)/shard_map/adam_feed/pallas_call | solution.py:883
  561.2 4.0 slice_select_fusion.1
  573.9 5.4 collective-permute-done.61.refs_2_
  591.9 10.6 %collective-permute-done.68 = bf16[1,240,640]{2,1,0:T(8,128)(2,1)S(1)} collective-permute-done((bf16[1,240,640]{2,1,0:T(8,128)(2,1)S(1)}, bf16[1,240,640]{2,1,0:T(8,128)(2,1)S(1)}, u32[]{:S(2)}, u32[]{:S(2)}) %collective-permute-start.68) | collective-permute-done | bytes 307232 | tf_op jit(solution)/shard_map/ppermute | solution.py:175
  604.6 4.1 slice_select_fusion
  (587 shorter events, 201.1 us)
Async XLA Ops:
  7.2 60.0 %collective-permute-start = (bf16[750,1280]{1,0:T(8,128)(2,1)}, bf16[750,1280]{1,0:T(8,128)(2,1)}, u32[]{:S(2)}, u32[]{:S(2)}) collective-permute-start(bf16[750,1280]{1,0:T(8,128)(2,1)} %param.18), channel_id=1, source_target_pairs={{1,16},{3,18},{5,20},{7,22},{9,24},{11,26},{13,28},{15,30},{16,1},... | collective-permute-start | bytes 5760008 | tf_op jit(solution)/shard_map/ppermute | solution.py:72
  42.4 37.9 %collective-permute-start.8 = (bf16[1,320,1280]{2,1,0:T(8,128)(2,1)S(1)}, bf16[1,320,1280]{2,1,0:T(8,128)(2,1)S(1)}, u32[]{:S(2)}, u32[]{:S(2)}) collective-permute-start(bf16[1,320,1280]{2,1,0:T(8,128)(2,1)S(1)} %pad_maximum_fusion.3), channel_id=1, source_target_pairs={{0,8},{1,9},{2,10},{3,11},{4,12},{5,13},{6,14},{7,15},{8,0},{9,1},... | collective-permute-start | bytes 2457608 | tf_op jit(solution)/shard_map/ppermute | solution.py:123
  67.6 28.6 %collective-permute-start.11 = (bf16[8,112,640]{2,1,0:T(8,128)(2,1)S(1)}, bf16[8,112,640]{2,1,0:T(8,128)(2,1)S(1)}, u32[]{:S(2)}, u32[]{:S(2)}) collective-permute-start(bf16[8,112,640]{2,1,0:T(8,128)(2,1)S(1)} %pad_maximum_fusion.2.refs_4_), channel_id=1, source_target_pairs={{0,1},{1,0},{2,3},{3,2},{4,5},{5,4},{6,7},{7,6},{8,9},{9,8},{10,11... | collective-permute-start | bytes 3440648 | tf_op jit(solution)/shard_map/ppermute | solution.py:128
  70.5 31.0 %collective-permute-start.10 = (bf16[8,112,640]{2,1,0:T(8,128)(2,1)S(1)}, bf16[8,112,640]{2,1,0:T(8,128)(2,1)S(1)}, u32[]{:S(2)}, u32[]{:S(2)}) collective-permute-start(bf16[8,112,640]{2,1,0:T(8,128)(2,1)S(1)} %pad_maximum_fusion.1.refs_2_), channel_id=1, source_target_pairs={{0,4},{1,5},{2,6},{3,7},{4,0},{5,1},{6,2},{7,3},{8,12},{9,13},{10,... | collective-permute-start | bytes 3440648 | tf_op jit(solution)/shard_map/ppermute | solution.py:128
  70.5 31.0 %collective-permute-start.9 = (bf16[8,112,640]{2,1,0:T(8,128)(2,1)S(1)}, bf16[8,112,640]{2,1,0:T(8,128)(2,1)S(1)}, u32[]{:S(2)}, u32[]{:S(2)}) collective-permute-start(bf16[8,112,640]{2,1,0:T(8,128)(2,1)S(1)} %pad_maximum_fusion.refs_0_), channel_id=1, source_target_pairs={{0,2},{1,3},{2,0},{3,1},{4,6},{5,7},{6,4},{7,5},{8,10},{9,11},{10,... | collective-permute-start | bytes 3440648 | tf_op jit(solution)/shard_map/ppermute | solution.py:128
  81.1 75.2 %collective-permute-start.20 = (bf16[750,1280]{1,0:T(8,128)(2,1)}, bf16[750,1280]{1,0:T(8,128)(2,1)}, u32[]{:S(2)}, u32[]{:S(2)}) collective-permute-start(bf16[750,1280]{1,0:T(8,128)(2,1)} %param.19), channel_id=1, source_target_pairs={{1,16},{3,18},{5,20},{7,22},{9,24},{11,26},{13,28},{15,30},{16,1},... | collective-permute-start | bytes 5760008 | tf_op jit(solution)/shard_map/ppermute | solution.py:72
  124.4 29.1 %collective-permute-start.16 = (bf16[4,80,1280]{2,1,0:T(8,128)(2,1)S(1)}, bf16[4,80,1280]{2,1,0:T(8,128)(2,1)S(1)}, u32[]{:S(2)}, u32[]{:S(2)}) collective-permute-start(bf16[4,80,1280]{2,1,0:T(8,128)(2,1)S(1)} %get-tuple-element.492), channel_id=1, source_target_pairs={{0,4},{1,5},{2,6},{3,7},{4,0},{5,1},{6,2},{7,3},{8,12},{9,13},{10,... | collective-permute-start | bytes 2457608 | tf_op jit(solution)/shard_map/ppermute | solution.py:128
  125.2 28.3 %collective-permute-start.15 = (bf16[4,80,1280]{2,1,0:T(8,128)(2,1)S(1)}, bf16[4,80,1280]{2,1,0:T(8,128)(2,1)S(1)}, u32[]{:S(2)}, u32[]{:S(2)}) collective-permute-start(bf16[4,80,1280]{2,1,0:T(8,128)(2,1)S(1)} %get-tuple-element.494), channel_id=1, source_target_pairs={{0,2},{1,3},{2,0},{3,1},{4,6},{5,7},{6,4},{7,5},{8,10},{9,11},{10,... | collective-permute-start | bytes 2457608 | tf_op jit(solution)/shard_map/ppermute | solution.py:128
  125.8 27.8 %collective-permute-start.18 = (bf16[2,80,1280]{2,1,0:T(8,128)(2,1)S(1)}, bf16[2,80,1280]{2,1,0:T(8,128)(2,1)S(1)}, u32[]{:S(2)}, u32[]{:S(2)}) collective-permute-start(bf16[2,80,1280]{2,1,0:T(8,128)(2,1)S(1)} %pad_maximum_fusion.11), channel_id=1, source_target_pairs={{0,2},{1,3},{2,0},{3,1},{4,6},{5,7},{6,4},{7,5},{8,10},{9,11},{10,... | collective-permute-start | bytes 1228808 | tf_op jit(solution)/shard_map/ppermute | solution.py:128
  127.4 26.1 %collective-permute-start.17 = (bf16[2,80,1280]{2,1,0:T(8,128)(2,1)S(1)}, bf16[2,80,1280]{2,1,0:T(8,128)(2,1)S(1)}, u32[]{:S(2)}, u32[]{:S(2)}) collective-permute-start(bf16[2,80,1280]{2,1,0:T(8,128)(2,1)S(1)} %pad_maximum_fusion.10), channel_id=1, source_target_pairs={{0,1},{1,0},{2,3},{3,2},{4,5},{5,4},{6,7},{7,6},{8,9},{9,8},{10,11... | collective-permute-start | bytes 1228808 | tf_op jit(solution)/shard_map/ppermute | solution.py:128
  158.1 43.3 %collective-permute-start.24 = (bf16[768,1280]{1,0:T(8,128)(2,1)S(1)}, bf16[768,1280]{1,0:T(8,128)(2,1)S(1)}, u32[]{:S(2)}, u32[]{:S(2)}) collective-permute-start(bf16[768,1280]{1,0:T(8,128)(2,1)S(1)} %pad.13.refs_2_.refs_5_), channel_id=1, source_target_pairs={{0,16},{16,0},{1,17},{17,1},{2,18},{18,2},{3,19},{19,3},{4,20},{20... | collective-permute-start | bytes 5898248 | tf_op jit(solution)/shard_map/ppermute | solution.py:58
  159.5 43.9 %collective-permute-start.22 = (bf16[8,80,1280]{2,1,0:T(8,128)(2,1)}, bf16[8,80,1280]{2,1,0:T(8,128)(2,1)S(1)}, u32[]{:S(2)}, u32[]{:S(2)}) collective-permute-start(bf16[8,80,1280]{2,1,0:T(8,128)(2,1)} %constant_dynamic-update-slice_fusion.10.refs_6_), channel_id=1, source_target_pairs={{0,2},{1,3},{2,0},{3,1},{4,6},{5,7},{6,4},{7,5},{8,10},{9,11},{10,... | collective-permute-start | bytes 4915208 | tf_op jit(solution)/shard_map/ppermute | solution.py:128
  159.8 43.6 %collective-permute-start.21 = (bf16[8,80,1280]{2,1,0:T(8,128)(2,1)}, bf16[8,80,1280]{2,1,0:T(8,128)(2,1)S(1)}, u32[]{:S(2)}, u32[]{:S(2)}) collective-permute-start(bf16[8,80,1280]{2,1,0:T(8,128)(2,1)} %constant_dynamic-update-slice_fusion.6.refs_4_), channel_id=1, source_target_pairs={{0,1},{1,0},{2,3},{3,2},{4,5},{5,4},{6,7},{7,6},{8,9},{9,8},{10,11... | collective-permute-start | bytes 4915208 | tf_op jit(solution)/shard_map/ppermute | solution.py:128
  161.5 40.0 %collective-permute-start.25 = (bf16[4,80,1280]{2,1,0:T(8,128)(2,1)S(1)}, bf16[4,80,1280]{2,1,0:T(8,128)(2,1)S(1)}, u32[]{:S(2)}, u32[]{:S(2)}) collective-permute-start(bf16[4,80,1280]{2,1,0:T(8,128)(2,1)S(1)} %copy-done.111), channel_id=1, source_target_pairs={{0,4},{1,5},{2,6},{3,7},{4,0},{5,1},{6,2},{7,3},{8,12},{9,13},{10,... | collective-permute-start | bytes 2457608 | tf_op jit(solution)/shard_map/ppermute | solution.py:128
  163.8 37.7 %collective-permute-start.23 = (bf16[4,80,1280]{2,1,0:T(8,128)(2,1)S(1)}, bf16[4,80,1280]{2,1,0:T(8,128)(2,1)S(1)}, u32[]{:S(2)}, u32[]{:S(2)}) collective-permute-start(bf16[4,80,1280]{2,1,0:T(8,128)(2,1)S(1)} %constant_dynamic-update-slice_fusion.14), channel_id=1, source_target_pairs={{0,4},{1,5},{2,6},{3,7},{4,0},{5,1},{6,2},{7,3},{8,12},{9,13},{10,... | collective-permute-start | bytes 2457608 | tf_op jit(solution)/shard_map/ppermute | solution.py:128
  217.7 51.4 %collective-permute-start.30 = (bf16[8,80,1280]{2,1,0:T(8,128)(2,1)}, bf16[8,80,1280]{2,1,0:T(8,128)(2,1)}, u32[]{:S(2)}, u32[]{:S(2)}) collective-permute-start(bf16[8,80,1280]{2,1,0:T(8,128)(2,1)} %constant_dynamic-update-slice_fusion.20.refs_6_), channel_id=1, source_target_pairs={{0,1},{1,0},{2,3},{3,2},{4,5},{5,4},{6,7},{7,6},{8,9},{9,8},{10,11... | collective-permute-start | bytes 4915208 | tf_op jit(solution)/shard_map/ppermute | solution.py:128
  218.0 51.2 %collective-permute-start.29 = (bf16[8,80,1280]{2,1,0:T(8,128)(2,1)}, bf16[8,80,1280]{2,1,0:T(8,128)(2,1)}, u32[]{:S(2)}, u32[]{:S(2)}) collective-permute-start(bf16[8,80,1280]{2,1,0:T(8,128)(2,1)} %constant_dynamic-update-slice_fusion.18.refs_4_), channel_id=1, source_target_pairs={{0,2},{1,3},{2,0},{3,1},{4,6},{5,7},{6,4},{7,5},{8,10},{9,11},{10,... | collective-permute-start | bytes 4915208 | tf_op jit(solution)/shard_map/ppermute | solution.py:128
  269.1 62.5 %collective-permute-start.31 = (bf16[2,768,1280]{2,1,0:T(8,128)(2,1)}, bf16[2,768,1280]{2,1,0:T(8,128)(2,1)}, u32[]{:S(2)}, u32[]{:S(2)}) collective-permute-start(bf16[2,768,1280]{2,1,0:T(8,128)(2,1)} %get-tuple-element.293), channel_id=1, source_target_pairs={{0,16},{16,0},{1,17},{17,1},{2,18},{18,2},{3,19},{19,3},{4,20},{20... | collective-permute-start | bytes 11796488 | tf_op jit(solution)/shard_map/ppermute | solution.py:58
  269.3 62.3 %collective-permute-start.33 = (bf16[8,80,1280]{2,1,0:T(8,128)(2,1)}, bf16[8,80,1280]{2,1,0:T(8,128)(2,1)}, u32[]{:S(2)}, u32[]{:S(2)}) collective-permute-start(bf16[8,80,1280]{2,1,0:T(8,128)(2,1)} %get-tuple-element.291), channel_id=1, source_target_pairs={{0,4},{1,5},{2,6},{3,7},{4,0},{5,1},{6,2},{7,3},{8,12},{9,13},{10,... | collective-permute-start | bytes 4915208 | tf_op jit(solution)/shard_map/ppermute | solution.py:180
  271.3 60.3 %collective-permute-start.32 = (bf16[8,80,1280]{2,1,0:T(8,128)(2,1)}, bf16[8,80,1280]{2,1,0:T(8,128)(2,1)S(1)}, u32[]{:S(2)}, u32[]{:S(2)}) collective-permute-start(bf16[8,80,1280]{2,1,0:T(8,128)(2,1)} %get-tuple-element.289), channel_id=1, source_target_pairs={{0,2},{1,3},{2,0},{3,1},{4,6},{5,7},{6,4},{7,5},{8,10},{9,11},{10,... | collective-permute-start | bytes 4915208 | tf_op jit(solution)/shard_map/ppermute | solution.py:180
  354.6 59.3 %collective-permute-start.39 = (bf16[8,80,1280]{2,1,0:T(8,128)(2,1)}, bf16[8,80,1280]{2,1,0:T(8,128)(2,1)}, u32[]{:S(2)}, u32[]{:S(2)}) collective-permute-start(bf16[8,80,1280]{2,1,0:T(8,128)(2,1)} %get-tuple-element.306), channel_id=1, source_target_pairs={{0,4},{1,5},{2,6},{3,7},{4,0},{5,1},{6,2},{7,3},{8,12},{9,13},{10,... | collective-permute-start | bytes 4915208 | tf_op jit(solution)/shard_map/ppermute | solution.py:180
  354.7 59.2 %collective-permute-start.38 = (bf16[8,80,1280]{2,1,0:T(8,128)(2,1)}, bf16[8,80,1280]{2,1,0:T(8,128)(2,1)S(1)}, u32[]{:S(2)}, u32[]{:S(2)}) collective-permute-start(bf16[8,80,1280]{2,1,0:T(8,128)(2,1)} %get-tuple-element.304), channel_id=1, source_target_pairs={{0,2},{1,3},{2,0},{3,1},{4,6},{5,7},{6,4},{7,5},{8,10},{9,11},{10,... | collective-permute-start | bytes 4915208 | tf_op jit(solution)/shard_map/ppermute | solution.py:180
  358.6 60.5 %collective-permute-start.36 = (bf16[4,80,1280]{2,1,0:T(8,128)(2,1)}, bf16[4,80,1280]{2,1,0:T(8,128)(2,1)S(1)}, u32[]{:S(2)}, u32[]{:S(2)}) collective-permute-start(bf16[4,80,1280]{2,1,0:T(8,128)(2,1)} %get-tuple-element.311), channel_id=1, source_target_pairs={{0,1},{1,0},{2,3},{3,2},{4,5},{5,4},{6,7},{7,6},{8,9},{9,8},{10,11... | collective-permute-start | bytes 2457608 | tf_op jit(solution)/shard_map/ppermute | solution.py:180
  359.4 59.7 %collective-permute-start.37 = (bf16[4,80,1280]{2,1,0:T(8,128)(2,1)S(1)}, bf16[4,80,1280]{2,1,0:T(8,128)(2,1)S(1)}, u32[]{:S(2)}, u32[]{:S(2)}) collective-permute-start(bf16[4,80,1280]{2,1,0:T(8,128)(2,1)S(1)} %get-tuple-element.312), channel_id=1, source_target_pairs={{0,1},{1,0},{2,3},{3,2},{4,5},{5,4},{6,7},{7,6},{8,9},{9,8},{10,11... | collective-permute-start | bytes 2457608 | tf_op jit(solution)/shard_map/ppermute | solution.py:180
  398.0 31.9 %collective-permute-start.40 = (bf16[8,80,640]{2,1,0:T(8,128)(2,1)}, bf16[8,80,640]{2,1,0:T(8,128)(2,1)}, u32[]{:S(2)}, u32[]{:S(2)}) collective-permute-start(bf16[8,80,640]{2,1,0:T(8,128)(2,1)} %get-tuple-element.323), channel_id=1, source_target_pairs={{0,4},{1,5},{2,6},{3,7},{4,0},{5,1},{6,2},{7,3},{8,12},{9,13},{10,... | collective-permute-start | bytes 2457608 | tf_op jit(solution)/shard_map/ppermute | solution.py:180
  417.4 32.0 %collective-permute-start.43 = (bf16[4,80,1280]{2,1,0:T(8,128)(2,1)}, bf16[4,80,1280]{2,1,0:T(8,128)(2,1)}, u32[]{:S(2)}, u32[]{:S(2)}) collective-permute-start(bf16[4,80,1280]{2,1,0:T(8,128)(2,1)} %get-tuple-element.335), channel_id=1, source_target_pairs={{0,1},{1,0},{2,3},{3,2},{4,5},{5,4},{6,7},{7,6},{8,9},{9,8},{10,11... | collective-permute-start | bytes 2457608 | tf_op jit(solution)/shard_map/ppermute | solution.py:180
  417.4 31.9 %collective-permute-start.44 = (bf16[4,80,1280]{2,1,0:T(8,128)(2,1)}, bf16[4,80,1280]{2,1,0:T(8,128)(2,1)}, u32[]{:S(2)}, u32[]{:S(2)}) collective-permute-start(bf16[4,80,1280]{2,1,0:T(8,128)(2,1)} %get-tuple-element.336), channel_id=1, source_target_pairs={{0,2},{1,3},{2,0},{3,1},{4,6},{5,7},{6,4},{7,5},{8,10},{9,11},{10,... | collective-permute-start | bytes 2457608 | tf_op jit(solution)/shard_map/ppermute | solution.py:180
  421.5 26.1 %collective-permute-start.41 = (bf16[2,80,1280]{2,1,0:T(8,128)(2,1)}, bf16[2,80,1280]{2,1,0:T(8,128)(2,1)}, u32[]{:S(2)}, u32[]{:S(2)}) collective-permute-start(bf16[2,80,1280]{2,1,0:T(8,128)(2,1)} %get-tuple-element.329), channel_id=1, source_target_pairs={{0,4},{1,5},{2,6},{3,7},{4,0},{5,1},{6,2},{7,3},{8,12},{9,13},{10,... | collective-permute-start | bytes 1228808 | tf_op jit(solution)/shard_map/ppermute | solution.py:180
  431.7 29.0 %collective-permute-start.45 = (bf16[4,80,640]{2,1,0:T(8,128)(2,1)}, bf16[4,80,640]{2,1,0:T(8,128)(2,1)S(1)}, u32[]{:S(2)}, u32[]{:S(2)}) collective-permute-start(bf16[4,80,640]{2,1,0:T(8,128)(2,1)} %add_blocks.19), channel_id=1, source_target_pairs={{0,2},{1,3},{2,0},{3,1},{4,6},{5,7},{6,4},{7,5},{8,10},{9,11},{10,... | collective-permute-start | bytes 1228808 | tf_op jit(solution)/shard_map/ppermute | solution.py:180
  481.3 42.8 %collective-permute-start.46 = (bf16[768,1280]{1,0:T(8,128)(2,1)}, bf16[768,1280]{1,0:T(8,128)(2,1)}, u32[]{:S(2)}, u32[]{:S(2)}) collective-permute-start(bf16[768,1280]{1,0:T(8,128)(2,1)} %get-tuple-element.355), channel_id=1, source_target_pairs={{1,16},{3,18},{5,20},{7,22},{9,24},{11,26},{13,28},{15,30},{16,1},... | collective-permute-start | bytes 5898248 | tf_op jit(solution)/shard_map/ppermute | solution.py:72
  509.9 34.0 %collective-permute-start.55 = (f32[1,360,1280]{2,1,0:T(8,128)}, f32[1,360,1280]{2,1,0:T(8,128)}, u32[]{:S(2)}, u32[]{:S(2)}) collective-permute-start(f32[1,360,1280]{2,1,0:T(8,128)} %maximum_dynamic-update-slice_fusion), channel_id=1, source_target_pairs={{0,16},{16,0},{1,17},{17,1},{2,18},{18,2},{3,19},{19,3},{4,20},{20... | collective-permute-start | bytes 5529608 | tf_op jit(solution)/shard_map/ppermute | solution.py:58
  524.2 44.2 %collective-permute-start.54 = (bf16[768,1280]{1,0:T(8,128)(2,1)}, bf16[768,1280]{1,0:T(8,128)(2,1)}, u32[]{:S(2)}, u32[]{:S(2)}) collective-permute-start(bf16[768,1280]{1,0:T(8,128)(2,1)} %copy-done.100), channel_id=1, source_target_pairs={{1,16},{3,18},{5,20},{7,22},{9,24},{11,26},{13,28},{15,30},{16,1},... | collective-permute-start | bytes 5898248 | tf_op jit(solution)/shard_map/ppermute | solution.py:72
  (181 other events, 1607.3 us)

commit v3 on v2

--- a/solution.py
+++ b/solution.py
@@ -1139,25 +1139,38 @@
                 sent = chunks_b.step() + chunks_out.step()
             mixed_low = after(mixed_low, *sent)
             sent = sent + [mixed_low]
-            swapped_mixed, _ = swap_clips(mixed[:half_rows], mixed_low)
+            swapped_mixed, mixed_got = swap_clips(mixed[:half_rows], mixed_low)
         else:
             own_a = chunks_a.result(done)
             sent = chunks_b.step(done) + own_a + chunks_out.step(done)
     flat = [[piece[which].reshape(each * HEAD_DIM, rows) for piece in grads] for which in range(3)]
     flat[0][0] = after(flat[0][0], *sent)
-    partial_one, send_one = project_back([piece for group in flat for piece in group], w_qkv)
-    mixed = swapped_mixed(partial_one)
-    own_b = chunks_b.result(partial_one)
-    (own_out,) = chunks_out.result(partial_one)
-    got_one = across_cores(after(send_one, *own_b, own_out))
+    names = ("zxy", "xyz", "yzx")
+    parts = project_grads(normed_one, flat, [scatter_plan(back[name]) for name in names])
+    own_b = chunks_b.result(parts[0][0])
+    (own_out,) = chunks_out.result(parts[0][0])
     early = [over_groups(value) for value in own_a + own_b + [own_out]]
     cut_rows = block // 2
     wide_out = jnp.concatenate([early[4][:, :cut_rows], early[4][:, cut_rows:]], 2)
     early_other = across_cores(jnp.concatenate(early[:4] + [wide_out], 1))
+    chunks_late = Halving(parts, [back[name] for name in names])
+    sent = chunks_late.step(*own_b, own_out, after(mixed_got, parts[0][0]))
+    flat[0][0] = after(flat[0][0], *sent)
+    partial_one, send_one = project_back([piece for group in flat for piece in group], w_qkv)
+    early_other = after(early_other, partial_one)
+    splits = [early_other[:, i * block : (i + 1) * block] for i in range(4)]
+    wide_out = early_other[:, 4 * block :]
+    early_other = splits + [jnp.concatenate([wide_out[:, :, :half], wide_out[:, :, half:]], 1)]
+    sent = chunks_late.step(partial_one)
+    got_one = across_cores(after(send_one, *sent))
     grad_frames, early_send, sums_one = norm_back(
-        (partial_one, got_one), frames_own, gain_one, grad_middle, False
-    )
-    swapped, swapped_got = swap_clips(grad_frames[:half_rows], early_send)
+        (after(partial_one, *sent), got_one), frames_own, gain_one, grad_middle, False
+    )
+    sent = chunks_late.step(early_send)
+    for _ in range(count - 4):
+        sent = chunks_late.step()
+    swapped, swapped_got = swap_clips(grad_frames[:half_rows], after(early_send, *sent))
+
     def in_half(values):
         return lax.dynamic_update_slice_in_dim(jnp.zeros((width,), F32), values, core * half, 0)
 
@@ -1183,40 +1196,26 @@
     ).reshape(shards, small_size)
     small_sum = SmallSum(grad_small)
     small_sum.start()
-    names = ("zxy", "xyz", "yzx")
-    parts = project_grads(
-        after(normed_one, early_send, small_sum.kept), flat, [scatter_plan(back[name]) for name in names]
-    )
-    early_other = after(early_other, parts[0][0])
-    small_sum.finish(parts[0][0])
-    splits = [early_other[:, i * block : (i + 1) * block] for i in range(4)]
-    wide_out = early_other[:, 4 * block :]
-    early_other = splits + [jnp.concatenate([wide_out[:, :, :half], wide_out[:, :, half:]], 1)]
-    chunks_late = Halving(parts, [back[name] for name in names])
-    sent = chunks_late.step(early_other[0], small_sum.held)
+    mixed = swapped_mixed(*sent, small_sum.kept)
+    small_sum.finish(mixed)
+    sent = chunks_late.step(small_sum.held)
     small_sum.start()
-
     new_up, new_down = adam_feed(
-        [after(early[0], *sent)] + early[1:4],
+        [after(early[0], *sent, small_sum.kept)] + early[1:4],
         early_other[:4],
         (master_up, first_up, second_up),
         (master_down, first_down, second_down),
         shards,
     )
-    small_sum.finish(new_up[0])
-    sent = chunks_late.step(new_up[0], small_sum.held, after(swapped_got, new_up[0]))
+    late = chunks_late.result(new_up[0])
+    small_sum.finish(*late)
     small_sum.start()
-    grad_frames = swapped(*sent)
-    total_out = by_core(core, early[4][0], after(early_other[4], *sent)[0], 1)
-    while len(chunks_late.got[0]) < count:
-        sent = chunks_late.step(*([small_sum.finish()] if small_sum.mask >= 1 else []))
-        if small_sum.mask >= 1:
-            small_sum.start()
-    if small_sum.held.shape[0] > 1:
-        small_sum.finish()
+    grad_frames = swapped(*late)
+    total_out = by_core(core, early[4][0], after(early_other[4], *late)[0], 1)
+    late = over_groups(jnp.concatenate(late, 0))
+    late_other = across_cores(late)
+    small_sum.finish(grad_frames)
     total_small = small_sum.result()
-    late = over_groups(jnp.concatenate(chunks_late.result(), 0))
-    late_other = across_cores(late)
     total_qkv = by_core(core, late, late_other, 2)
 
     new_qkv = adam_update(master_qkv, first_qkv, second_qkv, total_qkv, RATES[0], DECAYS[0])

time: 621 us -> 616 us (level)
  local copies, waits for them, and re-layouts: 60.2 us -> 70.1 us
    unnamed x305 -> x361, local copies, waits for them, and re-layouts: 33.1 us -> 45.9 us
  transfers between devices with their start and end apart: 72 -> 72, of which waited for: 25 -> 21; matrix products, arithmetic and copies ran while one was open for 10% -> 10% of each run, Pallas kernels for 49% -> 48%
where the time goes in v3:
time: 616 us; the launch traced here: 609 us
  Pallas kernels  314 us (51%)
  waiting for transfers between devices  119 us (19%)
  starting transfers between devices  72.8 us (12%)
  local copies, waits for them, and re-layouts  70.1 us (11%)
  other arithmetic  29.6 us (5%)
    pallas_call x2, Pallas kernels, feed(): call(body, shapes, limit=60, grid=(2 + tiles,), in_specs=[whole] * 4 + [A...  105 us
    ppermute x21, waiting for transfers between devices, start(): lax.ppermute(held, 'shard', xor_pairs(shards, mask))  61.6 us
    pallas_call x4, Pallas kernels, attend_back(): pl.pallas_call(functools.partial(attend_back_kernel, step=step), grid=(he...  52.6 us
    unnamed x361, local copies, waits for them, and re-layouts  45.9 us
    pallas_call x2, Pallas kernels, attend(): pl.pallas_call(functools.partial(attend_kernel, step=step), grid=(heads,)...  34.9 us
    ppermute x25, starting transfers between devices, step(): lax.ppermute(send, 'shard', xor_pairs(shards, mask))  26.1 us
    ppermute x2, waiting for transfers between devices, start(): together = lax.ppermute(together, 'shard', xor_pairs(shards, masks[0]))  21.9 us
    ppermute x21, starting transfers between devices, start(): lax.ppermute(held, 'shard', xor_pairs(shards, mask))  20.6 us
  transfers between devices with their start and end apart: 72, of which 21 were waited for; matrix products, arithmetic and copies ran while one was open for 10% of the time, Pallas kernels for 48%

profile of v3, /device:TPU:0, one launch (start us, length us, event | category | flops | bytes accessed | tf_op | source)
XLA Modules:
  0.0 608.8 jit_solution(1436988576120836073)
XLA Ops:
  3.1 4.1 collective-permute-start.1
  12.8 13.6 %collective-permute-done.1 = bf16[1,336,640]{2,1,0:T(8,128)(2,1)S(1)} collective-permute-done((bf16[1,336,640]{2,1,0:T(8,128)(2,1)S(1)}, bf16[1,336,640]{2,1,0:T(8,128)(2,1)S(1)}, u32[]{:S(2)}, u32[]{:S(2)}) %collective-permute-start.1) | collective-permute-done | bytes 430112 | tf_op jit(solution)/shard_map/ppermute | solution.py:123
  42.4 3.4 collective-permute-start.8
  52.8 13.3 %collective-permute-done.3 = bf16[4,112,640]{2,1,0:T(8,128)(2,1)} collective-permute-done((bf16[4,112,640]{2,1,0:T(8,128)(2,1)}, bf16[4,112,640]{2,1,0:T(8,128)(2,1)}, u32[]{:S(2)}, u32[]{:S(2)}) %collective-permute-start.3) | collective-permute-done | bytes 573472 | tf_op jit(solution)/shard_map/ppermute | solution.py:128
  72.1 8.3 %collective-permute-done.8 = bf16[1,320,1280]{2,1,0:T(8,128)(2,1)S(1)} collective-permute-done((bf16[1,320,1280]{2,1,0:T(8,128)(2,1)S(1)}, bf16[1,320,1280]{2,1,0:T(8,128)(2,1)S(1)}, u32[]{:S(2)}, u32[]{:S(2)}) %collective-permute-start.8) | collective-permute-done | bytes 819232 | tf_op jit(solution)/shard_map/ppermute | solution.py:123
  83.0 13.2 %collective-permute-done.11.refs_5_ = bf16[8,112,640]{2,1,0:T(8,128)(2,1)S(1)} collective-permute-done((bf16[8,112,640]{2,1,0:T(8,128)(2,1)S(1)}, bf16[8,112,640]{2,1,0:T(8,128)(2,1)S(1)}, u32[]{:S(2)}, u32[]{:S(2)}) %collective-permute-start.11) | collective-permute-done | bytes 1146912 | tf_op jit(solution)/shard_map/ppermute | solution.py:128
  96.2 5.3 collective-permute-done.10.refs_3_
  101.5 4.6 place_first.1
  112.0 11.6 %collective-permute-done.13 = bf16[2,80,1280]{2,1,0:T(8,128)(2,1)S(1)} collective-permute-done((bf16[2,80,1280]{2,1,0:T(8,128)(2,1)S(1)}, bf16[2,80,1280]{2,1,0:T(8,128)(2,1)S(1)}, u32[]{:S(2)}, u32[]{:S(2)}) %collective-permute-start.13) | collective-permute-done | bytes 409632 | tf_op jit(solution)/shard_map/ppermute | solution.py:128
  127.5 16.4 %project.1 = (bf16[1536,1280]{1,0:T(8,128)(2,1)}, bf16[1920,1536]{1,0:T(8,128)(2,1)}) custom-call(bf16[768,1280]{1,0:T(8,128)(2,1)S(1)} %pad.12.own_ref.frames_ref.refs_2_, bf16[768,1280]{1,0:T(8,128)(2,1)S(1)} %collective-permute-done.14.other_ref, f32[1,1280]{1,0:T(1,128)S(1)} %broadcast_in_dim.97.gain_ref.refs_4_, ...), custom_call_target="tpu_custom_call" | custom-call | bytes 1048576 | tf_op jit(solution)/shard_map/project/pallas_call | solution.py:328
  143.8 9.7 %collective-permute-done.18 = bf16[2,80,1280]{2,1,0:T(8,128)(2,1)S(1)} collective-permute-done((bf16[2,80,1280]{2,1,0:T(8,128)(2,1)S(1)}, bf16[2,80,1280]{2,1,0:T(8,128)(2,1)S(1)}, u32[]{:S(2)}, u32[]{:S(2)}) %collective-permute-start.18) | collective-permute-done | bytes 409632 | tf_op jit(solution)/shard_map/ppermute | solution.py:128
  163.9 17.3 %attend.2 = (bf16[4,80,1536]{2,1,0:T(8,128)(2,1)S(1)}, f32[4,1,1536]{2,1,0:T(1,128)S(1)}) custom-call(bf16[32,1536]{1,0:T(8,128)(2,1)S(1)} %pad_maximum_fusion.19.mask_ref, bf16[3,8,80,1536]{3,2,1,0:T(8,128)(2,1)} %bitcast.104, bf16[3,8,80,1536]{3,2,1,0:T(8,128)(2,1)} %bitcast.105, bf16[3,8,80,1536]{3,2,1,0:T(8,128)(2,1)} %bitcast.106), custom_call_target="tpu_custom_call" | custom-call | bytes 1048576 | tf_op jit(solution)/shard_map/attend/pallas_call | solution.py:375
  181.8 17.6 %attend.3 = (bf16[4,80,1536]{2,1,0:T(8,128)(2,1)S(1)}, f32[4,1,1536]{2,1,0:T(1,128)S(1)}) custom-call(bf16[32,1536]{1,0:T(8,128)(2,1)S(1)} %pad_maximum_fusion.19.mask_ref, bf16[3,8,80,1536]{3,2,1,0:T(8,128)(2,1)} %bitcast.107, bf16[3,8,80,1536]{3,2,1,0:T(8,128)(2,1)} %bitcast.108, bf16[3,8,80,1536]{3,2,1,0:T(8,128)(2,1)} %bitcast.109), custom_call_target="tpu_custom_call" | custom-call | bytes 1048576 | tf_op jit(solution)/shard_map/attend/pallas_call | solution.py:375
  208.7 8.9 %attended.1 = (f32[768,1280]{1,0:T(8,128)}, bf16[768,1280]{1,0:T(8,128)(2,1)}) custom-call(bf16[320,1536]{1,0:T(8,128)(2,1)S(1)} %bitcast.74, bf16[320,1536]{1,0:T(8,128)(2,1)S(1)} %bitcast.71, bf16[320,1536]{1,0:T(8,128)(2,1)S(1)} %collective-permute-done.26.ga.refs_6_, bf16[320,1536]{1,0:T(8,128)(2,1)S(1)} %collective-permute-done.27.gb.refs_7_, ...), custom_call_target="tpu_custom_call" | custom-call | bytes 1048576 | tf_op jit(solution)/shard_map/attended/pallas_call | solution.py:494
  223.1 46.0 %feed.2 = (f32[768,1280]{1,0:T(8,128)}, f32[768,1280]{1,0:T(8,128)}, bf16[2,768,1280]{2,1,0:T(8,128)(2,1)}, f32[1,1280]{1,0:T(1,128)}, bf16[8,80,1280]{2,1,0:T(8...) custom-call(bf16[768,1280]{1,0:T(8,128)(2,1)} %get-tuple-element.303, ...), custom_call_target="tpu_custom_call" | custom-call | bytes 1048576 | tf_op jit(solution)/shard_map/feed/pallas_call | solution.py:617
  272.7 59.0 %feed.3 = (f32[768,1280]{1,0:T(8,128)}, f32[768,1280]{1,0:T(8,128)}, bf16[2,768,1280]{2,1,0:T(8,128)(2,1)}, f32[1,1280]{1,0:T(1,128)}, bf16[8,80,1280]{2,1,0:T(8...) custom-call(bf16[768,1280]{1,0:T(8,128)(2,1)} %get-tuple-element.303, ...), custom_call_target="tpu_custom_call" | custom-call | bytes 1048576 | tf_op jit(solution)/shard_map/feed/pallas_call | solution.py:617
  331.8 7.0 %collective-permute-done.34.refs_3_.gb_ref = bf16[2,768,1280]{2,1,0:T(8,128)(2,1)S(1)} collective-permute-done((bf16[2,768,1280]{2,1,0:T(8,128)(2,1)}, bf16[2,768,1280]{2,1,0:T(8,128)(2,1)S(1)}, u32[]{:S(2)}, u32[]{:S(2)}) %collective-permute-start.34) | collective-permute-done | bytes 3932192 | tf_op jit(solution)/shard_map/ppermute | solution.py:58
  340.7 10.0 %norm_back.2 = (f32[768,1280]{1,0:T(8,128)}, bf16[768,1280]{1,0:T(8,128)(2,1)S(1)}, f32[8,1280]{1,0:T(8,128)S(1)}) custom-call(f32[768,1280]{1,0:T(8,128)} %get-tuple-element.294.refs_0_, f32[768,1280]{1,0:T(8,128)} %get-tuple-element.304.refs_1_, bf16[2,768,1280]{2,1,0:T(8,128)(2,1)} %collective-permute-done.31.refs_2_.ga_ref, ...), custom_call_target="tpu_custom_call" | custom-call | bytes 1048576 | tf_op jit(solution)/shard_map/norm_back/pallas_call | solution.py:678
  350.9 3.8 collective-permute-done.35.refs_1_
  361.0 10.8 %attended_back.1 = (bf16[640,1536]{1,0:T(8,128)(2,1)}, bf16[8,80,640]{2,1,0:T(8,128)(2,1)S(1)}, bf16[4,80,640]{2,1,0:T(8,128)(2,1)S(1)}, bf16[2,80,640]{2,1,0:T(...) custom-call(bf16[768,1280]{1,0:T(8,128)(2,1)} %copy-done.38, ...), custom_call_target="tpu_custom_call" | custom-call | bytes 1048576 | tf_op jit(solution)/shard_map/attended_back/pallas_call | solution.py:748
  374.4 13.1 %attend_back.4 = (bf16[2,80,1536]{2,1,0:T(8,128)(2,1)S(1)}, bf16[2,80,1536]{2,1,0:T(8,128)(2,1)S(1)}, bf16[2,80,1536]{2,1,0:T(8,128)(2,1)S(1)}) custom-call(bf16[32,1536]{1,0:T(8,128)(2,1)S(1)} %pad_maximum_fusion.19.mask_ref, bf16[3,8,80,1536]{3,2,1,0:T(8,128)(2,1)} %bitcast.110, bf16[3,8,80,1536]{3,2,1,0:T(8,128)(2,1)} %bitcast.111, ...), custom_call_target="tpu_custom_call" | custom-call | bytes 1048576 | tf_op jit(solution)/shard_map/attend_back/pallas_call | solution.py:445
  388.3 6.5 %mix.1 = (f32[768,1280]{1,0:T(8,128)S(1)}, bf16[768,1280]{1,0:T(8,128)(2,1)S(1)}) custom-call(f32[768,1280]{1,0:T(8,128)} %get-tuple-element.326.a_ref, f32[768,1280]{1,0:T(8,128)} %get-tuple-element.327.b_ref, bf16[2,768,1280]{2,1,0:T(8,128)(2,1)} %collective-permute-done.31.refs_2_.ga_ref, bf16[2,768,1280]{2,1,0:T(8,128)(2,1)} %copy-done.131, ...), custom_call_target="tpu_custom_call" | custom-call | bytes 1048576 | tf_op jit(solution)/shard_map/mix/pallas_call | solution.py:706
  400.7 13.1 %attend_back.5 = (bf16[2,80,1536]{2,1,0:T(8,128)(2,1)S(1)}, bf16[2,80,1536]{2,1,0:T(8,128)(2,1)S(1)}, bf16[2,80,1536]{2,1,0:T(8,128)(2,1)S(1)}) custom-call(bf16[32,1536]{1,0:T(8,128)(2,1)S(1)} %pad_maximum_fusion.19.mask_ref, bf16[3,8,80,1536]{3,2,1,0:T(8,128)(2,1)} %bitcast.113, bf16[3,8,80,1536]{3,2,1,0:T(8,128)(2,1)} %bitcast.114, ...), custom_call_target="tpu_custom_call" | custom-call | bytes 1048576 | tf_op jit(solution)/shard_map/attend_back/pallas_call | solution.py:445
  424.0 13.0 %attend_back.6 = (bf16[2,80,1536]{2,1,0:T(8,128)(2,1)S(1)}, bf16[2,80,1536]{2,1,0:T(8,128)(2,1)S(1)}, bf16[2,80,1536]{2,1,0:T(8,128)(2,1)S(1)}) custom-call(bf16[32,1536]{1,0:T(8,128)(2,1)S(1)} %pad_maximum_fusion.19.mask_ref, bf16[3,8,80,1536]{3,2,1,0:T(8,128)(2,1)} %bitcast.116, bf16[3,8,80,1536]{3,2,1,0:T(8,128)(2,1)} %bitcast.117, ...), custom_call_target="tpu_custom_call" | custom-call | bytes 1048576 | tf_op jit(solution)/shard_map/attend_back/pallas_call | solution.py:445
  442.4 12.0 %collective-permute-done.45.refs_2_ = bf16[4,80,640]{2,1,0:T(8,128)(2,1)S(1)} collective-permute-done((bf16[4,80,640]{2,1,0:T(8,128)(2,1)S(1)}, bf16[4,80,640]{2,1,0:T(8,128)(2,1)S(1)}, u32[]{:S(2)}, u32[]{:S(2)}) %collective-permute-start.45) | collective-permute-done | bytes 409632 | tf_op jit(solution)/shard_map/ppermute | solution.py:180
  462.6 13.4 %attend_back.7 = (bf16[2,80,1536]{2,1,0:T(8,128)(2,1)S(1)}, bf16[2,80,1536]{2,1,0:T(8,128)(2,1)S(1)}, bf16[2,80,1536]{2,1,0:T(8,128)(2,1)S(1)}) custom-call(bf16[32,1536]{1,0:T(8,128)(2,1)S(1)} %pad_maximum_fusion.19.mask_ref, bf16[3,8,80,1536]{3,2,1,0:T(8,128)(2,1)} %bitcast.119, bf16[3,8,80,1536]{3,2,1,0:T(8,128)(2,1)} %bitcast.120, ...), custom_call_target="tpu_custom_call" | custom-call | bytes 1048576 | tf_op jit(solution)/shard_map/attend_back/pallas_call | solution.py:445
  485.2 13.4 %project_grads.1 = (bf16[8,80,640]{2,1,0:T(8,128)(2,1)}, bf16[4,80,640]{2,1,0:T(8,128)(2,1)S(1)}, bf16[2,80,640]{2,1,0:T(8,128)(2,1)S(1)}, bf16[1,80,640]{2,1,0:...) custom-call(bf16[1536,1280]{1,0:T(8,128)(2,1)} %get-tuple-element.36, ...), custom_call_target="tpu_custom_call" | custom-call | bytes 1048576 | tf_op jit(solution)/shard_map/project_grads/pallas_call | solution.py:815
  522.9 13.9 %project_back.1 = (f32[768,1280]{1,0:T(8,128)}, bf16[768,1280]{1,0:T(8,128)(2,1)}) custom-call(bf16[160,1536]{1,0:T(8,128)(2,1)S(1)} %bitcast.77, bf16[160,1536]{1,0:T(8,128)(2,1)S(1)} %bitcast.82, bf16[160,1536]{1,0:T(8,128)(2,1)S(1)} %bitcast.86, bf16[160,1536]{1,0:T(8,128)(2,1)S(1)} %bitcast.90, bf16[160,1536]{1,0:T(8,128)(2,1)S(1)} %bitcast.94, ...), custom_call_target="tpu_custom_call" | custom-call | bytes 1048576 | tf_op jit(solution)/shard_map/project_back/pallas_call | solution.py:781
  554.1 8.1 %norm_back.3 = (f32[768,1280]{1,0:T(8,128)}, bf16[768,1280]{1,0:T(8,128)(2,1)S(1)}, f32[8,1280]{1,0:T(8,128)S(1)}) custom-call(f32[768,1280]{1,0:T(8,128)} %get-tuple-element.418.refs_0_, bf16[768,1280]{1,0:T(8,128)(2,1)} %collective-permute-done.56.refs_1_, bf16[768,1280]{1,0:T(8,128)(2,1)S(1)} %copy-done.1, f32[768,1280]{1,0:T(8,128)} %get-tuple-element.421.refs_3_, ...), custom_call_target="tpu_custom_call" | custom-call | bytes 1048576 | tf_op jit(solution)/shard_map/norm_back/pallas_call | solution.py:678
  571.8 5.0 slice_select_fusion.1
  581.0 9.6 %adam_feed.1 = (f32[80,5120]{1,0:T(8,128)}, bf16[80,5120]{1,0:T(8,128)(2,1)}, f32[80,5120]{1,0:T(8,128)}, f32[80,5120]{1,0:T(8,128)}, f32[4,80,1280]{2,1,0:T(8,1...) custom-call(f32[1,80,1280]{2,1,0:T(8,128)S(1)} %copy-done.63, ...), custom_call_target="tpu_custom_call" | custom-call | bytes 1048576 | tf_op jit(solution)/shard_map/adam_feed/pallas_call | solution.py:883
  590.7 4.7 collective-permute-done.66
  (643 shorter events, 195.6 us)
Async XLA Ops:
  7.2 60.0 %collective-permute-start = (bf16[750,1280]{1,0:T(8,128)(2,1)}, bf16[750,1280]{1,0:T(8,128)(2,1)}, u32[]{:S(2)}, u32[]{:S(2)}) collective-permute-start(bf16[750,1280]{1,0:T(8,128)(2,1)} %param.18), channel_id=1, source_target_pairs={{1,16},{3,18},{5,20},{7,22},{9,24},{11,26},{13,28},{15,30},{16,1},... | collective-permute-start | bytes 5760008 | tf_op jit(solution)/shard_map/ppermute | solution.py:72
  42.4 37.9 %collective-permute-start.8 = (bf16[1,320,1280]{2,1,0:T(8,128)(2,1)S(1)}, bf16[1,320,1280]{2,1,0:T(8,128)(2,1)S(1)}, u32[]{:S(2)}, u32[]{:S(2)}) collective-permute-start(bf16[1,320,1280]{2,1,0:T(8,128)(2,1)S(1)} %pad_maximum_fusion.3), channel_id=1, source_target_pairs={{0,8},{1,9},{2,10},{3,11},{4,12},{5,13},{6,14},{7,15},{8,0},{9,1},... | collective-permute-start | bytes 2457608 | tf_op jit(solution)/shard_map/ppermute | solution.py:123
  67.6 28.6 %collective-permute-start.11 = (bf16[8,112,640]{2,1,0:T(8,128)(2,1)S(1)}, bf16[8,112,640]{2,1,0:T(8,128)(2,1)S(1)}, u32[]{:S(2)}, u32[]{:S(2)}) collective-permute-start(bf16[8,112,640]{2,1,0:T(8,128)(2,1)S(1)} %pad_maximum_fusion.2.refs_4_), channel_id=1, source_target_pairs={{0,1},{1,0},{2,3},{3,2},{4,5},{5,4},{6,7},{7,6},{8,9},{9,8},{10,11... | collective-permute-start | bytes 3440648 | tf_op jit(solution)/shard_map/ppermute | solution.py:128
  70.5 31.0 %collective-permute-start.10 = (bf16[8,112,640]{2,1,0:T(8,128)(2,1)S(1)}, bf16[8,112,640]{2,1,0:T(8,128)(2,1)S(1)}, u32[]{:S(2)}, u32[]{:S(2)}) collective-permute-start(bf16[8,112,640]{2,1,0:T(8,128)(2,1)S(1)} %pad_maximum_fusion.1.refs_2_), channel_id=1, source_target_pairs={{0,4},{1,5},{2,6},{3,7},{4,0},{5,1},{6,2},{7,3},{8,12},{9,13},{10,... | collective-permute-start | bytes 3440648 | tf_op jit(solution)/shard_map/ppermute | solution.py:128
  70.5 31.0 %collective-permute-start.9 = (bf16[8,112,640]{2,1,0:T(8,128)(2,1)S(1)}, bf16[8,112,640]{2,1,0:T(8,128)(2,1)S(1)}, u32[]{:S(2)}, u32[]{:S(2)}) collective-permute-start(bf16[8,112,640]{2,1,0:T(8,128)(2,1)S(1)} %pad_maximum_fusion.refs_0_), channel_id=1, source_target_pairs={{0,2},{1,3},{2,0},{3,1},{4,6},{5,7},{6,4},{7,5},{8,10},{9,11},{10,... | collective-permute-start | bytes 3440648 | tf_op jit(solution)/shard_map/ppermute | solution.py:128
  81.1 75.2 %collective-permute-start.20 = (bf16[750,1280]{1,0:T(8,128)(2,1)}, bf16[750,1280]{1,0:T(8,128)(2,1)}, u32[]{:S(2)}, u32[]{:S(2)}) collective-permute-start(bf16[750,1280]{1,0:T(8,128)(2,1)} %param.19), channel_id=1, source_target_pairs={{1,16},{3,18},{5,20},{7,22},{9,24},{11,26},{13,28},{15,30},{16,1},... | collective-permute-start | bytes 5760008 | tf_op jit(solution)/shard_map/ppermute | solution.py:72
  124.4 29.1 %collective-permute-start.16 = (bf16[4,80,1280]{2,1,0:T(8,128)(2,1)S(1)}, bf16[4,80,1280]{2,1,0:T(8,128)(2,1)S(1)}, u32[]{:S(2)}, u32[]{:S(2)}) collective-permute-start(bf16[4,80,1280]{2,1,0:T(8,128)(2,1)S(1)} %get-tuple-element.510), channel_id=1, source_target_pairs={{0,4},{1,5},{2,6},{3,7},{4,0},{5,1},{6,2},{7,3},{8,12},{9,13},{10,... | collective-permute-start | bytes 2457608 | tf_op jit(solution)/shard_map/ppermute | solution.py:128
  125.2 28.3 %collective-permute-start.15 = (bf16[4,80,1280]{2,1,0:T(8,128)(2,1)S(1)}, bf16[4,80,1280]{2,1,0:T(8,128)(2,1)S(1)}, u32[]{:S(2)}, u32[]{:S(2)}) collective-permute-start(bf16[4,80,1280]{2,1,0:T(8,128)(2,1)S(1)} %get-tuple-element.512), channel_id=1, source_target_pairs={{0,2},{1,3},{2,0},{3,1},{4,6},{5,7},{6,4},{7,5},{8,10},{9,11},{10,... | collective-permute-start | bytes 2457608 | tf_op jit(solution)/shard_map/ppermute | solution.py:128
  125.8 27.8 %collective-permute-start.18 = (bf16[2,80,1280]{2,1,0:T(8,128)(2,1)S(1)}, bf16[2,80,1280]{2,1,0:T(8,128)(2,1)S(1)}, u32[]{:S(2)}, u32[]{:S(2)}) collective-permute-start(bf16[2,80,1280]{2,1,0:T(8,128)(2,1)S(1)} %pad_maximum_fusion.11), channel_id=1, source_target_pairs={{0,2},{1,3},{2,0},{3,1},{4,6},{5,7},{6,4},{7,5},{8,10},{9,11},{10,... | collective-permute-start | bytes 1228808 | tf_op jit(solution)/shard_map/ppermute | solution.py:128
  158.1 43.4 %collective-permute-start.24 = (bf16[768,1280]{1,0:T(8,128)(2,1)S(1)}, bf16[768,1280]{1,0:T(8,128)(2,1)S(1)}, u32[]{:S(2)}, u32[]{:S(2)}) collective-permute-start(bf16[768,1280]{1,0:T(8,128)(2,1)S(1)} %pad.13.refs_2_.refs_5_), channel_id=1, source_target_pairs={{0,16},{16,0},{1,17},{17,1},{2,18},{18,2},{3,19},{19,3},{4,20},{20... | collective-permute-start | bytes 5898248 | tf_op jit(solution)/shard_map/ppermute | solution.py:58
  159.5 44.0 %collective-permute-start.22 = (bf16[8,80,1280]{2,1,0:T(8,128)(2,1)}, bf16[8,80,1280]{2,1,0:T(8,128)(2,1)S(1)}, u32[]{:S(2)}, u32[]{:S(2)}) collective-permute-start(bf16[8,80,1280]{2,1,0:T(8,128)(2,1)} %constant_dynamic-update-slice_fusion.10.refs_6_), channel_id=1, source_target_pairs={{0,2},{1,3},{2,0},{3,1},{4,6},{5,7},{6,4},{7,5},{8,10},{9,11},{10,... | collective-permute-start | bytes 4915208 | tf_op jit(solution)/shard_map/ppermute | solution.py:128
  159.8 43.7 %collective-permute-start.21 = (bf16[8,80,1280]{2,1,0:T(8,128)(2,1)}, bf16[8,80,1280]{2,1,0:T(8,128)(2,1)S(1)}, u32[]{:S(2)}, u32[]{:S(2)}) collective-permute-start(bf16[8,80,1280]{2,1,0:T(8,128)(2,1)} %constant_dynamic-update-slice_fusion.6.refs_4_), channel_id=1, source_target_pairs={{0,1},{1,0},{2,3},{3,2},{4,5},{5,4},{6,7},{7,6},{8,9},{9,8},{10,11... | collective-permute-start | bytes 4915208 | tf_op jit(solution)/shard_map/ppermute | solution.py:128
  161.5 40.1 %collective-permute-start.25 = (bf16[4,80,1280]{2,1,0:T(8,128)(2,1)S(1)}, bf16[4,80,1280]{2,1,0:T(8,128)(2,1)S(1)}, u32[]{:S(2)}, u32[]{:S(2)}) collective-permute-start(bf16[4,80,1280]{2,1,0:T(8,128)(2,1)S(1)} %copy-done.141), channel_id=1, source_target_pairs={{0,4},{1,5},{2,6},{3,7},{4,0},{5,1},{6,2},{7,3},{8,12},{9,13},{10,... | collective-permute-start | bytes 2457608 | tf_op jit(solution)/shard_map/ppermute | solution.py:128
  163.8 37.8 %collective-permute-start.23 = (bf16[4,80,1280]{2,1,0:T(8,128)(2,1)S(1)}, bf16[4,80,1280]{2,1,0:T(8,128)(2,1)S(1)}, u32[]{:S(2)}, u32[]{:S(2)}) collective-permute-start(bf16[4,80,1280]{2,1,0:T(8,128)(2,1)S(1)} %constant_dynamic-update-slice_fusion.14), channel_id=1, source_target_pairs={{0,4},{1,5},{2,6},{3,7},{4,0},{5,1},{6,2},{7,3},{8,12},{9,13},{10,... | collective-permute-start | bytes 2457608 | tf_op jit(solution)/shard_map/ppermute | solution.py:128
  217.8 51.3 %collective-permute-start.30 = (bf16[8,80,1280]{2,1,0:T(8,128)(2,1)}, bf16[8,80,1280]{2,1,0:T(8,128)(2,1)}, u32[]{:S(2)}, u32[]{:S(2)}) collective-permute-start(bf16[8,80,1280]{2,1,0:T(8,128)(2,1)} %constant_dynamic-update-slice_fusion.20.refs_6_), channel_id=1, source_target_pairs={{0,1},{1,0},{2,3},{3,2},{4,5},{5,4},{6,7},{7,6},{8,9},{9,8},{10,11... | collective-permute-start | bytes 4915208 | tf_op jit(solution)/shard_map/ppermute | solution.py:128
  218.1 51.1 %collective-permute-start.29 = (bf16[8,80,1280]{2,1,0:T(8,128)(2,1)}, bf16[8,80,1280]{2,1,0:T(8,128)(2,1)}, u32[]{:S(2)}, u32[]{:S(2)}) collective-permute-start(bf16[8,80,1280]{2,1,0:T(8,128)(2,1)} %constant_dynamic-update-slice_fusion.18.refs_4_), channel_id=1, source_target_pairs={{0,2},{1,3},{2,0},{3,1},{4,6},{5,7},{6,4},{7,5},{8,10},{9,11},{10,... | collective-permute-start | bytes 4915208 | tf_op jit(solution)/shard_map/ppermute | solution.py:128
  269.2 62.5 %collective-permute-start.31 = (bf16[2,768,1280]{2,1,0:T(8,128)(2,1)}, bf16[2,768,1280]{2,1,0:T(8,128)(2,1)}, u32[]{:S(2)}, u32[]{:S(2)}) collective-permute-start(bf16[2,768,1280]{2,1,0:T(8,128)(2,1)} %get-tuple-element.302), channel_id=1, source_target_pairs={{0,16},{16,0},{1,17},{17,1},{2,18},{18,2},{3,19},{19,3},{4,20},{20... | collective-permute-start | bytes 11796488 | tf_op jit(solution)/shard_map/ppermute | solution.py:58
  269.4 62.3 %collective-permute-start.33 = (bf16[8,80,1280]{2,1,0:T(8,128)(2,1)}, bf16[8,80,1280]{2,1,0:T(8,128)(2,1)}, u32[]{:S(2)}, u32[]{:S(2)}) collective-permute-start(bf16[8,80,1280]{2,1,0:T(8,128)(2,1)} %get-tuple-element.300), channel_id=1, source_target_pairs={{0,4},{1,5},{2,6},{3,7},{4,0},{5,1},{6,2},{7,3},{8,12},{9,13},{10,... | collective-permute-start | bytes 4915208 | tf_op jit(solution)/shard_map/ppermute | solution.py:180
  271.4 60.3 %collective-permute-start.32 = (bf16[8,80,1280]{2,1,0:T(8,128)(2,1)}, bf16[8,80,1280]{2,1,0:T(8,128)(2,1)S(1)}, u32[]{:S(2)}, u32[]{:S(2)}) collective-permute-start(bf16[8,80,1280]{2,1,0:T(8,128)(2,1)} %get-tuple-element.298), channel_id=1, source_target_pairs={{0,2},{1,3},{2,0},{3,1},{4,6},{5,7},{6,4},{7,5},{8,10},{9,11},{10,... | collective-permute-start | bytes 4915208 | tf_op jit(solution)/shard_map/ppermute | solution.py:180
  354.7 63.6 %collective-permute-start.39 = (bf16[8,80,1280]{2,1,0:T(8,128)(2,1)}, bf16[8,80,1280]{2,1,0:T(8,128)(2,1)}, u32[]{:S(2)}, u32[]{:S(2)}) collective-permute-start(bf16[8,80,1280]{2,1,0:T(8,128)(2,1)} %get-tuple-element.315), channel_id=1, source_target_pairs={{0,4},{1,5},{2,6},{3,7},{4,0},{5,1},{6,2},{7,3},{8,12},{9,13},{10,... | collective-permute-start | bytes 4915208 | tf_op jit(solution)/shard_map/ppermute | solution.py:180
  354.8 63.5 %collective-permute-start.38 = (bf16[8,80,1280]{2,1,0:T(8,128)(2,1)}, bf16[8,80,1280]{2,1,0:T(8,128)(2,1)S(1)}, u32[]{:S(2)}, u32[]{:S(2)}) collective-permute-start(bf16[8,80,1280]{2,1,0:T(8,128)(2,1)} %get-tuple-element.313), channel_id=1, source_target_pairs={{0,2},{1,3},{2,0},{3,1},{4,6},{5,7},{6,4},{7,5},{8,10},{9,11},{10,... | collective-permute-start | bytes 4915208 | tf_op jit(solution)/shard_map/ppermute | solution.py:180
  358.9 55.8 %collective-permute-start.36 = (bf16[4,80,1280]{2,1,0:T(8,128)(2,1)}, bf16[4,80,1280]{2,1,0:T(8,128)(2,1)S(1)}, u32[]{:S(2)}, u32[]{:S(2)}) collective-permute-start(bf16[4,80,1280]{2,1,0:T(8,128)(2,1)} %get-tuple-element.320), channel_id=1, source_target_pairs={{0,1},{1,0},{2,3},{3,2},{4,5},{5,4},{6,7},{7,6},{8,9},{9,8},{10,11... | collective-permute-start | bytes 2457608 | tf_op jit(solution)/shard_map/ppermute | solution.py:180
  359.1 56.3 %collective-permute-start.37 = (bf16[4,80,1280]{2,1,0:T(8,128)(2,1)}, bf16[4,80,1280]{2,1,0:T(8,128)(2,1)S(1)}, u32[]{:S(2)}, u32[]{:S(2)}) collective-permute-start(bf16[4,80,1280]{2,1,0:T(8,128)(2,1)} %get-tuple-element.321), channel_id=1, source_target_pairs={{0,1},{1,0},{2,3},{3,2},{4,5},{5,4},{6,7},{7,6},{8,9},{9,8},{10,11... | collective-permute-start | bytes 2457608 | tf_op jit(solution)/shard_map/ppermute | solution.py:180
  420.6 34.4 %collective-permute-start.43 = (bf16[4,80,1280]{2,1,0:T(8,128)(2,1)}, bf16[4,80,1280]{2,1,0:T(8,128)(2,1)S(1)}, u32[]{:S(2)}, u32[]{:S(2)}) collective-permute-start(bf16[4,80,1280]{2,1,0:T(8,128)(2,1)} %get-tuple-element.344), channel_id=1, source_target_pairs={{0,1},{1,0},{2,3},{3,2},{4,5},{5,4},{6,7},{7,6},{8,9},{9,8},{10,11... | collective-permute-start | bytes 2457608 | tf_op jit(solution)/shard_map/ppermute | solution.py:180
  421.8 33.2 %collective-permute-start.44 = (bf16[4,80,1280]{2,1,0:T(8,128)(2,1)S(1)}, bf16[4,80,1280]{2,1,0:T(8,128)(2,1)S(1)}, u32[]{:S(2)}, u32[]{:S(2)}) collective-permute-start(bf16[4,80,1280]{2,1,0:T(8,128)(2,1)S(1)} %get-tuple-element.345), channel_id=1, source_target_pairs={{0,2},{1,3},{2,0},{3,1},{4,6},{5,7},{6,4},{7,5},{8,10},{9,11},{10,... | collective-permute-start | bytes 2457608 | tf_op jit(solution)/shard_map/ppermute | solution.py:180
  422.3 32.1 %collective-permute-start.45 = (bf16[4,80,640]{2,1,0:T(8,128)(2,1)S(1)}, bf16[4,80,640]{2,1,0:T(8,128)(2,1)S(1)}, u32[]{:S(2)}, u32[]{:S(2)}) collective-permute-start(bf16[4,80,640]{2,1,0:T(8,128)(2,1)S(1)} %add_blocks.19), channel_id=1, source_target_pairs={{0,2},{1,3},{2,0},{3,1},{4,6},{5,7},{6,4},{7,5},{8,10},{9,11},{10,... | collective-permute-start | bytes 1228808 | tf_op jit(solution)/shard_map/ppermute | solution.py:180
  460.7 46.1 %collective-permute-start.46 = (bf16[768,1280]{1,0:T(8,128)(2,1)}, bf16[768,1280]{1,0:T(8,128)(2,1)}, u32[]{:S(2)}, u32[]{:S(2)}) collective-permute-start(bf16[768,1280]{1,0:T(8,128)(2,1)} %copy-done.125), channel_id=1, source_target_pairs={{1,16},{3,18},{5,20},{7,22},{9,24},{11,26},{13,28},{15,30},{16,1},... | collective-permute-start | bytes 5898248 | tf_op jit(solution)/shard_map/ppermute | solution.py:72
  506.7 30.1 %collective-permute-start.55 = (bf16[8,80,640]{2,1,0:T(8,128)(2,1)}, bf16[8,80,640]{2,1,0:T(8,128)(2,1)S(1)}, u32[]{:S(2)}, u32[]{:S(2)}) collective-permute-start(bf16[8,80,640]{2,1,0:T(8,128)(2,1)} %get-tuple-element.406), channel_id=1, source_target_pairs={{0,1},{1,0},{2,3},{3,2},{4,5},{5,4},{6,7},{7,6},{8,9},{9,8},{10,11... | collective-permute-start | bytes 2457608 | tf_op jit(solution)/shard_map/ppermute | solution.py:180
  507.1 29.8 %collective-permute-start.54 = (bf16[8,80,640]{2,1,0:T(8,128)(2,1)}, bf16[8,80,640]{2,1,0:T(8,128)(2,1)S(1)}, u32[]{:S(2)}, u32[]{:S(2)}) collective-permute-start(bf16[8,80,640]{2,1,0:T(8,128)(2,1)} %get-tuple-element.404), channel_id=1, source_target_pairs={{0,4},{1,5},{2,6},{3,7},{4,0},{5,1},{6,2},{7,3},{8,12},{9,13},{10,... | collective-permute-start | bytes 2457608 | tf_op jit(solution)/shard_map/ppermute | solution.py:180
  508.7 28.1 %collective-permute-start.53 = (bf16[8,80,640]{2,1,0:T(8,128)(2,1)}, bf16[8,80,640]{2,1,0:T(8,128)(2,1)S(1)}, u32[]{:S(2)}, u32[]{:S(2)}) collective-permute-start(bf16[8,80,640]{2,1,0:T(8,128)(2,1)} %get-tuple-element.402), channel_id=1, source_target_pairs={{0,2},{1,3},{2,0},{3,1},{4,6},{5,7},{6,4},{7,5},{8,10},{9,11},{10,... | collective-permute-start | bytes 2457608 | tf_op jit(solution)/shard_map/ppermute | solution.py:180
  510.8 35.6 %collective-permute-start.65 = (f32[1,360,1280]{2,1,0:T(8,128)}, f32[1,360,1280]{2,1,0:T(8,128)}, u32[]{:S(2)}, u32[]{:S(2)}) collective-permute-start(f32[1,360,1280]{2,1,0:T(8,128)} %maximum_dynamic-update-slice_fusion), channel_id=1, source_target_pairs={{0,16},{16,0},{1,17},{17,1},{2,18},{18,2},{3,19},{19,3},{4,20},{20... | collective-permute-start | bytes 5529608 | tf_op jit(solution)/shard_map/ppermute | solution.py:58
  570.9 27.8 %collective-permute-start.60 = (bf16[768,1280]{1,0:T(8,128)(2,1)}, bf16[768,1280]{1,0:T(8,128)(2,1)S(1)}, u32[]{:S(2)}, u32[]{:S(2)}) collective-permute-start(bf16[768,1280]{1,0:T(8,128)(2,1)} %copy-done.126), channel_id=1, source_target_pairs={{1,16},{3,18},{5,20},{7,22},{9,24},{11,26},{13,28},{15,30},{16,1},... | collective-permute-start | bytes 5898248 | tf_op jit(solution)/shard_map/ppermute | solution.py:72
  (209 other events, 1647.7 us)

commit v4 on v3

--- a/solution.py
+++ b/solution.py
@@ -1104,10 +1104,10 @@
         w_out_other,
         (flat_a, flat_b),
         (got_a, got_b),
-        scatter_plan(back["xyz"]),
+        scatter_plan(back["xzy"]),
         shards,
     )
-    chunks_out = Halving([list(out_parts)], [back["xyz"]])
+    chunks_out = Halving([list(out_parts)], [back["xzy"]])
     grad_context = grad_context.reshape(heads, HEAD_DIM, rows)
     calls = 4
     each = heads // calls

time: 616 us -> 614 us (level)
    ppermute x25, waiting for transfers between devices: 12 us -> 1.56 us  [step(): lax.ppermute(send, 'shard', xor_pairs(shards, mask))]
    ppermute x3, waiting for transfers between devices: 5.76 us -> 13.2 us  [step(): together = lax.ppermute(together, 'shard', xor_pairs(shards, masks[0]))]
  transfers between devices with their start and end apart: 72 -> 72, of which waited for: 21 -> 22; matrix products, arithmetic and copies ran while one was open for 10% -> 10% of each run, Pallas kernels for 48% -> 48%
where the time goes in v4:
time: 614 us; the launch traced here: 607 us
  Pallas kernels  314 us (51%)
  waiting for transfers between devices  117 us (19%)
  local copies, waits for them, and re-layouts  72.6 us (12%)
  starting transfers between devices  70.7 us (12%)
  other arithmetic  29.6 us (5%)
    pallas_call x2, Pallas kernels, feed(): call(body, shapes, limit=60, grid=(2 + tiles,), in_specs=[whole] * 4 + [A...  105 us
    ppermute x21, waiting for transfers between devices, start(): lax.ppermute(held, 'shard', xor_pairs(shards, mask))  61.6 us
    pallas_call x4, Pallas kernels, attend_back(): pl.pallas_call(functools.partial(attend_back_kernel, step=step), grid=(he...  52.6 us
    unnamed x361, local copies, waits for them, and re-layouts  48.4 us
    pallas_call x2, Pallas kernels, attend(): pl.pallas_call(functools.partial(attend_kernel, step=step), grid=(heads,)...  34.9 us
    ppermute x25, starting transfers between devices, step(): lax.ppermute(send, 'shard', xor_pairs(shards, mask))  25.6 us
    ppermute x2, waiting for transfers between devices, start(): together = lax.ppermute(together, 'shard', xor_pairs(shards, masks[0]))  21.9 us
    ppermute x21, starting transfers between devices, start(): lax.ppermute(held, 'shard', xor_pairs(shards, mask))  20.6 us
  transfers between devices with their start and end apart: 72, of which 22 were waited for; matrix products, arithmetic and copies ran while one was open for 10% of the time, Pallas kernels for 48%

profile of v4, /device:TPU:0, one launch (start us, length us, event | category | flops | bytes accessed | tf_op | source)
XLA Modules:
  0.0 606.6 jit_solution(11335766785632318338)
XLA Ops:
  3.1 4.1 collective-permute-start.1
  12.8 13.6 %collective-permute-done.1 = bf16[1,336,640]{2,1,0:T(8,128)(2,1)S(1)} collective-permute-done((bf16[1,336,640]{2,1,0:T(8,128)(2,1)S(1)}, bf16[1,336,640]{2,1,0:T(8,128)(2,1)S(1)}, u32[]{:S(2)}, u32[]{:S(2)}) %collective-permute-start.1) | collective-permute-done | bytes 430112 | tf_op jit(solution)/shard_map/ppermute | solution.py:123
  42.4 3.4 collective-permute-start.8
  52.8 13.3 %collective-permute-done.3 = bf16[4,112,640]{2,1,0:T(8,128)(2,1)} collective-permute-done((bf16[4,112,640]{2,1,0:T(8,128)(2,1)}, bf16[4,112,640]{2,1,0:T(8,128)(2,1)}, u32[]{:S(2)}, u32[]{:S(2)}) %collective-permute-start.3) | collective-permute-done | bytes 573472 | tf_op jit(solution)/shard_map/ppermute | solution.py:128
  72.1 8.3 %collective-permute-done.8 = bf16[1,320,1280]{2,1,0:T(8,128)(2,1)S(1)} collective-permute-done((bf16[1,320,1280]{2,1,0:T(8,128)(2,1)S(1)}, bf16[1,320,1280]{2,1,0:T(8,128)(2,1)S(1)}, u32[]{:S(2)}, u32[]{:S(2)}) %collective-permute-start.8) | collective-permute-done | bytes 819232 | tf_op jit(solution)/shard_map/ppermute | solution.py:123
  83.0 13.2 %collective-permute-done.11.refs_5_ = bf16[8,112,640]{2,1,0:T(8,128)(2,1)S(1)} collective-permute-done((bf16[8,112,640]{2,1,0:T(8,128)(2,1)S(1)}, bf16[8,112,640]{2,1,0:T(8,128)(2,1)S(1)}, u32[]{:S(2)}, u32[]{:S(2)}) %collective-permute-start.11) | collective-permute-done | bytes 1146912 | tf_op jit(solution)/shard_map/ppermute | solution.py:128
  96.2 5.3 collective-permute-done.10.refs_3_
  101.5 4.6 place_first.1
  112.0 11.6 %collective-permute-done.13 = bf16[2,80,1280]{2,1,0:T(8,128)(2,1)S(1)} collective-permute-done((bf16[2,80,1280]{2,1,0:T(8,128)(2,1)S(1)}, bf16[2,80,1280]{2,1,0:T(8,128)(2,1)S(1)}, u32[]{:S(2)}, u32[]{:S(2)}) %collective-permute-start.13) | collective-permute-done | bytes 409632 | tf_op jit(solution)/shard_map/ppermute | solution.py:128
  127.5 16.4 %project.1 = (bf16[1536,1280]{1,0:T(8,128)(2,1)}, bf16[1920,1536]{1,0:T(8,128)(2,1)}) custom-call(bf16[768,1280]{1,0:T(8,128)(2,1)S(1)} %pad.12.own_ref.frames_ref.refs_2_, bf16[768,1280]{1,0:T(8,128)(2,1)S(1)} %collective-permute-done.14.other_ref, f32[1,1280]{1,0:T(1,128)S(1)} %broadcast_in_dim.97.gain_ref.refs_4_, ...), custom_call_target="tpu_custom_call" | custom-call | bytes 1048576 | tf_op jit(solution)/shard_map/project/pallas_call | solution.py:328
  143.8 9.7 %collective-permute-done.18 = bf16[2,80,1280]{2,1,0:T(8,128)(2,1)S(1)} collective-permute-done((bf16[2,80,1280]{2,1,0:T(8,128)(2,1)S(1)}, bf16[2,80,1280]{2,1,0:T(8,128)(2,1)S(1)}, u32[]{:S(2)}, u32[]{:S(2)}) %collective-permute-start.18) | collective-permute-done | bytes 409632 | tf_op jit(solution)/shard_map/ppermute | solution.py:128
  163.9 17.3 %attend.2 = (bf16[4,80,1536]{2,1,0:T(8,128)(2,1)S(1)}, f32[4,1,1536]{2,1,0:T(1,128)S(1)}) custom-call(bf16[32,1536]{1,0:T(8,128)(2,1)S(1)} %pad_maximum_fusion.19.mask_ref, bf16[3,8,80,1536]{3,2,1,0:T(8,128)(2,1)} %bitcast.104, bf16[3,8,80,1536]{3,2,1,0:T(8,128)(2,1)} %bitcast.105, bf16[3,8,80,1536]{3,2,1,0:T(8,128)(2,1)} %bitcast.106), custom_call_target="tpu_custom_call" | custom-call | bytes 1048576 | tf_op jit(solution)/shard_map/attend/pallas_call | solution.py:375
  181.8 17.6 %attend.3 = (bf16[4,80,1536]{2,1,0:T(8,128)(2,1)S(1)}, f32[4,1,1536]{2,1,0:T(1,128)S(1)}) custom-call(bf16[32,1536]{1,0:T(8,128)(2,1)S(1)} %pad_maximum_fusion.19.mask_ref, bf16[3,8,80,1536]{3,2,1,0:T(8,128)(2,1)} %bitcast.107, bf16[3,8,80,1536]{3,2,1,0:T(8,128)(2,1)} %bitcast.108, bf16[3,8,80,1536]{3,2,1,0:T(8,128)(2,1)} %bitcast.109), custom_call_target="tpu_custom_call" | custom-call | bytes 1048576 | tf_op jit(solution)/shard_map/attend/pallas_call | solution.py:375
  208.7 8.9 %attended.1 = (f32[768,1280]{1,0:T(8,128)}, bf16[768,1280]{1,0:T(8,128)(2,1)}) custom-call(bf16[320,1536]{1,0:T(8,128)(2,1)S(1)} %bitcast.74, bf16[320,1536]{1,0:T(8,128)(2,1)S(1)} %bitcast.71, bf16[320,1536]{1,0:T(8,128)(2,1)S(1)} %collective-permute-done.26.ga.refs_6_, bf16[320,1536]{1,0:T(8,128)(2,1)S(1)} %collective-permute-done.27.gb.refs_7_, ...), custom_call_target="tpu_custom_call" | custom-call | bytes 1048576 | tf_op jit(solution)/shard_map/attended/pallas_call | solution.py:494
  223.1 46.0 %feed.2 = (f32[768,1280]{1,0:T(8,128)}, f32[768,1280]{1,0:T(8,128)}, bf16[2,768,1280]{2,1,0:T(8,128)(2,1)}, f32[1,1280]{1,0:T(1,128)}, bf16[8,80,1280]{2,1,0:T(8...) custom-call(bf16[768,1280]{1,0:T(8,128)(2,1)} %get-tuple-element.303, ...), custom_call_target="tpu_custom_call" | custom-call | bytes 1048576 | tf_op jit(solution)/shard_map/feed/pallas_call | solution.py:617
  272.7 59.0 %feed.3 = (f32[768,1280]{1,0:T(8,128)}, f32[768,1280]{1,0:T(8,128)}, bf16[2,768,1280]{2,1,0:T(8,128)(2,1)}, f32[1,1280]{1,0:T(1,128)}, bf16[8,80,1280]{2,1,0:T(8...) custom-call(bf16[768,1280]{1,0:T(8,128)(2,1)} %get-tuple-element.303, ...), custom_call_target="tpu_custom_call" | custom-call | bytes 1048576 | tf_op jit(solution)/shard_map/feed/pallas_call | solution.py:617
  331.8 7.0 %collective-permute-done.34.refs_3_.gb_ref = bf16[2,768,1280]{2,1,0:T(8,128)(2,1)S(1)} collective-permute-done((bf16[2,768,1280]{2,1,0:T(8,128)(2,1)}, bf16[2,768,1280]{2,1,0:T(8,128)(2,1)S(1)}, u32[]{:S(2)}, u32[]{:S(2)}) %collective-permute-start.34) | collective-permute-done | bytes 3932192 | tf_op jit(solution)/shard_map/ppermute | solution.py:58
  340.7 10.0 %norm_back.2 = (f32[768,1280]{1,0:T(8,128)}, bf16[768,1280]{1,0:T(8,128)(2,1)S(1)}, f32[8,1280]{1,0:T(8,128)S(1)}) custom-call(f32[768,1280]{1,0:T(8,128)} %get-tuple-element.294.refs_0_, f32[768,1280]{1,0:T(8,128)} %get-tuple-element.304.refs_1_, bf16[2,768,1280]{2,1,0:T(8,128)(2,1)} %collective-permute-done.31.refs_2_.ga_ref, ...), custom_call_target="tpu_custom_call" | custom-call | bytes 1048576 | tf_op jit(solution)/shard_map/norm_back/pallas_call | solution.py:678
  350.9 3.8 collective-permute-done.35.refs_1_
  361.0 10.8 %attended_back.1 = (bf16[640,1536]{1,0:T(8,128)(2,1)}, bf16[8,80,640]{2,1,0:T(8,128)(2,1)S(1)}, bf16[4,80,640]{2,1,0:T(8,128)(2,1)S(1)}, bf16[2,80,640]{2,1,0:T(...) custom-call(bf16[768,1280]{1,0:T(8,128)(2,1)} %copy-done.38, ...), custom_call_target="tpu_custom_call" | custom-call | bytes 1048576 | tf_op jit(solution)/shard_map/attended_back/pallas_call | solution.py:748
  374.4 13.1 %attend_back.4 = (bf16[2,80,1536]{2,1,0:T(8,128)(2,1)S(1)}, bf16[2,80,1536]{2,1,0:T(8,128)(2,1)S(1)}, bf16[2,80,1536]{2,1,0:T(8,128)(2,1)S(1)}) custom-call(bf16[32,1536]{1,0:T(8,128)(2,1)S(1)} %pad_maximum_fusion.19.mask_ref, bf16[3,8,80,1536]{3,2,1,0:T(8,128)(2,1)} %bitcast.110, bf16[3,8,80,1536]{3,2,1,0:T(8,128)(2,1)} %bitcast.111, ...), custom_call_target="tpu_custom_call" | custom-call | bytes 1048576 | tf_op jit(solution)/shard_map/attend_back/pallas_call | solution.py:445
  388.3 6.5 %mix.1 = (f32[768,1280]{1,0:T(8,128)S(1)}, bf16[768,1280]{1,0:T(8,128)(2,1)S(1)}) custom-call(f32[768,1280]{1,0:T(8,128)} %get-tuple-element.326.a_ref, f32[768,1280]{1,0:T(8,128)} %get-tuple-element.327.b_ref, bf16[2,768,1280]{2,1,0:T(8,128)(2,1)} %collective-permute-done.31.refs_2_.ga_ref, bf16[2,768,1280]{2,1,0:T(8,128)(2,1)} %copy-done.131, ...), custom_call_target="tpu_custom_call" | custom-call | bytes 1048576 | tf_op jit(solution)/shard_map/mix/pallas_call | solution.py:706
  399.4 13.1 %attend_back.5 = (bf16[2,80,1536]{2,1,0:T(8,128)(2,1)S(1)}, bf16[2,80,1536]{2,1,0:T(8,128)(2,1)S(1)}, bf16[2,80,1536]{2,1,0:T(8,128)(2,1)S(1)}) custom-call(bf16[32,1536]{1,0:T(8,128)(2,1)S(1)} %pad_maximum_fusion.19.mask_ref, bf16[3,8,80,1536]{3,2,1,0:T(8,128)(2,1)} %bitcast.113, bf16[3,8,80,1536]{3,2,1,0:T(8,128)(2,1)} %bitcast.114, ...), custom_call_target="tpu_custom_call" | custom-call | bytes 1048576 | tf_op jit(solution)/shard_map/attend_back/pallas_call | solution.py:445
  424.0 13.0 %attend_back.6 = (bf16[2,80,1536]{2,1,0:T(8,128)(2,1)S(1)}, bf16[2,80,1536]{2,1,0:T(8,128)(2,1)S(1)}, bf16[2,80,1536]{2,1,0:T(8,128)(2,1)S(1)}) custom-call(bf16[32,1536]{1,0:T(8,128)(2,1)S(1)} %pad_maximum_fusion.19.mask_ref, bf16[3,8,80,1536]{3,2,1,0:T(8,128)(2,1)} %bitcast.116, bf16[3,8,80,1536]{3,2,1,0:T(8,128)(2,1)} %bitcast.117, ...), custom_call_target="tpu_custom_call" | custom-call | bytes 1048576 | tf_op jit(solution)/shard_map/attend_back/pallas_call | solution.py:445
  451.5 7.5 %collective-permute-done.49 = bf16[1,160,1280]{2,1,0:T(8,128)(2,1)S(1)} collective-permute-done((bf16[1,160,1280]{2,1,0:T(8,128)(2,1)S(1)}, bf16[1,160,1280]{2,1,0:T(8,128)(2,1)S(1)}, u32[]{:S(2)}, u32[]{:S(2)}) %collective-permute-start.49) | collective-permute-done | bytes 409632 | tf_op jit(solution)/shard_map/ppermute | solution.py:175
  459.1 13.4 %attend_back.7 = (bf16[2,80,1536]{2,1,0:T(8,128)(2,1)S(1)}, bf16[2,80,1536]{2,1,0:T(8,128)(2,1)S(1)}, bf16[2,80,1536]{2,1,0:T(8,128)(2,1)S(1)}) custom-call(bf16[32,1536]{1,0:T(8,128)(2,1)S(1)} %pad_maximum_fusion.19.mask_ref, bf16[3,8,80,1536]{3,2,1,0:T(8,128)(2,1)} %bitcast.119, bf16[3,8,80,1536]{3,2,1,0:T(8,128)(2,1)} %bitcast.120, ...), custom_call_target="tpu_custom_call" | custom-call | bytes 1048576 | tf_op jit(solution)/shard_map/attend_back/pallas_call | solution.py:445
  481.6 13.4 %project_grads.1 = (bf16[8,80,640]{2,1,0:T(8,128)(2,1)}, bf16[4,80,640]{2,1,0:T(8,128)(2,1)S(1)}, bf16[2,80,640]{2,1,0:T(8,128)(2,1)S(1)}, bf16[1,80,640]{2,1,0:...) custom-call(bf16[1536,1280]{1,0:T(8,128)(2,1)} %get-tuple-element.36, ...), custom_call_target="tpu_custom_call" | custom-call | bytes 1048576 | tf_op jit(solution)/shard_map/project_grads/pallas_call | solution.py:815
  520.8 13.9 %project_back.1 = (f32[768,1280]{1,0:T(8,128)}, bf16[768,1280]{1,0:T(8,128)(2,1)}) custom-call(bf16[160,1536]{1,0:T(8,128)(2,1)S(1)} %bitcast.77, bf16[160,1536]{1,0:T(8,128)(2,1)S(1)} %bitcast.82, bf16[160,1536]{1,0:T(8,128)(2,1)S(1)} %bitcast.86, bf16[160,1536]{1,0:T(8,128)(2,1)S(1)} %bitcast.90, bf16[160,1536]{1,0:T(8,128)(2,1)S(1)} %bitcast.94, ...), custom_call_target="tpu_custom_call" | custom-call | bytes 1048576 | tf_op jit(solution)/shard_map/project_back/pallas_call | solution.py:781
  550.5 8.1 %norm_back.3 = (f32[768,1280]{1,0:T(8,128)}, bf16[768,1280]{1,0:T(8,128)(2,1)S(1)}, f32[8,1280]{1,0:T(8,128)S(1)}) custom-call(f32[768,1280]{1,0:T(8,128)} %get-tuple-element.418.refs_0_, bf16[768,1280]{1,0:T(8,128)(2,1)} %collective-permute-done.56.refs_1_, bf16[768,1280]{1,0:T(8,128)(2,1)S(1)} %copy-done.1, f32[768,1280]{1,0:T(8,128)} %get-tuple-element.421.refs_3_, ...), custom_call_target="tpu_custom_call" | custom-call | bytes 1048576 | tf_op jit(solution)/shard_map/norm_back/pallas_call | solution.py:678
  569.7 5.0 slice_select_fusion.1
  578.5 9.6 %adam_feed.1 = (f32[80,5120]{1,0:T(8,128)}, bf16[80,5120]{1,0:T(8,128)(2,1)}, f32[80,5120]{1,0:T(8,128)}, f32[80,5120]{1,0:T(8,128)}, f32[4,80,1280]{2,1,0:T(8,1...) custom-call(f32[1,80,1280]{2,1,0:T(8,128)S(1)} %copy-done.63, ...), custom_call_target="tpu_custom_call" | custom-call | bytes 1048576 | tf_op jit(solution)/shard_map/adam_feed/pallas_call | solution.py:883
  588.1 5.7 collective-permute-done.66
  (643 shorter events, 197.0 us)
Async XLA Ops:
  7.2 60.0 %collective-permute-start = (bf16[750,1280]{1,0:T(8,128)(2,1)}, bf16[750,1280]{1,0:T(8,128)(2,1)}, u32[]{:S(2)}, u32[]{:S(2)}) collective-permute-start(bf16[750,1280]{1,0:T(8,128)(2,1)} %param.18), channel_id=1, source_target_pairs={{1,16},{3,18},{5,20},{7,22},{9,24},{11,26},{13,28},{15,30},{16,1},... | collective-permute-start | bytes 5760008 | tf_op jit(solution)/shard_map/ppermute | solution.py:72
  42.4 37.9 %collective-permute-start.8 = (bf16[1,320,1280]{2,1,0:T(8,128)(2,1)S(1)}, bf16[1,320,1280]{2,1,0:T(8,128)(2,1)S(1)}, u32[]{:S(2)}, u32[]{:S(2)}) collective-permute-start(bf16[1,320,1280]{2,1,0:T(8,128)(2,1)S(1)} %pad_maximum_fusion.3), channel_id=1, source_target_pairs={{0,8},{1,9},{2,10},{3,11},{4,12},{5,13},{6,14},{7,15},{8,0},{9,1},... | collective-permute-start | bytes 2457608 | tf_op jit(solution)/shard_map/ppermute | solution.py:123
  67.6 28.6 %collective-permute-start.11 = (bf16[8,112,640]{2,1,0:T(8,128)(2,1)S(1)}, bf16[8,112,640]{2,1,0:T(8,128)(2,1)S(1)}, u32[]{:S(2)}, u32[]{:S(2)}) collective-permute-start(bf16[8,112,640]{2,1,0:T(8,128)(2,1)S(1)} %pad_maximum_fusion.2.refs_4_), channel_id=1, source_target_pairs={{0,1},{1,0},{2,3},{3,2},{4,5},{5,4},{6,7},{7,6},{8,9},{9,8},{10,11... | collective-permute-start | bytes 3440648 | tf_op jit(solution)/shard_map/ppermute | solution.py:128
  70.5 31.0 %collective-permute-start.10 = (bf16[8,112,640]{2,1,0:T(8,128)(2,1)S(1)}, bf16[8,112,640]{2,1,0:T(8,128)(2,1)S(1)}, u32[]{:S(2)}, u32[]{:S(2)}) collective-permute-start(bf16[8,112,640]{2,1,0:T(8,128)(2,1)S(1)} %pad_maximum_fusion.1.refs_2_), channel_id=1, source_target_pairs={{0,4},{1,5},{2,6},{3,7},{4,0},{5,1},{6,2},{7,3},{8,12},{9,13},{10,... | collective-permute-start | bytes 3440648 | tf_op jit(solution)/shard_map/ppermute | solution.py:128
  70.5 31.0 %collective-permute-start.9 = (bf16[8,112,640]{2,1,0:T(8,128)(2,1)S(1)}, bf16[8,112,640]{2,1,0:T(8,128)(2,1)S(1)}, u32[]{:S(2)}, u32[]{:S(2)}) collective-permute-start(bf16[8,112,640]{2,1,0:T(8,128)(2,1)S(1)} %pad_maximum_fusion.refs_0_), channel_id=1, source_target_pairs={{0,2},{1,3},{2,0},{3,1},{4,6},{5,7},{6,4},{7,5},{8,10},{9,11},{10,... | collective-permute-start | bytes 3440648 | tf_op jit(solution)/shard_map/ppermute | solution.py:128
  81.1 75.2 %collective-permute-start.20 = (bf16[750,1280]{1,0:T(8,128)(2,1)}, bf16[750,1280]{1,0:T(8,128)(2,1)}, u32[]{:S(2)}, u32[]{:S(2)}) collective-permute-start(bf16[750,1280]{1,0:T(8,128)(2,1)} %param.19), channel_id=1, source_target_pairs={{1,16},{3,18},{5,20},{7,22},{9,24},{11,26},{13,28},{15,30},{16,1},... | collective-permute-start | bytes 5760008 | tf_op jit(solution)/shard_map/ppermute | solution.py:72
  124.4 29.1 %collective-permute-start.16 = (bf16[4,80,1280]{2,1,0:T(8,128)(2,1)S(1)}, bf16[4,80,1280]{2,1,0:T(8,128)(2,1)S(1)}, u32[]{:S(2)}, u32[]{:S(2)}) collective-permute-start(bf16[4,80,1280]{2,1,0:T(8,128)(2,1)S(1)} %get-tuple-element.510), channel_id=1, source_target_pairs={{0,4},{1,5},{2,6},{3,7},{4,0},{5,1},{6,2},{7,3},{8,12},{9,13},{10,... | collective-permute-start | bytes 2457608 | tf_op jit(solution)/shard_map/ppermute | solution.py:128
  125.2 28.3 %collective-permute-start.15 = (bf16[4,80,1280]{2,1,0:T(8,128)(2,1)S(1)}, bf16[4,80,1280]{2,1,0:T(8,128)(2,1)S(1)}, u32[]{:S(2)}, u32[]{:S(2)}) collective-permute-start(bf16[4,80,1280]{2,1,0:T(8,128)(2,1)S(1)} %get-tuple-element.512), channel_id=1, source_target_pairs={{0,2},{1,3},{2,0},{3,1},{4,6},{5,7},{6,4},{7,5},{8,10},{9,11},{10,... | collective-permute-start | bytes 2457608 | tf_op jit(solution)/shard_map/ppermute | solution.py:128
  125.8 27.8 %collective-permute-start.18 = (bf16[2,80,1280]{2,1,0:T(8,128)(2,1)S(1)}, bf16[2,80,1280]{2,1,0:T(8,128)(2,1)S(1)}, u32[]{:S(2)}, u32[]{:S(2)}) collective-permute-start(bf16[2,80,1280]{2,1,0:T(8,128)(2,1)S(1)} %pad_maximum_fusion.11), channel_id=1, source_target_pairs={{0,2},{1,3},{2,0},{3,1},{4,6},{5,7},{6,4},{7,5},{8,10},{9,11},{10,... | collective-permute-start | bytes 1228808 | tf_op jit(solution)/shard_map/ppermute | solution.py:128
  158.1 43.4 %collective-permute-start.24 = (bf16[768,1280]{1,0:T(8,128)(2,1)S(1)}, bf16[768,1280]{1,0:T(8,128)(2,1)S(1)}, u32[]{:S(2)}, u32[]{:S(2)}) collective-permute-start(bf16[768,1280]{1,0:T(8,128)(2,1)S(1)} %pad.13.refs_2_.refs_5_), channel_id=1, source_target_pairs={{0,16},{16,0},{1,17},{17,1},{2,18},{18,2},{3,19},{19,3},{4,20},{20... | collective-permute-start | bytes 5898248 | tf_op jit(solution)/shard_map/ppermute | solution.py:58
  159.5 44.0 %collective-permute-start.22 = (bf16[8,80,1280]{2,1,0:T(8,128)(2,1)}, bf16[8,80,1280]{2,1,0:T(8,128)(2,1)S(1)}, u32[]{:S(2)}, u32[]{:S(2)}) collective-permute-start(bf16[8,80,1280]{2,1,0:T(8,128)(2,1)} %constant_dynamic-update-slice_fusion.10.refs_6_), channel_id=1, source_target_pairs={{0,2},{1,3},{2,0},{3,1},{4,6},{5,7},{6,4},{7,5},{8,10},{9,11},{10,... | collective-permute-start | bytes 4915208 | tf_op jit(solution)/shard_map/ppermute | solution.py:128
  159.8 43.7 %collective-permute-start.21 = (bf16[8,80,1280]{2,1,0:T(8,128)(2,1)}, bf16[8,80,1280]{2,1,0:T(8,128)(2,1)S(1)}, u32[]{:S(2)}, u32[]{:S(2)}) collective-permute-start(bf16[8,80,1280]{2,1,0:T(8,128)(2,1)} %constant_dynamic-update-slice_fusion.6.refs_4_), channel_id=1, source_target_pairs={{0,1},{1,0},{2,3},{3,2},{4,5},{5,4},{6,7},{7,6},{8,9},{9,8},{10,11... | collective-permute-start | bytes 4915208 | tf_op jit(solution)/shard_map/ppermute | solution.py:128
  161.5 40.1 %collective-permute-start.25 = (bf16[4,80,1280]{2,1,0:T(8,128)(2,1)S(1)}, bf16[4,80,1280]{2,1,0:T(8,128)(2,1)S(1)}, u32[]{:S(2)}, u32[]{:S(2)}) collective-permute-start(bf16[4,80,1280]{2,1,0:T(8,128)(2,1)S(1)} %copy-done.141), channel_id=1, source_target_pairs={{0,4},{1,5},{2,6},{3,7},{4,0},{5,1},{6,2},{7,3},{8,12},{9,13},{10,... | collective-permute-start | bytes 2457608 | tf_op jit(solution)/shard_map/ppermute | solution.py:128
  163.8 37.8 %collective-permute-start.23 = (bf16[4,80,1280]{2,1,0:T(8,128)(2,1)S(1)}, bf16[4,80,1280]{2,1,0:T(8,128)(2,1)S(1)}, u32[]{:S(2)}, u32[]{:S(2)}) collective-permute-start(bf16[4,80,1280]{2,1,0:T(8,128)(2,1)S(1)} %constant_dynamic-update-slice_fusion.14), channel_id=1, source_target_pairs={{0,4},{1,5},{2,6},{3,7},{4,0},{5,1},{6,2},{7,3},{8,12},{9,13},{10,... | collective-permute-start | bytes 2457608 | tf_op jit(solution)/shard_map/ppermute | solution.py:128
  217.8 51.3 %collective-permute-start.30 = (bf16[8,80,1280]{2,1,0:T(8,128)(2,1)}, bf16[8,80,1280]{2,1,0:T(8,128)(2,1)}, u32[]{:S(2)}, u32[]{:S(2)}) collective-permute-start(bf16[8,80,1280]{2,1,0:T(8,128)(2,1)} %constant_dynamic-update-slice_fusion.20.refs_6_), channel_id=1, source_target_pairs={{0,1},{1,0},{2,3},{3,2},{4,5},{5,4},{6,7},{7,6},{8,9},{9,8},{10,11... | collective-permute-start | bytes 4915208 | tf_op jit(solution)/shard_map/ppermute | solution.py:128
  218.1 51.1 %collective-permute-start.29 = (bf16[8,80,1280]{2,1,0:T(8,128)(2,1)}, bf16[8,80,1280]{2,1,0:T(8,128)(2,1)}, u32[]{:S(2)}, u32[]{:S(2)}) collective-permute-start(bf16[8,80,1280]{2,1,0:T(8,128)(2,1)} %constant_dynamic-update-slice_fusion.18.refs_4_), channel_id=1, source_target_pairs={{0,2},{1,3},{2,0},{3,1},{4,6},{5,7},{6,4},{7,5},{8,10},{9,11},{10,... | collective-permute-start | bytes 4915208 | tf_op jit(solution)/shard_map/ppermute | solution.py:128
  269.2 62.5 %collective-permute-start.31 = (bf16[2,768,1280]{2,1,0:T(8,128)(2,1)}, bf16[2,768,1280]{2,1,0:T(8,128)(2,1)}, u32[]{:S(2)}, u32[]{:S(2)}) collective-permute-start(bf16[2,768,1280]{2,1,0:T(8,128)(2,1)} %get-tuple-element.302), channel_id=1, source_target_pairs={{0,16},{16,0},{1,17},{17,1},{2,18},{18,2},{3,19},{19,3},{4,20},{20... | collective-permute-start | bytes 11796488 | tf_op jit(solution)/shard_map/ppermute | solution.py:58
  269.4 62.3 %collective-permute-start.33 = (bf16[8,80,1280]{2,1,0:T(8,128)(2,1)}, bf16[8,80,1280]{2,1,0:T(8,128)(2,1)}, u32[]{:S(2)}, u32[]{:S(2)}) collective-permute-start(bf16[8,80,1280]{2,1,0:T(8,128)(2,1)} %get-tuple-element.300), channel_id=1, source_target_pairs={{0,4},{1,5},{2,6},{3,7},{4,0},{5,1},{6,2},{7,3},{8,12},{9,13},{10,... | collective-permute-start | bytes 4915208 | tf_op jit(solution)/shard_map/ppermute | solution.py:180
  271.4 60.3 %collective-permute-start.32 = (bf16[8,80,1280]{2,1,0:T(8,128)(2,1)}, bf16[8,80,1280]{2,1,0:T(8,128)(2,1)S(1)}, u32[]{:S(2)}, u32[]{:S(2)}) collective-permute-start(bf16[8,80,1280]{2,1,0:T(8,128)(2,1)} %get-tuple-element.298), channel_id=1, source_target_pairs={{0,2},{1,3},{2,0},{3,1},{4,6},{5,7},{6,4},{7,5},{8,10},{9,11},{10,... | collective-permute-start | bytes 4915208 | tf_op jit(solution)/shard_map/ppermute | solution.py:180
  354.7 64.9 %collective-permute-start.39 = (bf16[8,80,1280]{2,1,0:T(8,128)(2,1)}, bf16[8,80,1280]{2,1,0:T(8,128)(2,1)}, u32[]{:S(2)}, u32[]{:S(2)}) collective-permute-start(bf16[8,80,1280]{2,1,0:T(8,128)(2,1)} %get-tuple-element.315), channel_id=1, source_target_pairs={{0,4},{1,5},{2,6},{3,7},{4,0},{5,1},{6,2},{7,3},{8,12},{9,13},{10,... | collective-permute-start | bytes 4915208 | tf_op jit(solution)/shard_map/ppermute | solution.py:180
  354.8 64.8 %collective-permute-start.38 = (bf16[8,80,1280]{2,1,0:T(8,128)(2,1)}, bf16[8,80,1280]{2,1,0:T(8,128)(2,1)S(1)}, u32[]{:S(2)}, u32[]{:S(2)}) collective-permute-start(bf16[8,80,1280]{2,1,0:T(8,128)(2,1)} %get-tuple-element.313), channel_id=1, source_target_pairs={{0,2},{1,3},{2,0},{3,1},{4,6},{5,7},{6,4},{7,5},{8,10},{9,11},{10,... | collective-permute-start | bytes 4915208 | tf_op jit(solution)/shard_map/ppermute | solution.py:180
  358.9 54.4 %collective-permute-start.36 = (bf16[4,80,1280]{2,1,0:T(8,128)(2,1)}, bf16[4,80,1280]{2,1,0:T(8,128)(2,1)S(1)}, u32[]{:S(2)}, u32[]{:S(2)}) collective-permute-start(bf16[4,80,1280]{2,1,0:T(8,128)(2,1)} %get-tuple-element.320), channel_id=1, source_target_pairs={{0,1},{1,0},{2,3},{3,2},{4,5},{5,4},{6,7},{7,6},{8,9},{9,8},{10,11... | collective-permute-start | bytes 2457608 | tf_op jit(solution)/shard_map/ppermute | solution.py:180
  359.1 55.0 %collective-permute-start.37 = (bf16[4,80,1280]{2,1,0:T(8,128)(2,1)}, bf16[4,80,1280]{2,1,0:T(8,128)(2,1)S(1)}, u32[]{:S(2)}, u32[]{:S(2)}) collective-permute-start(bf16[4,80,1280]{2,1,0:T(8,128)(2,1)} %get-tuple-element.321), channel_id=1, source_target_pairs={{0,1},{1,0},{2,3},{3,2},{4,5},{5,4},{6,7},{7,6},{8,9},{9,8},{10,11... | collective-permute-start | bytes 2457608 | tf_op jit(solution)/shard_map/ppermute | solution.py:180
  442.5 30.7 %collective-permute-start.50 = (bf16[2,80,640]{2,1,0:T(8,128)(2,1)S(1)}, bf16[2,80,640]{2,1,0:T(8,128)(2,1)S(1)}, u32[]{:S(2)}, u32[]{:S(2)}) collective-permute-start(bf16[2,80,640]{2,1,0:T(8,128)(2,1)S(1)} %add_blocks.22), channel_id=1, source_target_pairs={{0,1},{1,0},{2,3},{3,2},{4,5},{5,4},{6,7},{7,6},{8,9},{9,8},{10,11... | collective-permute-start | bytes 614408 | tf_op jit(solution)/shard_map/ppermute | solution.py:180
  448.2 28.8 %collective-permute-start.47 = (bf16[2,80,1280]{2,1,0:T(8,128)(2,1)}, bf16[2,80,1280]{2,1,0:T(8,128)(2,1)S(1)}, u32[]{:S(2)}, u32[]{:S(2)}) collective-permute-start(bf16[2,80,1280]{2,1,0:T(8,128)(2,1)} %get-tuple-element.360), channel_id=1, source_target_pairs={{0,4},{1,5},{2,6},{3,7},{4,0},{5,1},{6,2},{7,3},{8,12},{9,13},{10,... | collective-permute-start | bytes 1228808 | tf_op jit(solution)/shard_map/ppermute | solution.py:180
  448.8 28.2 %collective-permute-start.48 = (bf16[2,80,1280]{2,1,0:T(8,128)(2,1)}, bf16[2,80,1280]{2,1,0:T(8,128)(2,1)}, u32[]{:S(2)}, u32[]{:S(2)}) collective-permute-start(bf16[2,80,1280]{2,1,0:T(8,128)(2,1)} %get-tuple-element.361), channel_id=1, source_target_pairs={{0,1},{1,0},{2,3},{3,2},{4,5},{5,4},{6,7},{7,6},{8,9},{9,8},{10,11... | collective-permute-start | bytes 1228808 | tf_op jit(solution)/shard_map/ppermute | solution.py:180
  449.6 53.5 %collective-permute-start.46 = (bf16[768,1280]{1,0:T(8,128)(2,1)}, bf16[768,1280]{1,0:T(8,128)(2,1)}, u32[]{:S(2)}, u32[]{:S(2)}) collective-permute-start(bf16[768,1280]{1,0:T(8,128)(2,1)} %copy-done.125), channel_id=1, source_target_pairs={{1,16},{3,18},{5,20},{7,22},{9,24},{11,26},{13,28},{15,30},{16,1},... | collective-permute-start | bytes 5898248 | tf_op jit(solution)/shard_map/ppermute | solution.py:72
  503.1 31.7 %collective-permute-start.55 = (bf16[8,80,640]{2,1,0:T(8,128)(2,1)}, bf16[8,80,640]{2,1,0:T(8,128)(2,1)S(1)}, u32[]{:S(2)}, u32[]{:S(2)}) collective-permute-start(bf16[8,80,640]{2,1,0:T(8,128)(2,1)} %get-tuple-element.406), channel_id=1, source_target_pairs={{0,1},{1,0},{2,3},{3,2},{4,5},{5,4},{6,7},{7,6},{8,9},{9,8},{10,11... | collective-permute-start | bytes 2457608 | tf_op jit(solution)/shard_map/ppermute | solution.py:180
  504.3 30.5 %collective-permute-start.54 = (bf16[8,80,640]{2,1,0:T(8,128)(2,1)}, bf16[8,80,640]{2,1,0:T(8,128)(2,1)S(1)}, u32[]{:S(2)}, u32[]{:S(2)}) collective-permute-start(bf16[8,80,640]{2,1,0:T(8,128)(2,1)} %get-tuple-element.404), channel_id=1, source_target_pairs={{0,4},{1,5},{2,6},{3,7},{4,0},{5,1},{6,2},{7,3},{8,12},{9,13},{10,... | collective-permute-start | bytes 2457608 | tf_op jit(solution)/shard_map/ppermute | solution.py:180
  506.0 28.8 %collective-permute-start.53 = (bf16[8,80,640]{2,1,0:T(8,128)(2,1)}, bf16[8,80,640]{2,1,0:T(8,128)(2,1)S(1)}, u32[]{:S(2)}, u32[]{:S(2)}) collective-permute-start(bf16[8,80,640]{2,1,0:T(8,128)(2,1)} %get-tuple-element.402), channel_id=1, source_target_pairs={{0,2},{1,3},{2,0},{3,1},{4,6},{5,7},{6,4},{7,5},{8,10},{9,11},{10,... | collective-permute-start | bytes 2457608 | tf_op jit(solution)/shard_map/ppermute | solution.py:180
  508.7 35.6 %collective-permute-start.65 = (f32[1,360,1280]{2,1,0:T(8,128)}, f32[1,360,1280]{2,1,0:T(8,128)}, u32[]{:S(2)}, u32[]{:S(2)}) collective-permute-start(f32[1,360,1280]{2,1,0:T(8,128)} %maximum_dynamic-update-slice_fusion), channel_id=1, source_target_pairs={{0,16},{16,0},{1,17},{17,1},{2,18},{18,2},{3,19},{19,3},{4,20},{20... | collective-permute-start | bytes 5529608 | tf_op jit(solution)/shard_map/ppermute | solution.py:58
  568.8 27.2 %collective-permute-start.60 = (bf16[768,1280]{1,0:T(8,128)(2,1)}, bf16[768,1280]{1,0:T(8,128)(2,1)S(1)}, u32[]{:S(2)}, u32[]{:S(2)}) collective-permute-start(bf16[768,1280]{1,0:T(8,128)(2,1)} %copy-done.126), channel_id=1, source_target_pairs={{1,16},{3,18},{5,20},{7,22},{9,24},{11,26},{13,28},{15,30},{16,1},... | collective-permute-start | bytes 5898248 | tf_op jit(solution)/shard_map/ppermute | solution.py:72
  (209 other events, 1630.8 us)
